TPU v7x, 1024 devices: a whole 8x8x8 slice. The times are simulated.
1024 devices in a mesh: depth: 64 (over y, x), lat: 16 (over z, core).
Axes of the slice: x: 8, y: 8, z: 8, core: 2. Of those that a mesh axis runs over, the one named last changes fastest.
Arguments:
- thermal_values: float32 [4096, 128, 128], P('depth', 'lat'), may hold values from 0 to 1
- reactant_fraction: float32 [4096, 128, 128], P('depth', 'lat'), may hold values from 0 to 1
- active_sheet_number: int32 [64], P('depth'), may hold values from 1 to 64, 2048 in all
- colour_lookup_library: bfloat16 [8, 4, 128], replicated, may hold values from 0 to 1
- colour_lookup_choice: int32 [4], replicated, may hold values from 0 to 7
- camera_direction: int32 [4], replicated, may hold values from 0 to 1
Outputs:
- temperature_next: float32 [4096, 128, 128], P('depth', 'lat')
- fuel_next: float32 [4096, 128, 128], P('depth', 'lat')
- image: float32 [4, 4, 16, 1024], P(None, None, 'lat', 'depth')
Inputs may be any that keep to these rules, and one draw needn't show every extreme that they name: `active_sheet_number`: the live layers of all blocks sum to 2048; some block has exactly 64.
All inputs are finite; a program needn't handle non-finite values.
Results may differ from a plain program's by a relative error of at most 0.0003.
Values sent between devices are 32-bit elements; how exact they have to be, the bound alone decides.
No kernel may reach another device: no remote copies, remote signals or barrier semaphores. Data moves between devices by JAX's collectives and lax.ppermute only.
A program may use at most 32 MiB of HBM per device.

v0:
```python
import jax
import jax.numpy as jnp
from jax import lax
from jax.sharding import PartitionSpec as P

MEAN_DEPTH = 32
STEPS = 2


time_step = 0.03
heat_release = 2.0
zeldovich = 8.0
expansion = 0.8


def extended_2(block, sides, width):
    for axis, dim in sides:
        count = lax.axis_size(axis)
        forward = [(i, i + 1) for i in range(count - 1)]
        backward = [(target, source) for source, target in forward]
        low = lax.ppermute(
            lax.slice_in_dim(block, block.shape[dim] - width, None, axis=dim), axis, forward
        )
        high = lax.ppermute(lax.slice_in_dim(block, 0, width, axis=dim), axis, backward)
        block = jnp.concatenate([low, block, high], axis=dim)
    return block


def from_partner(array, axis, apart):
    return lax.ppermute(array, axis, [(i, i ^ 1 << apart) for i in range(lax.axis_size(axis))])


def update_fields(solution_snapshot, neighbours, active_flags):
    heat_field = solution_snapshot[0]
    fuel_field = solution_snapshot[1]
    local_coef = 1.0 + 3.0 * heat_field
    heat_flux = jnp.zeros_like(heat_field)
    fuel_flux = jnp.zeros_like(fuel_field)
    for neighbour in neighbours:
        face_coef = 0.5 * (local_coef + 1.0 + 3.0 * neighbour[0])
        heat_flux = heat_flux + face_coef * (neighbour[0] - heat_field)
        fuel_flux = fuel_flux + 0.5 * face_coef * (neighbour[1] - fuel_field)
    shifted = heat_field - 1.0
    reaction = fuel_field * jnp.exp(zeldovich * shifted / (1.0 + expansion * shifted))
    new_heat = heat_field + time_step * (heat_flux + heat_release * reaction)
    new_fuel = fuel_field + time_step * (fuel_flux - reaction)
    return jnp.where(active_flags, jnp.stack([new_heat, new_fuel]), 0.0)


def composite_over(front_image, back_image, channel_axis):
    opacity = lax.slice_in_dim(front_image, 3, 4, axis=channel_axis)
    return front_image + (1.0 - opacity) * back_image


def advance(solution_snapshot, depth_count, active_flags):
    zero_index = jnp.zeros((), jnp.int32)
    last_layer = lax.dynamic_slice_in_dim(solution_snapshot, depth_count - 1, 1, 1)[:, 0]
    edges = jnp.stack([solution_snapshot[:, 0], last_layer], axis=1)
    rims = extended_2(edges, (("depth", 1),), 1)
    sides = extended_2(solution_snapshot, (("lat", 2),), 1)
    below_rim = rims[:, 0]
    above_rim = rims[:, 3]
    extended = jnp.concatenate(
        [below_rim[:, None], solution_snapshot, jnp.zeros_like(below_rim)[:, None]], axis=1
    )
    extended = lax.dynamic_update_slice(
        extended, above_rim[:, None], (zero_index, depth_count + 1, zero_index, zero_index)
    )
    column_padded = jnp.pad(solution_snapshot, ((0, 0), (0, 0), (0, 0), (1, 1)))
    neighbours = [
        extended[:, :-2],
        extended[:, 2:],
        sides[:, :, :-2],
        sides[:, :, 2:],
        column_padded[..., :-2],
        column_padded[..., 2:],
    ]
    return update_fields(solution_snapshot, neighbours, active_flags)


def render(
    solution_snapshot, depth_count, colour_lookup_library, colour_lookup_choice, camera_direction
):
    sheet_sum = solution_snapshot.shape[1]
    pixels = solution_snapshot.shape[2] * solution_snapshot.shape[3]
    bins = colour_lookup_library.shape[2]
    layer_block = 8
    cells = layer_block * pixels
    choose = (
        colour_lookup_choice[:, None] == jnp.arange(colour_lookup_library.shape[0])[None, :]
    ).astype(jnp.float32)
    tables = jnp.sum(
        choose[:, :, None, None] * colour_lookup_library.astype(jnp.float32)[None], axis=1
    )
    weight_tables = []
    for scalar_group in range(2):
        one_table = tables[2 * scalar_group : 2 * scalar_group + 2].reshape(8, bins)
        shifted_table = jnp.concatenate([one_table[:, 1:], one_table[:, -1:]], axis=1)
        weight_tables.append(
            jnp.concatenate([one_table, shifted_table], axis=0).astype(jnp.bfloat16)
        )
    per_cell = 3.0 / (MEAN_DEPTH * lax.axis_size("depth"))
    backward = camera_direction == 1
    bin_rows = lax.broadcasted_iota(jnp.int32, (bins, cells), 0)

    def add_block(block_number, accumulated):
        start = block_number * layer_block
        window = lax.dynamic_slice_in_dim(solution_snapshot, start, layer_block, 1)
        values = []
        for scalar_group in range(2):
            position = jnp.clip(window[scalar_group].reshape(cells), 0.0, 1.0) * (bins - 1)
            lower_bin = jnp.minimum(jnp.floor(position), bins - 2)
            fraction = position - lower_bin
            selector = (bin_rows == lower_bin.astype(jnp.int32)[None, :]).astype(jnp.bfloat16)
            looked_up = jnp.dot(
                weight_tables[scalar_group], selector, preferred_element_type=jnp.float32
            )
            low_value = looked_up[:8]
            high_value = looked_up[8:]
            values.append(
                (low_value + fraction[None] * (high_value - low_value)).reshape(
                    2, 4, layer_block, pixels
                )
            )
        values = jnp.concatenate(values, axis=0)
        layer_alive = (start + jnp.arange(layer_block) < depth_count)[None, :, None]
        optical = jnp.where(layer_alive, values[:, 3] * per_cell, 0.0)
        inclusive = jnp.cumsum(optical, axis=1)
        column_sum = inclusive[:, -1]
        preceding = jnp.where(
            backward[:, None, None], column_sum[:, None] - inclusive, inclusive - optical
        )
        weight = jnp.exp(-preceding) * (1.0 - jnp.exp(-optical))
        colour_sum = jnp.sum(weight[:, None] * values[:, :3], axis=2)
        opacity = 1.0 - jnp.exp(-column_sum)
        new_image = jnp.concatenate([colour_sum, opacity[:, None]], axis=1)
        return jnp.where(
            backward[:, None, None],
            composite_over(new_image, accumulated, 1),
            composite_over(accumulated, new_image, 1),
        )

    start_image = jnp.zeros((colour_lookup_choice.shape[0], 4, pixels), jnp.float32)
    block_total = sheet_sum // layer_block
    return lax.fori_loop(0, block_total, add_block, start_image)


def on_device(
    thermal_values,
    reactant_fraction,
    active_sheet_number,
    colour_lookup_library,
    colour_lookup_choice,
    camera_direction,
):
    depth_count = active_sheet_number[0]
    sheet_sum = thermal_values.shape[0]
    active_flags = (jnp.arange(sheet_sum) < depth_count)[None, :, None, None]
    solution_snapshot = jnp.where(active_flags, jnp.stack([thermal_values, reactant_fraction]), 0.0)
    for repeat in range(STEPS):
        solution_snapshot = advance(solution_snapshot, depth_count, active_flags)
    local_image = render(
        solution_snapshot,
        depth_count,
        colour_lookup_library,
        colour_lookup_choice,
        camera_direction,
    )
    functions = local_image.shape[0]
    pixels = local_image.shape[2]
    devices = lax.axis_size("depth")
    share = pixels // devices
    pieces = local_image.reshape(functions, 4, devices, share)
    position_index = lax.axis_index("depth")
    rounds = devices.bit_length() - 1
    for bit_number in range(rounds):
        halves = pieces.reshape(functions, 4, pieces.shape[2] // 2, 2, share)
        own_bit = position_index // 2**bit_number % 2
        kept_half = jnp.where(own_bit == 0, halves[:, :, :, 0], halves[:, :, :, 1])
        sent_half = jnp.where(own_bit == 0, halves[:, :, :, 1], halves[:, :, :, 0])
        received = from_partner(sent_half, "depth", bit_number)
        mine_front = (own_bit == camera_direction)[:, None, None, None]
        pieces = jnp.where(
            mine_front,
            composite_over(kept_half, received, 1),
            composite_over(received, kept_half, 1),
        )
    return (solution_snapshot[0], solution_snapshot[1], pieces)


def solution(mesh):
    placed = (P("depth", "lat", None), P("depth", "lat", None), P("depth"), P(), P(), P())
    return jax.shard_map(
        on_device,
        mesh=mesh,
        in_specs=placed,
        out_specs=(P("depth", "lat", None), P("depth", "lat", None), P(None, None, "lat", "depth")),
        check_vma=False,
    )
```

profile of v0, /device:TPU:512, one launch (start us, length us, event | category | flops | bytes accessed | tf_op | source)
XLA Modules:
  0.0 128.0 jit_solution(9309247529136169978)
XLA Ops:
  1.3 1.2 maximum_select_fusion
  2.5 3.4 %collective-permute-start = (f32[2,1,8,128]{3,2,1,0:T(8,128)S(1)}, f32[2,1,8,128]{3,2,1,0:T(8,128)S(1)}, u32[]{:S(2)}, u32[]{:S(2)}) collective-permute-start(f32[2,1,8,128]{3,2,1,0:T(8,128)S(1)} %get-tuple-element.240), channel_id=1, source_target_pairs={{0,16},{16,32},{32,48},{48,64},{64,80},{80,96},{96,112},{112,128},... | collective-permute-start | bytes 24584 | tf_op jit(solution)/shard_map/ppermute | solution.py:21
  5.9 1.3 %collective-permute-start.1 = (f32[2,1,8,128]{3,2,1,0:T(8,128)S(1)}, f32[2,1,8,128]{3,2,1,0:T(8,128)S(1)}, u32[]{:S(2)}, u32[]{:S(2)}) collective-permute-start(f32[2,1,8,128]{3,2,1,0:T(8,128)S(1)} %get-tuple-element.239), channel_id=1, source_target_pairs={{16,0},{32,16},{48,32},{64,48},{80,64},{96,80},{112,96},{128,112},... | collective-permute-start | bytes 24584 | tf_op jit(solution)/shard_map/ppermute | solution.py:24
  7.3 1.9 %collective-permute-start.2 = (f32[2,64,1,128]{3,2,1,0:T(1,128)S(1)}, f32[2,64,1,128]{3,2,1,0:T(1,128)S(1)}, u32[]{:S(2)}, u32[]{:S(2)}) collective-permute-start(f32[2,64,1,128]{3,2,1,0:T(1,128)S(1)} %get-tuple-element.241), channel_id=1, source_target_pairs={{0,1},{1,2},{2,3},{3,4},{4,5},{5,6},{6,7},{7,8},{8,9},{9,10},{10,1... | collective-permute-start | bytes 196616 | tf_op jit(solution)/shard_map/ppermute | solution.py:21
  9.3 4.9 %collective-permute-start.3 = (f32[2,64,1,128]{3,2,1,0:T(1,128)S(1)}, f32[2,64,1,128]{3,2,1,0:T(1,128)S(1)}, u32[]{:S(2)}, u32[]{:S(2)}) collective-permute-start(f32[2,64,1,128]{3,2,1,0:T(1,128)S(1)} %get-tuple-element.242), channel_id=1, source_target_pairs={{1,0},{2,1},{3,2},{4,3},{5,4},{6,5},{7,6},{8,7},{9,8},{10,9},{11,1... | collective-permute-start | bytes 196616 | tf_op jit(solution)/shard_map/ppermute | solution.py:24
  15.1 0.9 collective-permute-done.3
  17.3 4.5 %collective-permute-start.4 = (f32[2,1,8,128]{3,2,1,0:T(8,128)S(1)}, f32[2,1,8,128]{3,2,1,0:T(8,128)S(1)}, u32[]{:S(2)}, u32[]{:S(2)}) collective-permute-start(f32[2,1,8,128]{3,2,1,0:T(8,128)S(1)} %get-tuple-element.236), channel_id=1, source_target_pairs={{0,16},{16,32},{32,48},{48,64},{64,80},{80,96},{96,112},{112,128},... | collective-permute-start | bytes 24584 | tf_op jit(solution)/shard_map/ppermute | solution.py:21
  22.0 1.3 %collective-permute-start.5 = (f32[2,1,8,128]{3,2,1,0:T(8,128)S(1)}, f32[2,1,8,128]{3,2,1,0:T(8,128)S(1)}, u32[]{:S(2)}, u32[]{:S(2)}) collective-permute-start(f32[2,1,8,128]{3,2,1,0:T(8,128)S(1)} %get-tuple-element.235), channel_id=1, source_target_pairs={{16,0},{32,16},{48,32},{64,48},{80,64},{96,80},{112,96},{128,112},... | collective-permute-start | bytes 24584 | tf_op jit(solution)/shard_map/ppermute | solution.py:24
  23.3 3.0 %collective-permute-start.6 = (f32[2,64,1,128]{3,2,1,0:T(1,128)S(1)}, f32[2,64,1,128]{3,2,1,0:T(1,128)S(1)}, u32[]{:S(2)}, u32[]{:S(2)}) collective-permute-start(f32[2,64,1,128]{3,2,1,0:T(1,128)S(1)} %get-tuple-element.237), channel_id=1, source_target_pairs={{0,1},{1,2},{2,3},{3,4},{4,5},{5,6},{6,7},{7,8},{8,9},{9,10},{10,1... | collective-permute-start | bytes 196616 | tf_op jit(solution)/shard_map/ppermute | solution.py:21
  26.2 3.8 %collective-permute-start.7 = (f32[2,64,1,128]{3,2,1,0:T(1,128)S(1)}, f32[2,64,1,128]{3,2,1,0:T(1,128)S(1)}, u32[]{:S(2)}, u32[]{:S(2)}) collective-permute-start(f32[2,64,1,128]{3,2,1,0:T(1,128)S(1)} %get-tuple-element.238), channel_id=1, source_target_pairs={{1,0},{2,1},{3,2},{4,3},{5,4},{6,5},{7,6},{8,7},{9,8},{10,9},{11,1... | collective-permute-start | bytes 196616 | tf_op jit(solution)/shard_map/ppermute | solution.py:24
  30.3 1.7 %collective-permute-done.7 = f32[2,64,1,128]{3,2,1,0:T(1,128)S(1)} collective-permute-done((f32[2,64,1,128]{3,2,1,0:T(1,128)S(1)}, f32[2,64,1,128]{3,2,1,0:T(1,128)S(1)}, u32[]{:S(2)}, u32[]{:S(2)}) %collective-permute-start.7) | collective-permute-done | bytes 65568 | tf_op jit(solution)/shard_map/ppermute | solution.py:24
  33.3 0.8 slice_bitcast_fusion.1
  34.1 29.9 %while.15 = (s32[]{:T(128)}, f32[4,4,1024]{2,0,1:T(4,128)S(1)}, pred[4]{0:T(512)(128)(4,1)S(1)}, s32[]{:T(128)}, f32[2,64,8,128]{3,2,1,0:T(8,128)S(1)}, /*index=...) while((s32[]{:T(128)}, f32[4,4,1024]{2,0,1:T(4,128)S(1)}, ...), condition=%wide.region_4.5_spmd.clone.clone, body=%wide.region_1.4_spmd.clone.clone.sunk | while | flops 70717464 | bytes 7545066 | solution.py:145
  34.1 0.7 convolution_bitcast_fusion.4
  37.9 0.7 convolution_bitcast_fusion.4
  45.3 0.7 convolution_bitcast_fusion.4
  49.1 0.7 convolution_bitcast_fusion.4
  52.8 0.7 convolution_bitcast_fusion.4
  56.6 0.7 convolution_bitcast_fusion.4
  60.3 0.7 convolution_bitcast_fusion.4
  65.4 4.6 %collective-permute-start.8 = (f32[4,4,32,16]{3,2,1,0:T(8,128)S(1)}, f32[4,4,32,16]{3,2,1,0:T(8,128)S(1)}, u32[]{:S(2)}, u32[]{:S(2)}) collective-permute-start(f32[4,4,32,16]{3,2,1,0:T(8,128)S(1)} %bitcast.173), channel_id=1, source_target_pairs={{0,16},{16,0},{32,48},{48,32},{64,80},{80,64},{96,112},{112,96},{1... | collective-permute-start | bytes 98312 | tf_op jit(solution)/shard_map/ppermute | solution.py:30
  70.0 6.7 %collective-permute-done.8 = f32[4,4,32,16]{3,2,1,0:T(8,128)S(1)} collective-permute-done((f32[4,4,32,16]{3,2,1,0:T(8,128)S(1)}, f32[4,4,32,16]{3,2,1,0:T(8,128)S(1)}, u32[]{:S(2)}, u32[]{:S(2)}) %collective-permute-start.8) | collective-permute-done | bytes 32800 | tf_op jit(solution)/shard_map/ppermute | solution.py:30
  77.1 6.5 %collective-permute-start.9 = (f32[4,4,16,16]{3,2,1,0:T(8,128)S(1)}, f32[4,4,16,16]{3,2,1,0:T(8,128)S(1)}, u32[]{:S(2)}, u32[]{:S(2)}) collective-permute-start(f32[4,4,16,16]{3,2,1,0:T(8,128)S(1)} %get-tuple-element.244), channel_id=1, source_target_pairs={{0,32},{16,48},{32,0},{48,16},{64,96},{80,112},{96,64},{112,80},{1... | collective-permute-start | bytes 49160 | tf_op jit(solution)/shard_map/ppermute | solution.py:30
  83.6 6.5 %collective-permute-done.9 = f32[4,4,16,16]{3,2,1,0:T(8,128)S(1)} collective-permute-done((f32[4,4,16,16]{3,2,1,0:T(8,128)S(1)}, f32[4,4,16,16]{3,2,1,0:T(8,128)S(1)}, u32[]{:S(2)}, u32[]{:S(2)}) %collective-permute-start.9) | collective-permute-done | bytes 16416 | tf_op jit(solution)/shard_map/ppermute | solution.py:30
  90.3 7.5 %collective-permute-start.10 = (f32[4,4,8,16]{3,2,1,0:T(8,128)S(1)}, f32[4,4,8,16]{3,2,1,0:T(8,128)S(1)}, u32[]{:S(2)}, u32[]{:S(2)}) collective-permute-start(f32[4,4,8,16]{3,2,1,0:T(8,128)S(1)} %bitcast.182), channel_id=1, source_target_pairs={{0,64},{16,80},{32,96},{48,112},{64,0},{80,16},{96,32},{112,48},{1... | collective-permute-start | bytes 24584 | tf_op jit(solution)/shard_map/ppermute | solution.py:30
  97.9 2.5 %collective-permute-done.10 = f32[4,4,8,16]{3,2,1,0:T(8,128)S(1)} collective-permute-done((f32[4,4,8,16]{3,2,1,0:T(8,128)S(1)}, f32[4,4,8,16]{3,2,1,0:T(8,128)S(1)}, u32[]{:S(2)}, u32[]{:S(2)}) %collective-permute-start.10) | collective-permute-done | bytes 8224 | tf_op jit(solution)/shard_map/ppermute | solution.py:30
  100.6 6.7 %collective-permute-start.11 = (f32[4,4,4,16]{3,2,1,0:T(4,128)S(1)}, f32[4,4,4,16]{3,2,1,0:T(4,128)S(1)}, u32[]{:S(2)}, u32[]{:S(2)}) collective-permute-start(f32[4,4,4,16]{3,2,1,0:T(4,128)S(1)} %bitcast.185), channel_id=1, source_target_pairs={{0,128},{16,144},{32,160},{48,176},{64,192},{80,208},{96,224},{112... | collective-permute-start | bytes 12296 | tf_op jit(solution)/shard_map/ppermute | solution.py:30
  107.3 1.8 %collective-permute-done.11 = f32[4,4,4,16]{3,2,1,0:T(4,128)S(1)} collective-permute-done((f32[4,4,4,16]{3,2,1,0:T(4,128)S(1)}, f32[4,4,4,16]{3,2,1,0:T(4,128)S(1)}, u32[]{:S(2)}, u32[]{:S(2)}) %collective-permute-start.11) | collective-permute-done | bytes 4128 | tf_op jit(solution)/shard_map/ppermute | solution.py:30
  109.3 5.0 %collective-permute-start.12 = (f32[4,4,2,16]{3,2,1,0:T(2,128)S(1)}, f32[4,4,2,16]{3,2,1,0:T(2,128)S(1)}, u32[]{:S(2)}, u32[]{:S(2)}) collective-permute-start(f32[4,4,2,16]{3,2,1,0:T(2,128)S(1)} %bitcast.194), channel_id=1, source_target_pairs={{0,256},{16,272},{32,288},{48,304},{64,320},{80,336},{96,352},{112... | collective-permute-start | bytes 6152 | tf_op jit(solution)/shard_map/ppermute | solution.py:30
  114.3 1.7 %collective-permute-done.12 = f32[4,4,2,16]{3,2,1,0:T(2,128)S(1)} collective-permute-done((f32[4,4,2,16]{3,2,1,0:T(2,128)S(1)}, f32[4,4,2,16]{3,2,1,0:T(2,128)S(1)}, u32[]{:S(2)}, u32[]{:S(2)}) %collective-permute-start.12) | collective-permute-done | bytes 2080 | tf_op jit(solution)/shard_map/ppermute | solution.py:30
  116.1 9.6 %collective-permute-start.13 = (f32[4,4,1,16]{3,1,0,2:T(4,128)S(1)}, f32[4,4,1,16]{3,1,0,2:T(4,128)S(1)}, u32[]{:S(2)}, u32[]{:S(2)}) collective-permute-start(f32[4,4,1,16]{3,1,0,2:T(4,128)S(1)} %bitcast.198), channel_id=1, source_target_pairs={{0,512},{16,528},{32,544},{48,560},{64,576},{80,592},{96,608},{112... | collective-permute-start | bytes 3080 | tf_op jit(solution)/shard_map/ppermute | solution.py:30
  125.7 1.6 %collective-permute-done.13 = f32[4,4,1,16]{3,1,0,2:T(4,128)S(1)} collective-permute-done((f32[4,4,1,16]{3,1,0,2:T(4,128)S(1)}, f32[4,4,1,16]{3,1,0,2:T(4,128)S(1)}, u32[]{:S(2)}, u32[]{:S(2)}) %collective-permute-start.13) | collective-permute-done | bytes 1056 | tf_op jit(solution)/shard_map/ppermute | solution.py:30
  (200 shorter events, 30.7 us)
Async XLA Ops:
  1.3 12.9 %copy-start = (bf16[8,4,128]{2,1,0:T(4,128)(2,1)S(1)}, bf16[8,4,128]{2,1,0:T(4,128)(2,1)}, u32[]{:S(2)}) copy-start(bf16[8,4,128]{2,1,0:T(4,128)(2,1)} %param.11) | copy-start | bytes 24580
  1.3 12.9 %copy-start.2 = (s32[4]{0:T(128)S(1)}, s32[4]{0:T(128)}, u32[]{:S(2)}) copy-start(s32[4]{0:T(128)} %param.12) | copy-start | bytes 52
  2.5 12.2 %copy-start.1 = (s32[4]{0:T(128)S(1)}, s32[4]{0:T(128)}, u32[]{:S(2)}) copy-start(s32[4]{0:T(128)} %param.13) | copy-start | bytes 52
  2.5 12.4 %collective-permute-start = (f32[2,1,8,128]{3,2,1,0:T(8,128)S(1)}, f32[2,1,8,128]{3,2,1,0:T(8,128)S(1)}, u32[]{:S(2)}, u32[]{:S(2)}) collective-permute-start(f32[2,1,8,128]{3,2,1,0:T(8,128)S(1)} %get-tuple-element.240), channel_id=1, source_target_pairs={{0,16},{16,32},{32,48},{48,64},{64,80},{80,96},{96,112},{112,128},... | collective-permute-start | bytes 24584 | tf_op jit(solution)/shard_map/ppermute | solution.py:21
  5.9 9.1 %collective-permute-start.1 = (f32[2,1,8,128]{3,2,1,0:T(8,128)S(1)}, f32[2,1,8,128]{3,2,1,0:T(8,128)S(1)}, u32[]{:S(2)}, u32[]{:S(2)}) collective-permute-start(f32[2,1,8,128]{3,2,1,0:T(8,128)S(1)} %get-tuple-element.239), channel_id=1, source_target_pairs={{16,0},{32,16},{48,32},{64,48},{80,64},{96,80},{112,96},{128,112},... | collective-permute-start | bytes 24584 | tf_op jit(solution)/shard_map/ppermute | solution.py:24
  7.3 7.8 %collective-permute-start.2 = (f32[2,64,1,128]{3,2,1,0:T(1,128)S(1)}, f32[2,64,1,128]{3,2,1,0:T(1,128)S(1)}, u32[]{:S(2)}, u32[]{:S(2)}) collective-permute-start(f32[2,64,1,128]{3,2,1,0:T(1,128)S(1)} %get-tuple-element.241), channel_id=1, source_target_pairs={{0,1},{1,2},{2,3},{3,4},{4,5},{5,6},{6,7},{7,8},{8,9},{9,10},{10,1... | collective-permute-start | bytes 196616 | tf_op jit(solution)/shard_map/ppermute | solution.py:21
  9.3 6.7 %collective-permute-start.3 = (f32[2,64,1,128]{3,2,1,0:T(1,128)S(1)}, f32[2,64,1,128]{3,2,1,0:T(1,128)S(1)}, u32[]{:S(2)}, u32[]{:S(2)}) collective-permute-start(f32[2,64,1,128]{3,2,1,0:T(1,128)S(1)} %get-tuple-element.242), channel_id=1, source_target_pairs={{1,0},{2,1},{3,2},{4,3},{5,4},{6,5},{7,6},{8,7},{9,8},{10,9},{11,1... | collective-permute-start | bytes 196616 | tf_op jit(solution)/shard_map/ppermute | solution.py:24
  17.3 12.7 %collective-permute-start.4 = (f32[2,1,8,128]{3,2,1,0:T(8,128)S(1)}, f32[2,1,8,128]{3,2,1,0:T(8,128)S(1)}, u32[]{:S(2)}, u32[]{:S(2)}) collective-permute-start(f32[2,1,8,128]{3,2,1,0:T(8,128)S(1)} %get-tuple-element.236), channel_id=1, source_target_pairs={{0,16},{16,32},{32,48},{48,64},{64,80},{80,96},{96,112},{112,128},... | collective-permute-start | bytes 24584 | tf_op jit(solution)/shard_map/ppermute | solution.py:21
  22.0 8.2 %collective-permute-start.5 = (f32[2,1,8,128]{3,2,1,0:T(8,128)S(1)}, f32[2,1,8,128]{3,2,1,0:T(8,128)S(1)}, u32[]{:S(2)}, u32[]{:S(2)}) collective-permute-start(f32[2,1,8,128]{3,2,1,0:T(8,128)S(1)} %get-tuple-element.235), channel_id=1, source_target_pairs={{16,0},{32,16},{48,32},{64,48},{80,64},{96,80},{112,96},{128,112},... | collective-permute-start | bytes 24584 | tf_op jit(solution)/shard_map/ppermute | solution.py:24
  23.3 7.0 %collective-permute-start.6 = (f32[2,64,1,128]{3,2,1,0:T(1,128)S(1)}, f32[2,64,1,128]{3,2,1,0:T(1,128)S(1)}, u32[]{:S(2)}, u32[]{:S(2)}) collective-permute-start(f32[2,64,1,128]{3,2,1,0:T(1,128)S(1)} %get-tuple-element.237), channel_id=1, source_target_pairs={{0,1},{1,2},{2,3},{3,4},{4,5},{5,6},{6,7},{7,8},{8,9},{9,10},{10,1... | collective-permute-start | bytes 196616 | tf_op jit(solution)/shard_map/ppermute | solution.py:21
  26.2 5.7 %collective-permute-start.7 = (f32[2,64,1,128]{3,2,1,0:T(1,128)S(1)}, f32[2,64,1,128]{3,2,1,0:T(1,128)S(1)}, u32[]{:S(2)}, u32[]{:S(2)}) collective-permute-start(f32[2,64,1,128]{3,2,1,0:T(1,128)S(1)} %get-tuple-element.238), channel_id=1, source_target_pairs={{1,0},{2,1},{3,2},{4,3},{5,4},{6,5},{7,6},{8,7},{9,8},{10,9},{11,1... | collective-permute-start | bytes 196616 | tf_op jit(solution)/shard_map/ppermute | solution.py:24
  65.4 11.4 %collective-permute-start.8 = (f32[4,4,32,16]{3,2,1,0:T(8,128)S(1)}, f32[4,4,32,16]{3,2,1,0:T(8,128)S(1)}, u32[]{:S(2)}, u32[]{:S(2)}) collective-permute-start(f32[4,4,32,16]{3,2,1,0:T(8,128)S(1)} %bitcast.173), channel_id=1, source_target_pairs={{0,16},{16,0},{32,48},{48,32},{64,80},{80,64},{96,112},{112,96},{1... | collective-permute-start | bytes 98312 | tf_op jit(solution)/shard_map/ppermute | solution.py:30
  77.1 13.0 %collective-permute-start.9 = (f32[4,4,16,16]{3,2,1,0:T(8,128)S(1)}, f32[4,4,16,16]{3,2,1,0:T(8,128)S(1)}, u32[]{:S(2)}, u32[]{:S(2)}) collective-permute-start(f32[4,4,16,16]{3,2,1,0:T(8,128)S(1)} %get-tuple-element.244), channel_id=1, source_target_pairs={{0,32},{16,48},{32,0},{48,16},{64,96},{80,112},{96,64},{112,80},{1... | collective-permute-start | bytes 49160 | tf_op jit(solution)/shard_map/ppermute | solution.py:30
  90.3 10.1 %collective-permute-start.10 = (f32[4,4,8,16]{3,2,1,0:T(8,128)S(1)}, f32[4,4,8,16]{3,2,1,0:T(8,128)S(1)}, u32[]{:S(2)}, u32[]{:S(2)}) collective-permute-start(f32[4,4,8,16]{3,2,1,0:T(8,128)S(1)} %bitcast.182), channel_id=1, source_target_pairs={{0,64},{16,80},{32,96},{48,112},{64,0},{80,16},{96,32},{112,48},{1... | collective-permute-start | bytes 24584 | tf_op jit(solution)/shard_map/ppermute | solution.py:30
  100.6 8.6 %collective-permute-start.11 = (f32[4,4,4,16]{3,2,1,0:T(4,128)S(1)}, f32[4,4,4,16]{3,2,1,0:T(4,128)S(1)}, u32[]{:S(2)}, u32[]{:S(2)}) collective-permute-start(f32[4,4,4,16]{3,2,1,0:T(4,128)S(1)} %bitcast.185), channel_id=1, source_target_pairs={{0,128},{16,144},{32,160},{48,176},{64,192},{80,208},{96,224},{112... | collective-permute-start | bytes 12296 | tf_op jit(solution)/shard_map/ppermute | solution.py:30
  109.3 6.8 %collective-permute-start.12 = (f32[4,4,2,16]{3,2,1,0:T(2,128)S(1)}, f32[4,4,2,16]{3,2,1,0:T(2,128)S(1)}, u32[]{:S(2)}, u32[]{:S(2)}) collective-permute-start(f32[4,4,2,16]{3,2,1,0:T(2,128)S(1)} %bitcast.194), channel_id=1, source_target_pairs={{0,256},{16,272},{32,288},{48,304},{64,320},{80,336},{96,352},{112... | collective-permute-start | bytes 6152 | tf_op jit(solution)/shard_map/ppermute | solution.py:30
  116.1 11.2 %collective-permute-start.13 = (f32[4,4,1,16]{3,1,0,2:T(4,128)S(1)}, f32[4,4,1,16]{3,1,0,2:T(4,128)S(1)}, u32[]{:S(2)}, u32[]{:S(2)}) collective-permute-start(f32[4,4,1,16]{3,1,0,2:T(4,128)S(1)} %bitcast.198), channel_id=1, source_target_pairs={{0,512},{16,528},{32,544},{48,560},{64,576},{80,592},{96,608},{112... | collective-permute-start | bytes 3080 | tf_op jit(solution)/shard_map/ppermute | solution.py:30
where the time goes:
time: 129 us; the launch traced here: 128 us
  starting transfers between devices  64 us (50%)
  waiting for transfers between devices  23.5 us (18%)
  other arithmetic  17.9 us (14%)
  matrix products  11.7 us (9%)
  local copies, waits for them, and re-layouts  8.17 us (6%)
  between operations  1.88 us (1%)
    ppermute x6, starting transfers between devices, from_partner(): lax.ppermute(array, axis, [(i, i ^ 1 << apart) for i in range(lax.axis_si...  39.9 us
    ppermute x6, waiting for transfers between devices, from_partner(): lax.ppermute(array, axis, [(i, i ^ 1 << apart) for i in range(lax.axis_si...  20.8 us
    ppermute x4, starting transfers between devices, extended_2(): lax.ppermute(lax.slice_in_dim(block, block.shape[dim] - width, None, axis...  12.8 us
    dot_general x16, matrix products, add_block(): jnp.dot(weight_tables[scalar_group], selector, preferred_element_type=jnp...  11.7 us
    ppermute x4, starting transfers between devices, extended_2(): lax.ppermute(lax.slice_in_dim(block, 0, width, axis=dim), axis, backward)  11.3 us
    lt x8, other arithmetic, add_block(): layer_alive = (start + jnp.arange(layer_block) < depth_count)[None, :, None]  5.23 us
    reshape x16, local copies, waits for them, and re-layouts, add_block(): (low_value + fraction[None] * (high_value - low_value)).reshape(2, 4, lay...  3.28 us
    ppermute x4, waiting for transfers between devices, extended_2(): lax.ppermute(lax.slice_in_dim(block, 0, width, axis=dim), axis, backward)  2.61 us
  transfers between devices with their start and end apart: 14, of which 8 were waited for; matrix products, arithmetic and copies ran while one was open for 1% of the time, Pallas kernels for 0%

commit v1 on v0

v1 whole, which is shorter than its diff:
```python
import functools

import jax
import jax.numpy as jnp
from jax import lax
from jax.experimental import pallas as pl
from jax.experimental.pallas import tpu as pltpu
from jax.sharding import PartitionSpec as P

MEAN_DEPTH = 32
STEPS = 2

time_step = 0.03
heat_release = 2.0
zeldovich = 8.0
expansion = 0.8

VMEM = pltpu.VMEM
SMEM = pltpu.SMEM
F32 = jnp.float32


def in_vmem():
    return pl.BlockSpec(memory_space=VMEM)


def in_smem():
    return pl.BlockSpec(memory_space=SMEM)


def pack_rows(meta, theta, fuel, low_rows, high_rows, last_layer, first_layer):
    depth_count = meta[0]
    for number, field in enumerate((theta, fuel)):
        for row in range(2):
            low_rows[2 * number + row] = field[:, row, :]
            high_rows[2 * number + row] = field[:, 6 + row, :]
        last_layer[number] = field[depth_count - 1]
        first_layer[number] = field[0]


def pack_rims(
    meta, theta, fuel, rows_below, rows_above, upward, downward
):
    depth_count = meta[0]
    last = depth_count - 1
    second_last = jnp.maximum(depth_count - 2, 0)
    second = jnp.minimum(1, last)
    size = jnp.full((1, 128), depth_count.astype(F32))
    for number, field in enumerate((theta, fuel)):
        upward[number, 0] = field[last]
        upward[number, 1] = field[second_last]
        upward[number, 2, 0:1] = rows_below[2 * number + 1, pl.ds(last, 1), :]
        upward[number, 2, 1:2] = rows_above[2 * number, pl.ds(last, 1), :]
        upward[number, 2, 2:3] = size
        upward[number, 2, 3:8] = jnp.zeros((5, 128), F32)
        downward[number, 0] = field[0]
        downward[number, 1] = field[second]
        downward[number, 2, 0:1] = rows_below[2 * number + 1, 0:1, :]
        downward[number, 2, 1:2] = rows_above[2 * number, 0:1, :]
        downward[number, 2, 2:3] = size
        downward[number, 2, 3:8] = jnp.zeros((5, 128), F32)


def lanes():
    return lax.broadcasted_iota(jnp.int32, (8, 128), 1)


def sublanes():
    return lax.broadcasted_iota(jnp.int32, (8, 128), 0)


def left_of(x):
    return jnp.where(lanes() == 0, 0.0, pltpu.roll(x, 1, 1))


def right_of(x):
    return jnp.where(lanes() == 127, 0.0, pltpu.roll(x, 127, 1))


def row_below(x, halo_row):
    return jnp.where(sublanes() == 0, jnp.broadcast_to(halo_row, (8, 128)), pltpu.roll(x, 1, 0))


def row_above(x, halo_row):
    return jnp.where(sublanes() == 7, jnp.broadcast_to(halo_row, (8, 128)), pltpu.roll(x, 7, 0))


def stepped(heat, fuel, neighbours):
    heat_sum = neighbours[0][0]
    fuel_sum = neighbours[0][1]
    product_sum = neighbours[0][0] * neighbours[0][1]
    square_sum = neighbours[0][0] * neighbours[0][0]
    for heat_n, fuel_n in neighbours[1:]:
        heat_sum = heat_sum + heat_n
        fuel_sum = fuel_sum + fuel_n
        product_sum = product_sum + heat_n * fuel_n
        square_sum = square_sum + heat_n * heat_n
    heat_flux = (heat_sum - 6.0 * heat) + 1.5 * (square_sum - 6.0 * (heat * heat))
    fuel_flux = 0.5 * (
        (1.0 + 1.5 * heat) * (fuel_sum - 6.0 * fuel) + 1.5 * (product_sum - fuel * heat_sum)
    )
    ratio = zeldovich / expansion
    reaction = fuel * jnp.exp(ratio - ratio / ((1.0 - expansion) + expansion * heat))
    return (
        heat + time_step * (heat_flux + heat_release * reaction),
        fuel + time_step * (fuel_flux - reaction),
    )


def advance_and_render(
    places,
    functions,
    meta,
    choice,
    camera,
    theta,
    fuel,
    library,
    own_low,
    own_high,
    rows_below,
    rows_above,
    from_below,
    from_above,
    from_below_2,
    from_above_2,
    theta_next,
    fuel_next,
    image,
    field0,
    field1,
    edge0,
    edge1,
    tables,
    low_table,
    rise_table,
    copies,
):
    depth_count = meta[0]
    lat_index = meta[1]
    lat_count = meta[2]
    bins = library.shape[2]
    fetch = [
        pltpu.make_async_copy(source, field0.at[number, pl.ds(2, places)], copies.at[number])
        for number, source in enumerate((theta, fuel))
    ]
    for copy in fetch:
        copy.start()

    tables[...] = library[...].astype(F32)
    per_cell = 3.0 / meta[3].astype(F32)
    for f in range(functions):
        sign = jnp.where(camera[f] == 0, -per_cell, per_cell)
        for c in range(4):
            low = jnp.broadcast_to(tables[choice[f], c : c + 1, :], (8, bins))
            rise = pltpu.roll(low, bins - 1, 1) - low
            if c == 3:
                low = low * sign
                rise = rise * sign
            low_table[4 * f + c] = low
            rise_table[4 * f + c] = rise

    lead = 8
    for number in range(2):
        for row in range(2):
            edge0[number, row, lead : lead + places] = rows_below[2 * number + row]
            edge0[number, 2 + row, lead : lead + places] = rows_above[2 * number + row]
        edge0[number, 1, lead - 1 : lead] = from_below[number, 2, 0:1]
        edge0[number, 2, lead - 1 : lead] = from_below[number, 2, 1:2]
        edge0[number, 1, pl.ds(lead + depth_count, 1)] = from_above[number, 2, 0:1]
        edge0[number, 2, pl.ds(lead + depth_count, 1)] = from_above[number, 2, 1:2]

    for copy in fetch:
        copy.wait()
    below_size = jnp.broadcast_to(from_below[0, 2, 2:3], (8, 128))
    above_size = jnp.broadcast_to(from_above[0, 2, 2:3], (8, 128))
    for number in range(2):
        field0[number, 0] = jnp.where(below_size == 1.0, from_below_2[number], from_below[number, 1])
        field0[number, 1] = from_below[number, 0]
        field0[number, depth_count + 2] = from_above[number, 0]
        field0[number, depth_count + 3] = jnp.where(
            above_size == 1.0, from_above_2[number], from_above[number, 1]
        )

    for block in range(places // 8):
        at = lead + 8 * block
        for side in range(2):
            edge_row = 1 + side
            outer_row = 3 * side
            inner = (own_low, own_high)[side]
            heat = edge0[0, edge_row, at : at + 8]
            burn = edge0[1, edge_row, at : at + 8]
            around = []
            for shift in (-1, 1):
                around.append(
                    tuple(edge0[n, edge_row, at + shift : at + shift + 8] for n in range(2))
                )
            around.append(tuple(edge0[n, outer_row, at : at + 8] for n in range(2)))
            around.append(
                tuple(inner[2 * n + side, 8 * block : 8 * block + 8] for n in range(2))
            )
            around.append((left_of(heat), left_of(burn)))
            around.append((right_of(heat), right_of(burn)))
            new_heat, new_burn = stepped(heat, burn, around)
            outside = (lat_index == 0) if side == 0 else (lat_index == lat_count - 1)
            edge1[0, side, 8 * block : 8 * block + 8] = jnp.where(outside, 0.0, new_heat)
            edge1[1, side, 8 * block : 8 * block + 8] = jnp.where(outside, 0.0, new_burn)

    def block_step(field, at, count, edge_rows):
        heat = [field[0, at - 1 + j] for j in range(count + 2)]
        burn = [field[1, at - 1 + j] for j in range(count + 2)]
        results = []
        for j in range(1, count + 1):
            h, b = heat[j], burn[j]
            (h_low, b_low), (h_high, b_high) = edge_rows(j - 1)
            around = [
                (heat[j - 1], burn[j - 1]),
                (heat[j + 1], burn[j + 1]),
                (row_below(h, h_low), row_below(b, b_low)),
                (row_above(h, h_high), row_above(b, b_high)),
                (left_of(h), left_of(b)),
                (right_of(h), right_of(b)),
            ]
            results.append(stepped(h, b, around))
        return results

    unroll = 6

    def first_step(block, carry):
        start = block * unroll

        def edge_rows(j):
            place = lead - 1 + start + j
            return [
                tuple(edge0[n, 1 + side, pl.ds(place, 1), :] for n in range(2)) for side in range(2)
            ]

        for j, (h, b) in enumerate(block_step(field0, start + 1, unroll, edge_rows)):
            field1[0, start + j] = h
            field1[1, start + j] = b
        return carry

    lax.fori_loop(0, (places + 2) // unroll, first_step, 0)
    for number in range(2):
        field1[number, 0] = jnp.where(below_size > 0.0, field1[number, 0], 0.0)
        field1[number, depth_count + 1] = jnp.where(
            above_size > 0.0, field1[number, depth_count + 1], 0.0
        )

    unroll_2 = 4

    def second_step(block, carry):
        start = block * unroll_2

        def edge_rows(j):
            return [
                tuple(edge1[n, side, pl.ds(start + j, 1), :] for n in range(2)) for side in range(2)
            ]

        carry = list(carry)
        for j, new in enumerate(block_step(field1, start + 1, unroll_2, edge_rows)):
            alive = start + j < depth_count
            for number, out in enumerate((theta_next, fuel_next)):
                value = jnp.where(alive, new[number], 0.0)
                out[start + j] = value
                position = jnp.clip(value, 0.0, 1.0) * (bins - 1)
                lower = jnp.minimum(position.astype(jnp.int32), bins - 2)
                fraction = position - lower.astype(F32)

                def look_up(entry):
                    low = jnp.take_along_axis(low_table[entry], lower, axis=1)
                    rise = jnp.take_along_axis(rise_table[entry], lower, axis=1)
                    return low + fraction * rise

                for f in range(2 * number, 2 * number + 2):
                    gone, red, green, blue = carry[4 * f : 4 * f + 4]
                    depth = jnp.where(alive, look_up(4 * f + 3), 0.0)
                    gain = depth * (1.0 + depth * (0.5 + depth * (1.0 / 6.0)))
                    gain = gain + gone * gain
                    carry[4 * f] = gone + gain
                    carry[4 * f + 1] = red + gain * look_up(4 * f)
                    carry[4 * f + 2] = green + gain * look_up(4 * f + 1)
                    carry[4 * f + 3] = blue + gain * look_up(4 * f + 2)
        return tuple(carry)

    zero = jnp.zeros((8, 128), F32)
    sums = lax.fori_loop(0, places // unroll_2, second_step, (zero,) * (4 * functions))

    channels = []
    for f in range(functions):
        gone, red, green, blue = sums[4 * f : 4 * f + 4]
        scale = jnp.where(camera[f] == 0, -1.0, 1.0 / (1.0 + gone))
        channels += [red * scale, green * scale, blue * scale, gone * scale]

    group = lanes() // 16
    for half in range(2):
        regs = channels[8 * half : 8 * half + 8]
        for bit in (1, 2, 4):
            upper = (group & bit) != 0
            fresh = list(regs)
            for i in range(8):
                if i & bit:
                    continue
                a, b = regs[i], regs[i | bit]
                fresh[i] = jnp.where(upper, pltpu.roll(b, 16 * bit, 1), a)
                fresh[i | bit] = jnp.where(upper, b, pltpu.roll(a, 128 - 16 * bit, 1))
            regs = fresh
        for g in range(8):
            image[pl.ds(2 * g + half, 8, stride=16), :] = regs[g]


def composite(camera, pieces, image):
    sources = pieces.shape[0] // 2
    lane = lanes()
    row = sublanes()
    opacity_lane = lane // 64 * 64 + 48 + lane % 16
    for half in range(2):
        forward = jnp.where(
            lane < 64,
            (camera[2 * half] == 0).astype(jnp.int32),
            (camera[2 * half + 1] == 0).astype(jnp.int32),
        ) == 1
        values, clear, through = [], [], []
        carry = jnp.ones((8, 128), F32)
        for block in range(sources // 8):
            value = pieces[pl.ds(16 * block + half, 8, stride=2), :]
            passing = 1.0 - jnp.take_along_axis(value, opacity_lane, axis=1)
            product = passing
            for shift in (1, 2, 4):
                product = product * jnp.where(row >= shift, pltpu.roll(product, shift, 0), 1.0)
            product = product * carry
            carry = jnp.broadcast_to(product[7:8], (8, 128))
            values.append(value)
            clear.append(passing)
            through.append(product)
        total = jnp.zeros((8, 128), F32)
        for value, passing, product in zip(values, clear, through):
            top = jnp.where(forward, product, carry)
            bottom = jnp.where(forward, passing, product)
            total = total + value * (top / bottom)
        line = jnp.sum(total, axis=0, keepdims=True)
        for clo in range(8):
            channel = 8 * half + clo
            image[channel // 4, channel % 4] = line[:, 16 * clo : 16 * clo + 16]


def shifted(array, axis, by):
    count = lax.axis_size(axis)
    pairs = [(i, i + by) for i in range(count) if 0 <= i + by < count]
    return lax.ppermute(array, axis, pairs)


def on_device(
    thermal_values,
    reactant_fraction,
    active_sheet_number,
    colour_lookup_library,
    colour_lookup_choice,
    camera_direction,
):
    places = thermal_values.shape[0]
    functions = colour_lookup_choice.shape[0]
    devices = lax.axis_size("depth")
    meta = jnp.stack(
        [
            active_sheet_number[0],
            lax.axis_index("lat").astype(jnp.int32),
            jnp.int32(lax.axis_size("lat")),
            jnp.int32(MEAN_DEPTH * devices),
        ]
    )
    rows = jax.ShapeDtypeStruct((4, places, 128), F32)
    layers = jax.ShapeDtypeStruct((2, 8, 128), F32)
    rim = jax.ShapeDtypeStruct((2, 3, 8, 128), F32)
    low_rows, high_rows, last_layer, first_layer = pl.pallas_call(
        pack_rows,
        out_shape=(rows, rows, layers, layers),
        in_specs=[in_smem(), in_vmem(), in_vmem()],
        out_specs=(in_vmem(),) * 4,
        name="pack_rows",
    )(meta, thermal_values, reactant_fraction)
    rows_below = shifted(high_rows, "lat", 1)
    rows_above = shifted(low_rows, "lat", -1)
    from_below_2 = shifted(last_layer, "depth", 2)
    from_above_2 = shifted(first_layer, "depth", -2)
    upward, downward = pl.pallas_call(
        pack_rims,
        out_shape=(rim, rim),
        in_specs=[in_smem()] + [in_vmem()] * 4,
        out_specs=(in_vmem(),) * 2,
        name="pack_rims",
    )(meta, thermal_values, reactant_fraction, rows_below, rows_above)
    from_below = shifted(upward, "depth", 1)
    from_above = shifted(downward, "depth", -1)
    field = jax.ShapeDtypeStruct(thermal_values.shape, F32)
    bins = colour_lookup_library.shape[2]
    theta_next, fuel_next, pieces = pl.pallas_call(
        functools.partial(advance_and_render, places, functions),
        out_shape=(field, field, jax.ShapeDtypeStruct((2 * devices, 128), F32)),
        in_specs=[in_smem()] * 3 + [pl.BlockSpec(memory_space=pl.ANY)] * 2 + [in_vmem()] * 9,
        out_specs=(in_vmem(),) * 3,
        scratch_shapes=[
            VMEM((2, places + 4, 8, 128), F32),
            VMEM((2, places + 2, 8, 128), F32),
            VMEM((2, 4, places + 16, 128), F32),
            VMEM((2, 2, places, 128), F32),
            VMEM(colour_lookup_library.shape, F32),
            VMEM((4 * functions, 8, bins), F32),
            VMEM((4 * functions, 8, bins), F32),
            pltpu.SemaphoreType.DMA((2,)),
        ],
        name="advance_and_render",
    )(
        meta,
        colour_lookup_choice,
        camera_direction,
        thermal_values,
        reactant_fraction,
        colour_lookup_library,
        low_rows,
        high_rows,
        rows_below,
        rows_above,
        from_below,
        from_above,
        from_below_2,
        from_above_2,
    )
    pieces = lax.all_to_all(pieces, "depth", 0, 0, tiled=True)
    image = pl.pallas_call(
        composite,
        out_shape=jax.ShapeDtypeStruct((functions, 4, 1, 16), F32),
        in_specs=[in_smem(), in_vmem()],
        out_specs=in_vmem(),
        name="composite",
    )(camera_direction, pieces)
    return (theta_next, fuel_next, image)


def solution(mesh):
    placed = (P("depth", "lat", None), P("depth", "lat", None), P("depth"), P(), P(), P())
    return jax.shard_map(
        on_device,
        mesh=mesh,
        in_specs=placed,
        out_specs=(P("depth", "lat", None), P("depth", "lat", None), P(None, None, "lat", "depth")),
        check_vma=False,
    )
```

time: 129 us -> 74.5 us (0.58)
  starting transfers between devices: 64 us -> 15.9 us
  blocking collectives: 0 us -> 26.8 us
  other arithmetic: 17.9 us -> 0.65 us
  Pallas kernels: 0 us -> 15.1 us
  matrix products: 11.7 us -> 0 us
  waiting for transfers between devices: 23.5 us -> 12.4 us
  local copies, waits for them, and re-layouts: 8.17 us -> 1.88 us
    ppermute x14 -> x6, starting transfers between devices: 64 us -> 15.9 us  [shifted(): return lax.ppermute(array, axis, pairs)]
    all_to_all x0 -> x1, blocking collectives: none -> 26.8 us  [on_device(): pieces = lax.all_to_all(pieces, 'depth', 0, 0, tiled=True)]
    pallas_call x0 -> x4, Pallas kernels: none -> 15.1 us  [the longest x1 9.82 us: on_device(): pl.pallas_call(functools.partial(advance_and_render, places, functions),...]
    dot_general x16 -> x0, matrix products: 11.7 us -> none  [add_block(): jnp.dot(weight_tables[scalar_group], selector, preferred_element_type=jnp...]
    ppermute x14 -> x6, waiting for transfers between devices: 23.5 us -> 12.4 us  [shifted(): return lax.ppermute(array, axis, pairs)]
    lt x9 -> x0, other arithmetic: 5.23 us -> none  [the longest x8 5.23 us: add_block(): layer_alive = (start + jnp.arange(layer_block) < depth_count)[None, :, None]]
    reshape x16 -> x0, local copies, waits for them, and re-layouts: 3.28 us -> none  [add_block(): (low_value + fraction[None] * (high_value - low_value)).reshape(2, 4, lay...]
    select_n x22 -> x0, other arithmetic: 3.27 us -> none  [the longest x1 1.17 us: on_device(): jnp.where(active_flags, jnp.stack([thermal_values, reactant_fraction]), 0.0)]
  transfers between devices with their start and end apart: 14 -> 6, of which waited for: 8 -> 3; matrix products, arithmetic and copies ran while one was open for 1% -> 0% of each run, Pallas kernels for 0% -> 0%
where the time goes in v1:
time: 74.5 us; the launch traced here: 74 us
  blocking collectives  26.8 us (36%)
  starting transfers between devices  15.9 us (21%)
  Pallas kernels  15.1 us (20%)
  waiting for transfers between devices  12.4 us (17%)
  local copies, waits for them, and re-layouts  1.88 us (3%)
  between operations  1.39 us (2%)
    all_to_all x1, blocking collectives, on_device(): pieces = lax.all_to_all(pieces, 'depth', 0, 0, tiled=True)  26.8 us
    ppermute x6, starting transfers between devices, shifted(): return lax.ppermute(array, axis, pairs)  15.9 us
    ppermute x6, waiting for transfers between devices, shifted(): return lax.ppermute(array, axis, pairs)  12.4 us
    pallas_call x1, Pallas kernels, on_device(): pl.pallas_call(functools.partial(advance_and_render, places, functions),...  9.82 us
    pallas_call x1, Pallas kernels, on_device(): pl.pallas_call(pack_rows, out_shape=(rows, rows, layers, layers), in_spec...  1.88 us
    unnamed x16, local copies, waits for them, and re-layouts  1.88 us
    pallas_call x1, Pallas kernels, on_device(): pl.pallas_call(pack_rims, out_shape=(rim, rim), in_specs=[in_smem()] + [i...  1.74 us
    pallas_call x1, Pallas kernels, on_device(): pl.pallas_call(composite, out_shape=jax.ShapeDtypeStruct((functions, 4, 1...  1.66 us
  transfers between devices with their start and end apart: 6, of which 3 were waited for; matrix products, arithmetic and copies ran while one was open for 0% of the time, Pallas kernels for 0%

profile of v1, /device:TPU:512, one launch (start us, length us, event | category | flops | bytes accessed | tf_op | source)
XLA Modules:
  0.0 74.0 jit_solution(16241043051868523840)
XLA Ops:
  1.3 0.7 pad_add_fusion.meta
  1.9 1.9 %pack_rows.1 = (f32[4,64,128]{2,1,0:T(8,128)}, f32[4,64,128]{2,1,0:T(8,128)}, f32[2,8,128]{2,1,0:T(8,128)}, f32[2,8,128]{2,1,0:T(8,128)}) custom-call(s32[4]{0:T(128)} %pad_add_fusion.meta, f32[64,8,128]{2,1,0:T(8,128)} %theta.5, f32[64,8,128]{2,1,0:T(8,128)} %fuel.5), custom_call_target="tpu_custom_call" | custom-call | tf_op jit(solution)/shard_map/pack_rows/pallas_call | solution.py:375
  3.8 1.9 %collective-permute-start.1 = (f32[4,64,128]{2,1,0:T(8,128)}, f32[4,64,128]{2,1,0:T(8,128)S(1)}, u32[]{:S(2)}, u32[]{:S(2)}) collective-permute-start(f32[4,64,128]{2,1,0:T(8,128)} %get-tuple-element.12.own_low), channel_id=1, source_target_pairs={{1,0},{2,1},{3,2},{4,3},{5,4},{6,5},{7,6},{8,7},{9,8},{10,9},{11,1... | collective-permute-start | bytes 393224 | tf_op jit(solution)/shard_map/ppermute | solution.py:350
  5.7 0.0 copy-start.7
  5.7 0.0 copy-start.6
  5.8 2.5 %collective-permute-start = (f32[4,64,128]{2,1,0:T(8,128)}, f32[4,64,128]{2,1,0:T(8,128)S(1)}, u32[]{:S(2)}, u32[]{:S(2)}) collective-permute-start(f32[4,64,128]{2,1,0:T(8,128)} %get-tuple-element.13.own_high), channel_id=1, source_target_pairs={{0,1},{1,2},{2,3},{3,4},{4,5},{5,6},{6,7},{7,8},{8,9},{9,10},{10,1... | collective-permute-start | bytes 393224 | tf_op jit(solution)/shard_map/ppermute | solution.py:350
  8.3 0.2 collective-permute-done.1.rows_above
  8.5 0.0 copy-start
  8.5 5.0 %collective-permute-done.rows_below = f32[4,64,128]{2,1,0:T(8,128)S(1)} collective-permute-done((f32[4,64,128]{2,1,0:T(8,128)}, f32[4,64,128]{2,1,0:T(8,128)S(1)}, u32[]{:S(2)}, u32[]{:S(2)}) %collective-permute-start) | collective-permute-done | bytes 131104 | tf_op jit(solution)/shard_map/ppermute | solution.py:350
  13.6 0.0 copy-done
  13.6 0.0 copy-start.1
  13.6 0.7 copy-done.1
  14.2 1.7 %pack_rims.1 = (f32[2,3,8,128]{3,2,1,0:T(8,128)}, f32[2,3,8,128]{3,2,1,0:T(8,128)}) custom-call(s32[4]{0:T(128)} %pad_add_fusion.meta, f32[64,8,128]{2,1,0:T(8,128)} %theta.5, f32[64,8,128]{2,1,0:T(8,128)} %fuel.5, f32[4,64,128]{2,1,0:T(8,128)} %copy-done.1, f32[4,64,128]{2,1,0:T(8,128)} %copy-done), custom_call_target="tpu_custom_call" | custom-call | tf_op jit(solution)/shard_map/pack_rims/pallas_call | solution.py:386
  16.0 3.4 %collective-permute-start.2 = (f32[2,3,8,128]{3,2,1,0:T(8,128)}, f32[2,3,8,128]{3,2,1,0:T(8,128)S(1)}, u32[]{:S(2)}, u32[]{:S(2)}) collective-permute-start(f32[2,3,8,128]{3,2,1,0:T(8,128)} %get-tuple-element.14), channel_id=1, source_target_pairs={{0,16},{16,32},{32,48},{48,64},{64,80},{80,96},{96,112},{112,128},... | collective-permute-start | bytes 73736 | tf_op jit(solution)/shard_map/ppermute | solution.py:350
  19.4 1.3 %collective-permute-start.3 = (f32[2,3,8,128]{3,2,1,0:T(8,128)}, f32[2,3,8,128]{3,2,1,0:T(8,128)S(1)}, u32[]{:S(2)}, u32[]{:S(2)}) collective-permute-start(f32[2,3,8,128]{3,2,1,0:T(8,128)} %get-tuple-element.15), channel_id=1, source_target_pairs={{16,0},{32,16},{48,32},{64,48},{80,64},{96,80},{112,96},{128,112},... | collective-permute-start | bytes 73736 | tf_op jit(solution)/shard_map/ppermute | solution.py:350
  20.7 0.0 copy-done.7
  20.7 5.5 %collective-permute-start.4 = (f32[2,8,128]{2,1,0:T(8,128)S(1)}, f32[2,8,128]{2,1,0:T(8,128)S(1)}, u32[]{:S(2)}, u32[]{:S(2)}) collective-permute-start(f32[2,8,128]{2,1,0:T(8,128)S(1)} %copy-done.7), channel_id=1, source_target_pairs={{0,32},{16,48},{32,64},{48,80},{64,96},{80,112},{96,128},{112,144}... | collective-permute-start | bytes 24584 | tf_op jit(solution)/shard_map/ppermute | solution.py:350
  26.2 0.0 copy-done.6
  26.2 1.3 %collective-permute-start.5 = (f32[2,8,128]{2,1,0:T(8,128)S(1)}, f32[2,8,128]{2,1,0:T(8,128)S(1)}, u32[]{:S(2)}, u32[]{:S(2)}) collective-permute-start(f32[2,8,128]{2,1,0:T(8,128)S(1)} %copy-done.6), channel_id=1, source_target_pairs={{32,0},{48,16},{64,32},{80,48},{96,64},{112,80},{128,96},{144,112}... | collective-permute-start | bytes 24584 | tf_op jit(solution)/shard_map/ppermute | solution.py:350
  27.5 0.0 collective-permute-done.4.from_below_2
  27.5 0.0 copy-start.4
  27.5 7.0 %collective-permute-done.5.from_above_2 = f32[2,8,128]{2,1,0:T(8,128)S(1)} collective-permute-done((f32[2,8,128]{2,1,0:T(8,128)S(1)}, f32[2,8,128]{2,1,0:T(8,128)S(1)}, u32[]{:S(2)}, u32[]{:S(2)}) %collective-permute-start.5) | collective-permute-done | bytes 8224 | tf_op jit(solution)/shard_map/ppermute | solution.py:350
  34.6 0.0 collective-permute-done.2.from_below
  34.6 0.0 copy-start.2
  34.6 0.0 collective-permute-done.3.from_above
  34.6 0.0 copy-done.4
  34.6 0.6 copy-done.5
  35.2 0.0 copy-done.2
  35.2 0.6 copy-done.3
  35.8 9.8 %advance_and_render.1 = (f32[64,8,128]{2,1,0:T(8,128)}, f32[64,8,128]{2,1,0:T(8,128)}, f32[128,128]{1,0:T(8,128)}) custom-call(s32[4]{0:T(128)} %pad_add_fusion.meta, s32[4]{0:T(128)} %choice.1, s32[4]{0:T(128)} %camera.3, f32[64,8,128]{2,1,0:T(8,128)} %theta.5, f32[64,8,128]{2,1,0:T(8,128)} %fuel.5, bf16[8,4,128]{2,1,0:T(4,128)(2,1)} %library.1, ...), custom_call_target="tpu_custom_call" | custom-call | tf_op jit(solution)/shard_map/advance_and_render/pallas_call | solution.py:397
  45.6 26.8 %all_to_all.11 = f32[64,2,128]{2,1,0:T(2,128)} all-to-all(f32[64,2,128]{2,1,0:T(2,128)} %bitcast.4), channel_id=1, replica_groups=mesh['depth'=64,'lat'=16] {'depth'}, dimensions={0} | all-to-all | bytes 131072 | tf_op jit(solution)/shard_map/all_to_all | solution.py:429
  72.4 1.7 %composite.1 = f32[4,4,1,16]{3,2,1,0:T(1,128)} custom-call(s32[4]{0:T(128)} %camera.3, f32[128,128]{1,0:T(8,128)} %bitcast.3), custom_call_target="tpu_custom_call" | custom-call | tf_op jit(solution)/shard_map/composite/pallas_call | solution.py:430
  (2 shorter events, 0.0 us)
Async XLA Ops:
  3.8 4.7 %collective-permute-start.1 = (f32[4,64,128]{2,1,0:T(8,128)}, f32[4,64,128]{2,1,0:T(8,128)S(1)}, u32[]{:S(2)}, u32[]{:S(2)}) collective-permute-start(f32[4,64,128]{2,1,0:T(8,128)} %get-tuple-element.12.own_low), channel_id=1, source_target_pairs={{1,0},{2,1},{3,2},{4,3},{5,4},{6,5},{7,6},{8,7},{9,8},{10,9},{11,1... | collective-permute-start | bytes 393224 | tf_op jit(solution)/shard_map/ppermute | solution.py:350
  5.7 14.9 %copy-start.7 = (f32[2,8,128]{2,1,0:T(8,128)S(1)}, f32[2,8,128]{2,1,0:T(8,128)}, u32[]{:S(2)}) copy-start(f32[2,8,128]{2,1,0:T(8,128)} %get-tuple-element.16) | copy-start | bytes 24580
  5.7 20.4 %copy-start.6 = (f32[2,8,128]{2,1,0:T(8,128)S(1)}, f32[2,8,128]{2,1,0:T(8,128)}, u32[]{:S(2)}) copy-start(f32[2,8,128]{2,1,0:T(8,128)} %get-tuple-element.17) | copy-start | bytes 24580
  5.8 7.8 %collective-permute-start = (f32[4,64,128]{2,1,0:T(8,128)}, f32[4,64,128]{2,1,0:T(8,128)S(1)}, u32[]{:S(2)}, u32[]{:S(2)}) collective-permute-start(f32[4,64,128]{2,1,0:T(8,128)} %get-tuple-element.13.own_high), channel_id=1, source_target_pairs={{0,1},{1,2},{2,3},{3,4},{4,5},{5,6},{6,7},{7,8},{8,9},{9,10},{10,1... | collective-permute-start | bytes 393224 | tf_op jit(solution)/shard_map/ppermute | solution.py:350
  8.5 5.0 %copy-start = (f32[4,64,128]{2,1,0:T(8,128)}, f32[4,64,128]{2,1,0:T(8,128)S(1)}, u32[]{:S(2)}) copy-start(f32[4,64,128]{2,1,0:T(8,128)S(1)} %collective-permute-done.1.rows_above) | copy-start | bytes 393220
  13.6 0.7 copy-start.1
  16.0 18.6 %collective-permute-start.2 = (f32[2,3,8,128]{3,2,1,0:T(8,128)}, f32[2,3,8,128]{3,2,1,0:T(8,128)S(1)}, u32[]{:S(2)}, u32[]{:S(2)}) collective-permute-start(f32[2,3,8,128]{3,2,1,0:T(8,128)} %get-tuple-element.14), channel_id=1, source_target_pairs={{0,16},{16,32},{32,48},{48,64},{64,80},{80,96},{96,112},{112,128},... | collective-permute-start | bytes 73736 | tf_op jit(solution)/shard_map/ppermute | solution.py:350
  19.4 15.2 %collective-permute-start.3 = (f32[2,3,8,128]{3,2,1,0:T(8,128)}, f32[2,3,8,128]{3,2,1,0:T(8,128)S(1)}, u32[]{:S(2)}, u32[]{:S(2)}) collective-permute-start(f32[2,3,8,128]{3,2,1,0:T(8,128)} %get-tuple-element.15), channel_id=1, source_target_pairs={{16,0},{32,16},{48,32},{64,48},{80,64},{96,80},{112,96},{128,112},... | collective-permute-start | bytes 73736 | tf_op jit(solution)/shard_map/ppermute | solution.py:350
  20.7 6.8 %collective-permute-start.4 = (f32[2,8,128]{2,1,0:T(8,128)S(1)}, f32[2,8,128]{2,1,0:T(8,128)S(1)}, u32[]{:S(2)}, u32[]{:S(2)}) collective-permute-start(f32[2,8,128]{2,1,0:T(8,128)S(1)} %copy-done.7), channel_id=1, source_target_pairs={{0,32},{16,48},{32,64},{48,80},{64,96},{80,112},{96,128},{112,144}... | collective-permute-start | bytes 24584 | tf_op jit(solution)/shard_map/ppermute | solution.py:350
  26.2 8.4 %collective-permute-start.5 = (f32[2,8,128]{2,1,0:T(8,128)S(1)}, f32[2,8,128]{2,1,0:T(8,128)S(1)}, u32[]{:S(2)}, u32[]{:S(2)}) collective-permute-start(f32[2,8,128]{2,1,0:T(8,128)S(1)} %copy-done.6), channel_id=1, source_target_pairs={{32,0},{48,16},{64,32},{80,48},{96,64},{112,80},{128,96},{144,112}... | collective-permute-start | bytes 24584 | tf_op jit(solution)/shard_map/ppermute | solution.py:350
  27.5 7.1 %copy-start.4 = (f32[2,8,128]{2,1,0:T(8,128)}, f32[2,8,128]{2,1,0:T(8,128)S(1)}, u32[]{:S(2)}) copy-start(f32[2,8,128]{2,1,0:T(8,128)S(1)} %collective-permute-done.4.from_below_2) | copy-start | bytes 24580
  34.6 0.6 copy-start.5
  34.6 0.6 copy-start.2
  35.2 0.6 copy-start.3

commit v2 on v1

v2 whole, which is shorter than its diff:
```python
import functools

import jax
import jax.numpy as jnp
from jax import lax
from jax.experimental import pallas as pl
from jax.experimental.pallas import tpu as pltpu
from jax.sharding import PartitionSpec as P

MEAN_DEPTH = 32
STEPS = 2

time_step = 0.03
heat_release = 2.0
zeldovich = 8.0
expansion = 0.8

VMEM = pltpu.VMEM
SMEM = pltpu.SMEM
F32 = jnp.float32


def in_vmem():
    return pl.BlockSpec(memory_space=VMEM)


def in_smem():
    return pl.BlockSpec(memory_space=SMEM)


UNROLL_1 = 16
UNROLL_2 = 16


def pack_rows(
    counts, theta, fuel, field0, low_rows, high_rows, last_layer, first_layer, upward, downward, copies
):
    places = theta.shape[0]
    fetch = [
        pltpu.make_async_copy(source, field0.at[number, pl.ds(2, places)], copies.at[number])
        for number, source in enumerate((theta, fuel))
    ]
    for copy in fetch:
        copy.start()
    depth_count = counts[0]
    last = depth_count + 1
    second_last = jnp.maximum(depth_count, 2)
    second = jnp.minimum(3, last)
    size = jnp.broadcast_to(depth_count.astype(F32), (8, 128))
    for number in range(2):
        fetch[number].wait()
        for row in range(2):
            low_rows[2 * number + row] = field0[number, 2 : places + 2, row, :]
            high_rows[2 * number + row] = field0[number, 2 : places + 2, 6 + row, :]
        top = field0[number, last]
        bottom = field0[number, 2]
        last_layer[number] = top
        first_layer[number] = bottom
        upward[number, 0] = top
        upward[number, 1] = field0[number, second_last]
        upward[number, 2] = size
        downward[number, 0] = bottom
        downward[number, 1] = field0[number, second]
        downward[number, 2] = size


def pack_rims(
    counts, upward_in, downward_in, rows_below, rows_above, below_2, above_2, upward, downward
):
    last = counts[0] - 1
    for number in range(2):
        upward[number] = upward_in[number]
        downward[number] = downward_in[number]
        upward[number, 2, 0:1] = rows_below[2 * number + 1, pl.ds(last, 1), :]
        upward[number, 2, 1:2] = rows_above[2 * number, pl.ds(last, 1), :]
        downward[number, 2, 0:1] = rows_below[2 * number + 1, 0:1, :]
        downward[number, 2, 1:2] = rows_above[2 * number, 0:1, :]


def lanes():
    return lax.broadcasted_iota(jnp.int32, (8, 128), 1)


def sublanes():
    return lax.broadcasted_iota(jnp.int32, (8, 128), 0)


def left_of(x):
    return jnp.where(lanes() == 0, 0.0, pltpu.roll(x, 1, 1))


def right_of(x):
    return jnp.where(lanes() == 127, 0.0, pltpu.roll(x, 127, 1))


def row_below(x, halo_row):
    return jnp.where(sublanes() == 0, jnp.broadcast_to(halo_row, (8, 128)), pltpu.roll(x, 1, 0))


def row_above(x, halo_row):
    return jnp.where(sublanes() == 7, jnp.broadcast_to(halo_row, (8, 128)), pltpu.roll(x, 7, 0))


def stepped(heat, fuel, neighbours):
    heat_sum = neighbours[0][0]
    fuel_sum = neighbours[0][1]
    product_sum = neighbours[0][0] * neighbours[0][1]
    square_sum = neighbours[0][0] * neighbours[0][0]
    for heat_n, fuel_n in neighbours[1:]:
        heat_sum = heat_sum + heat_n
        fuel_sum = fuel_sum + fuel_n
        product_sum = product_sum + heat_n * fuel_n
        square_sum = square_sum + heat_n * heat_n
    heat_flux = (heat_sum - 6.0 * heat) + 1.5 * (square_sum - 6.0 * (heat * heat))
    fuel_flux = 0.5 * (
        (1.0 + 1.5 * heat) * (fuel_sum - 6.0 * fuel) + 1.5 * (product_sum - fuel * heat_sum)
    )
    ratio = zeldovich / expansion
    reaction = fuel * jnp.exp(ratio - ratio / ((1.0 - expansion) + expansion * heat))
    return (
        heat + time_step * (heat_flux + heat_release * reaction),
        fuel + time_step * (fuel_flux - reaction),
    )


LEAD = 8


def block_step(field, at, count, edge_rows):
    heat = [field[0, at - 1 + j] for j in range(count + 2)]
    burn = [field[1, at - 1 + j] for j in range(count + 2)]
    results = []
    for j in range(1, count + 1):
        h, b = heat[j], burn[j]
        (h_low, b_low), (h_high, b_high) = edge_rows(j - 1)
        around = [
            (heat[j - 1], burn[j - 1]),
            (heat[j + 1], burn[j + 1]),
            (row_below(h, h_low), row_below(b, b_low)),
            (row_above(h, h_high), row_above(b, b_high)),
            (left_of(h), left_of(b)),
            (right_of(h), right_of(b)),
        ]
        results.append(stepped(h, b, around))
    return results


def rows_beside(edge, sides, place):
    return [tuple(edge[n, side, pl.ds(place, 1), :] for n in range(2)) for side in sides]


def step_edges(edge0, inner, side, at, inner_at, count):
    edge_row = 1 + side
    outer_row = 3 * side

    def rows(ref, row, place):
        found = tuple(ref(n)[row(n), pl.ds(place, count), :] for n in range(2))
        return tuple(jnp.broadcast_to(x, (8, 128)) for x in found)

    def edge(row, shift):
        return rows(lambda n: edge0.at[n], lambda n: row, at + shift)

    heat, burn = edge(edge_row, 0)
    around = [
        edge(edge_row, -1),
        edge(edge_row, 1),
        edge(outer_row, 0),
        rows(lambda n: inner, lambda n: 2 * n + side, inner_at),
        (left_of(heat), left_of(burn)),
        (right_of(heat), right_of(burn)),
    ]
    outside = lax.axis_index("lat") == (0 if side == 0 else lax.axis_size("lat") - 1)
    return [jnp.where(outside, 0.0, x) for x in stepped(heat, burn, around)]


def inner_step(
    places,
    functions,
    all_layers,
    choice,
    camera,
    field0,
    library,
    own_low,
    own_high,
    rows_below,
    rows_above,
    field1,
    edge0,
    edge1,
    low_table,
    rise_table,
    tables,
):
    bins = library.shape[2]
    tables[...] = library[...].astype(F32)
    per_cell = 3.0 / all_layers
    for f in range(functions):
        sign = jnp.where(camera[f] == 0, -per_cell, per_cell)
        for c in range(4):
            low = jnp.broadcast_to(tables[choice[f], c : c + 1, :], (8, bins))
            rise = pltpu.roll(low, bins - 1, 1) - low
            if c == 3:
                low = low * sign
                rise = rise * sign
            low_table[4 * f + c] = low
            rise_table[4 * f + c] = rise

    for number in range(2):
        for row in range(2):
            edge0[number, row, LEAD : LEAD + places] = rows_below[2 * number + row]
            edge0[number, 2 + row, LEAD : LEAD + places] = rows_above[2 * number + row]

    for block in range(places // 8):
        for side in range(2):
            inner = (own_low, own_high)[side]
            fresh = step_edges(edge0, inner, side, LEAD + 8 * block, 8 * block, 8)
            for number in range(2):
                edge1[number, side, 8 * block : 8 * block + 8] = fresh[number]

    unroll = UNROLL_1

    def first_step(block, carry):
        start = block * unroll

        def edge_rows(j):
            return rows_beside(edge0, (1, 2), LEAD + start + j)

        for j, new in enumerate(block_step(field0, start + 2, unroll, edge_rows)):
            for number in range(2):
                field1[number, start + 1 + j] = new[number]
        return carry

    lax.fori_loop(0, places // unroll, first_step, 0)


def outer_step(
    places,
    functions,
    counts,
    camera,
    field0_in,
    field1_in,
    edge0_in,
    edge1_in,
    low_table,
    rise_table,
    own_low,
    own_high,
    from_below,
    from_above,
    from_below_2,
    from_above_2,
    theta_next,
    fuel_next,
    image,
    field0,
    field1,
    edge0,
    edge1,
    result,
    copies,
):
    depth_count = counts[0]
    bins = low_table.shape[2]
    below_size = jnp.broadcast_to(from_below[0, 2, 2:3], (8, 128))
    above_size = jnp.broadcast_to(from_above[0, 2, 2:3], (8, 128))
    for number in range(2):
        field0[number, 0] = jnp.where(below_size == 1.0, from_below_2[number], from_below[number, 1])
        field0[number, 1] = from_below[number, 0]
        field0[number, depth_count + 2] = from_above[number, 0]
        field0[number, depth_count + 3] = jnp.where(
            above_size == 1.0, from_above_2[number], from_above[number, 1]
        )
        for side in range(2):
            edge0[number, 1 + side, LEAD - 1 : LEAD] = from_below[number, 2, side : side + 1]
            edge0[number, 1 + side, pl.ds(LEAD + depth_count, 1)] = from_above[
                number, 2, side : side + 1
            ]
    for place in (0, depth_count - 1):
        for side in range(2):
            fresh = step_edges(edge0, (own_low, own_high)[side], side, LEAD + place, place, 1)
            for number in range(2):
                edge1[number, side, pl.ds(place, 1)] = fresh[number][0:1]
    for place, size in (
        (-1, below_size),
        (0, None),
        (depth_count - 1, None),
        (depth_count, above_size),
    ):

        def edge_rows(j, place=place):
            return rows_beside(edge0, (1, 2), LEAD + place)

        (fresh,) = block_step(field0, place + 2, 1, edge_rows)
        for number in range(2):
            value = fresh[number]
            field1[number, place + 1] = (
                value if size is None else jnp.where(size > 0.0, value, 0.0)
            )

    unroll = UNROLL_2

    def leave(number, first, count):
        return pltpu.make_async_copy(
            result.at[number, pl.ds(first, count)],
            (theta_next, fuel_next)[number].at[pl.ds(first, count)],
            copies.at[number],
        )

    def second_step(block, carry):
        start = block * unroll

        def edge_rows(j):
            return rows_beside(edge1, (0, 1), start + j)

        carry = list(carry)
        for j, new in enumerate(block_step(field1, start + 1, unroll, edge_rows)):
            alive = start + j < depth_count
            for number in range(2):
                value = jnp.where(alive, new[number], 0.0)
                result[number, start + j] = value
                position = jnp.clip(value, 0.0, 1.0) * (bins - 1)
                lower = jnp.minimum(position.astype(jnp.int32), bins - 2)
                fraction = position - lower.astype(F32)

                def look_up(entry):
                    low = jnp.take_along_axis(low_table[entry], lower, axis=1)
                    rise = jnp.take_along_axis(rise_table[entry], lower, axis=1)
                    return low + fraction * rise

                for f in range(2 * number, 2 * number + 2):
                    gone, red, green, blue = carry[4 * f : 4 * f + 4]
                    depth = jnp.where(alive, look_up(4 * f + 3), 0.0)
                    gain = depth * (1.0 + depth * (0.5 + depth * (1.0 / 6.0)))
                    gain = gain + gone * gain
                    carry[4 * f] = gone + gain
                    carry[4 * f + 1] = red + gain * look_up(4 * f)
                    carry[4 * f + 2] = green + gain * look_up(4 * f + 1)
                    carry[4 * f + 3] = blue + gain * look_up(4 * f + 2)
        for number in range(2):
            leave(number, start, unroll).start()
        return tuple(carry)

    zero = jnp.zeros((8, 128), F32)
    sums = lax.fori_loop(0, places // unroll, second_step, (zero,) * (4 * functions))

    channels = []
    for f in range(functions):
        gone, red, green, blue = sums[4 * f : 4 * f + 4]
        scale = jnp.where(camera[f] == 0, -1.0, 1.0 / (1.0 + gone))
        channels += [red * scale, green * scale, blue * scale, gone * scale]

    group = lanes() // 16
    for half in range(2):
        regs = channels[8 * half : 8 * half + 8]
        for bit in (1, 2, 4):
            upper = (group & bit) != 0
            fresh = list(regs)
            for i in range(8):
                if i & bit:
                    continue
                a, b = regs[i], regs[i | bit]
                fresh[i] = jnp.where(upper, pltpu.roll(b, 16 * bit, 1), a)
                fresh[i | bit] = jnp.where(upper, b, pltpu.roll(a, 128 - 16 * bit, 1))
            regs = fresh
        for g in range(8):
            image[pl.ds(2 * g + half, 8, stride=16), :] = regs[g]
    for number in range(2):
        leave(number, 0, places).wait()


def composite(camera, pieces, image):
    sources = pieces.shape[0] // 2
    lane = lanes()
    row = sublanes()
    opacity_lane = lane // 64 * 64 + 48 + lane % 16
    for half in range(2):
        forward = jnp.where(
            lane < 64,
            (camera[2 * half] == 0).astype(jnp.int32),
            (camera[2 * half + 1] == 0).astype(jnp.int32),
        ) == 1
        values, clear, through = [], [], []
        carry = jnp.ones((8, 128), F32)
        for block in range(sources // 8):
            value = pieces[pl.ds(16 * block + half, 8, stride=2), :]
            passing = 1.0 - jnp.take_along_axis(value, opacity_lane, axis=1)
            product = passing
            for shift in (1, 2, 4):
                product = product * jnp.where(row >= shift, pltpu.roll(product, shift, 0), 1.0)
            product = product * carry
            carry = jnp.broadcast_to(product[7:8], (8, 128))
            values.append(value)
            clear.append(passing)
            through.append(product)
        total = jnp.zeros((8, 128), F32)
        for value, passing, product in zip(values, clear, through):
            top = jnp.where(forward, product, carry)
            bottom = jnp.where(forward, passing, product)
            total = total + value * (top / bottom)
        line = jnp.sum(total, axis=0, keepdims=True)
        for clo in range(8):
            channel = 8 * half + clo
            image[channel // 4, channel % 4] = line[:, 16 * clo : 16 * clo + 16]


def shifted(array, axis, by):
    count = lax.axis_size(axis)
    pairs = [(i, i + by) for i in range(count) if 0 <= i + by < count]
    return lax.ppermute(array, axis, pairs)


def held(array):
    return pltpu.with_memory_space_constraint(array, VMEM)


def in_hbm(array):
    return pltpu.with_memory_space_constraint(array, pltpu.HBM)


def params():
    return pltpu.CompilerParams(vmem_limit_bytes=16 * 1024 * 1024)


def anywhere():
    return pl.BlockSpec(memory_space=pl.ANY)


def first_kernel(active_sheet_number, thermal_values, reactant_fraction):
    places = thermal_values.shape[0]
    rows = VMEM((4, places, 128), F32)
    layers = VMEM((2, 8, 128), F32)
    rim = VMEM((2, 3, 8, 128), F32)
    return pl.pallas_call(
        pack_rows,
        out_shape=(VMEM((2, places + 4, 8, 128), F32), rows, rows, layers, layers, rim, rim),
        in_specs=[in_smem()] + [anywhere()] * 2,
        out_specs=(in_vmem(),) * 7,
        scratch_shapes=[pltpu.SemaphoreType.DMA((2,))],
        compiler_params=params(),
        name="pack_rows",
    )(active_sheet_number, *map(in_hbm, (thermal_values, reactant_fraction)))


def rim_kernel(counts, upward, downward, *received):
    rim = VMEM((2, 3, 8, 128), F32)
    return pl.pallas_call(
        pack_rims,
        out_shape=(rim, rim),
        in_specs=[in_smem()] + [in_vmem()] * 6,
        out_specs=(in_vmem(),) * 2,
        compiler_params=params(),
        name="pack_rims",
    )(counts, *map(held, (upward, downward, *received)))


def inner_kernel(devices, choice, camera, field0, library, *rows):
    places = field0.shape[1] - 4
    functions = choice.shape[0]
    bins = library.shape[2]
    table = VMEM((4 * functions, 8, bins), F32)
    return pl.pallas_call(
        functools.partial(inner_step, places, functions, float(MEAN_DEPTH * devices)),
        out_shape=(
            VMEM((2, places + 2, 8, 128), F32),
            VMEM((2, 4, places + 16, 128), F32),
            VMEM((2, 2, places, 128), F32),
            table,
            table,
        ),
        in_specs=[in_smem()] * 2 + [in_vmem()] * 6,
        out_specs=(in_vmem(),) * 5,
        scratch_shapes=[VMEM(library.shape, F32)],
        compiler_params=params(),
        cost_estimate=pl.CostEstimate(flops=10**7, bytes_accessed=10**6, transcendentals=10**5),
        name="inner_step",
    )(choice, camera, held(field0), library, *map(held, rows))


def outer_kernel(devices, counts, camera, *arrays):
    field0, field1, edge0, edge1 = arrays[:4]
    places = field0.shape[1] - 4
    functions = camera.shape[0]
    field = jax.ShapeDtypeStruct((places, 8, 128), F32)
    return pl.pallas_call(
        functools.partial(outer_step, places, functions),
        out_shape=(field, field, VMEM((2 * devices, 128), F32))
        + tuple(VMEM(x.shape, F32) for x in (field0, field1, edge0, edge1)),
        in_specs=[in_smem()] * 2 + [in_vmem()] * len(arrays),
        out_specs=(anywhere(),) * 2 + (in_vmem(),) * 5,
        scratch_shapes=[
            VMEM((2, places, 8, 128), F32),
            pltpu.SemaphoreType.DMA((2,)),
        ],
        input_output_aliases={2 + i: 3 + i for i in range(4)},
        compiler_params=params(),
        cost_estimate=pl.CostEstimate(flops=2 * 10**7, bytes_accessed=10**6, transcendentals=10**5),
        name="outer_step",
    )(counts, camera, *map(held, arrays))[:3]


def last_kernel(functions, camera, pieces):
    return pl.pallas_call(
        composite,
        out_shape=jax.ShapeDtypeStruct((functions, 4, 1, 16), F32),
        in_specs=[in_smem(), in_vmem()],
        out_specs=in_vmem(),
        compiler_params=params(),
        name="composite",
    )(camera, held(pieces))


def on_device(
    thermal_values,
    reactant_fraction,
    active_sheet_number,
    colour_lookup_library,
    colour_lookup_choice,
    camera_direction,
):
    devices = lax.axis_size("depth")
    field0, own_low, own_high, last_layer, first_layer, upward, downward = first_kernel(
        active_sheet_number, thermal_values, reactant_fraction
    )
    rows_below = shifted(own_high, "lat", 1)
    rows_above = shifted(own_low, "lat", -1)
    below_2 = shifted(last_layer, "depth", 2)
    above_2 = shifted(first_layer, "depth", -2)
    upward, downward = rim_kernel(
        active_sheet_number, upward, downward, rows_below, rows_above, below_2, above_2
    )
    from_below = shifted(upward, "depth", 1)
    from_above = shifted(downward, "depth", -1)
    field1, edge0, edge1, low_table, rise_table = inner_kernel(
        devices,
        colour_lookup_choice,
        camera_direction,
        field0,
        colour_lookup_library,
        own_low,
        own_high,
        rows_below,
        rows_above,
    )
    theta_next, fuel_next, pieces = outer_kernel(
        devices,
        active_sheet_number,
        camera_direction,
        field0,
        field1,
        edge0,
        edge1,
        low_table,
        rise_table,
        own_low,
        own_high,
        from_below,
        from_above,
        below_2,
        above_2,
    )
    pieces = lax.all_to_all(pieces, "depth", 0, 0, tiled=True)
    image = last_kernel(colour_lookup_choice.shape[0], camera_direction, pieces)
    return (theta_next, fuel_next, image)


def solution(mesh):
    placed = (P("depth", "lat", None), P("depth", "lat", None), P("depth"), P(), P(), P())
    return jax.shard_map(
        on_device,
        mesh=mesh,
        in_specs=placed,
        out_specs=(P("depth", "lat", None), P("depth", "lat", None), P(None, None, "lat", "depth")),
        check_vma=False,
    )
```

time: 74.5 us -> 60.4 us (0.81)
  the two profiles are of different devices: /device:TPU:512 before, /device:TPU:385 now
where the time goes in v2:
time: 60.4 us; the launch traced here: 60 us
  blocking collectives  24 us (40%)
  starting transfers between devices  17.5 us (29%)
  waiting for transfers between devices  8.82 us (15%)
  Pallas kernels  8.31 us (14%)
  between operations  1.41 us (2%)
    all_to_all x1, blocking collectives, on_device(): pieces = lax.all_to_all(pieces, 'depth', 0, 0, tiled=True)  24 us
    ppermute x6, starting transfers between devices, shifted(): return lax.ppermute(array, axis, pairs)  17.5 us
    ppermute x6, waiting for transfers between devices, shifted(): return lax.ppermute(array, axis, pairs)  8.82 us
    pallas_call x1, Pallas kernels, outer_kernel(): pl.pallas_call(functools.partial(outer_step, places, functions), out_shap...  4.38 us
    pallas_call x1, Pallas kernels, inner_kernel(): pl.pallas_call(functools.partial(inner_step, places, functions, float(MEA...  1.45 us
    pallas_call x1, Pallas kernels, last_kernel(): pl.pallas_call(composite, out_shape=jax.ShapeDtypeStruct((functions, 4, 1...  1.35 us
  transfers between devices with their start and end apart: 6, of which 2 were waited for; matrix products, arithmetic and copies ran while one was open for 0% of the time, Pallas kernels for 2%

profile of v2, /device:TPU:385, one launch (start us, length us, event | category | flops | bytes accessed | tf_op | source)
XLA Modules:
  0.0 60.0 jit_solution(17693012836617345876)
XLA Ops:
  1.3 1.1 %pack_rows.1 = (f32[2,68,8,128]{3,2,1,0:T(8,128)S(1)}, f32[4,64,128]{2,1,0:T(8,128)S(1)}, f32[4,64,128]{2,1,0:T(8,128)S(1)}, f32[2,8,128]{2,1,0:T(8,128)S(1)}, f...) custom-call(s32[1]{0:T(128)S(6)} %copy.17.counts, f32[64,8,128]{2,1,0:T(8,128)} %theta.1, ...), custom_call_target="tpu_custom_call" | custom-call | tf_op jit(solution)/shard_map/pack_rows/pallas_call | solution.py:435
  2.4 2.6 %collective-permute-start.1 = (f32[4,64,128]{2,1,0:T(8,128)S(1)}, f32[4,64,128]{2,1,0:T(8,128)S(1)}, u32[]{:S(2)}, u32[]{:S(2)}) collective-permute-start(f32[4,64,128]{2,1,0:T(8,128)S(1)} %get-tuple-element.21.own_low), channel_id=1, source_target_pairs={{1,0},{2,1},{3,2},{4,3},{5,4},{6,5},{7,6},{8,7},{9,8},{10,9},{11,1... | collective-permute-start | bytes 393224 | tf_op jit(solution)/shard_map/ppermute | solution.py:411
  5.0 6.0 %collective-permute-start = (f32[4,64,128]{2,1,0:T(8,128)S(1)}, f32[4,64,128]{2,1,0:T(8,128)S(1)}, u32[]{:S(2)}, u32[]{:S(2)}) collective-permute-start(f32[4,64,128]{2,1,0:T(8,128)S(1)} %get-tuple-element.22.own_high), channel_id=1, source_target_pairs={{0,1},{1,2},{2,3},{3,4},{4,5},{5,6},{6,7},{7,8},{8,9},{9,10},{10,1... | collective-permute-start | bytes 393224 | tf_op jit(solution)/shard_map/ppermute | solution.py:411
  11.0 4.0 %collective-permute-start.2 = (f32[2,8,128]{2,1,0:T(8,128)S(1)}, f32[2,8,128]{2,1,0:T(8,128)S(1)}, u32[]{:S(2)}, u32[]{:S(2)}) collective-permute-start(f32[2,8,128]{2,1,0:T(8,128)S(1)} %get-tuple-element.30), channel_id=1, source_target_pairs={{0,32},{16,48},{32,64},{48,80},{64,96},{80,112},{96,128},{112,144}... | collective-permute-start | bytes 24584 | tf_op jit(solution)/shard_map/ppermute | solution.py:411
  15.1 1.3 %collective-permute-start.3 = (f32[2,8,128]{2,1,0:T(8,128)S(1)}, f32[2,8,128]{2,1,0:T(8,128)S(1)}, u32[]{:S(2)}, u32[]{:S(2)}) collective-permute-start(f32[2,8,128]{2,1,0:T(8,128)S(1)} %get-tuple-element.31), channel_id=1, source_target_pairs={{32,0},{48,16},{64,32},{80,48},{96,64},{112,80},{128,96},{144,112}... | collective-permute-start | bytes 24584 | tf_op jit(solution)/shard_map/ppermute | solution.py:411
  16.4 0.0 collective-permute-done.2.below_2.from_below_2
  16.4 5.0 %collective-permute-done.3.above_2.from_above_2 = f32[2,8,128]{2,1,0:T(8,128)S(1)} collective-permute-done((f32[2,8,128]{2,1,0:T(8,128)S(1)}, f32[2,8,128]{2,1,0:T(8,128)S(1)}, u32[]{:S(2)}, u32[]{:S(2)}) %collective-permute-start.3) | collective-permute-done | bytes 8224 | tf_op jit(solution)/shard_map/ppermute | solution.py:411
  21.4 0.0 collective-permute-done.1.rows_above
  21.4 0.0 collective-permute-done.rows_below
  21.4 0.0 copy-start
  21.4 2.3 %collective-permute-start.4 = (f32[2,3,8,128]{3,2,1,0:T(8,128)S(1)}, f32[2,3,8,128]{3,2,1,0:T(8,128)S(1)}, u32[]{:S(2)}, u32[]{:S(2)}) collective-permute-start(f32[2,3,8,128]{3,2,1,0:T(8,128)S(1)} %get-tuple-element.32), channel_id=1, source_target_pairs={{0,16},{16,32},{32,48},{48,64},{64,80},{80,96},{96,112},{112,128},... | collective-permute-start | bytes 73736 | tf_op jit(solution)/shard_map/ppermute | solution.py:411
  23.7 0.0 copy-start.1
  23.7 0.0 copy-start.2
  23.7 1.3 %collective-permute-start.5 = (f32[2,3,8,128]{3,2,1,0:T(8,128)S(1)}, f32[2,3,8,128]{3,2,1,0:T(8,128)S(1)}, u32[]{:S(2)}, u32[]{:S(2)}) collective-permute-start(f32[2,3,8,128]{3,2,1,0:T(8,128)S(1)} %get-tuple-element.33), channel_id=1, source_target_pairs={{16,0},{32,16},{48,32},{64,48},{80,64},{96,80},{112,96},{128,112},... | collective-permute-start | bytes 73736 | tf_op jit(solution)/shard_map/ppermute | solution.py:411
  25.0 0.0 copy-done
  25.0 0.0 copy-done.1
  25.0 0.0 copy-done.2
  25.0 1.4 %inner_step.1 = (f32[2,66,8,128]{3,2,1,0:T(8,128)S(1)}, f32[2,4,80,128]{3,2,1,0:T(8,128)S(1)}, f32[2,2,64,128]{3,2,1,0:T(8,128)S(1)}, f32[16,8,128]{2,1,0:T(8,128)S(1)}, f32[16,8,128]{2,1,0:T(8,128)S(1)}) custom-call(s32[4]{0:T(128)S(1)} %copy-done.2, s32[4]{0:T(128)S(1)} %copy-done.1, f32[2,68,8,128]{3,2,1,0:T(8,128)S(1)} %get-tuple-element.20.field0.field0_in, ...), custom_call_target="tpu_custom_call" | custom-call | flops 10000000 | bytes 1000000 | tf_op jit(solution)/shard_map/inner_step/pallas_call | solution.py:463
  26.5 0.0 collective-permute-done.4.from_below
  26.5 3.8 %collective-permute-done.5.from_above = f32[2,3,8,128]{3,2,1,0:T(8,128)S(1)} collective-permute-done((f32[2,3,8,128]{3,2,1,0:T(8,128)S(1)}, f32[2,3,8,128]{3,2,1,0:T(8,128)S(1)}, u32[]{:S(2)}, u32[]{:S(2)}) %collective-permute-start.5) | collective-permute-done | bytes 24608 | tf_op jit(solution)/shard_map/ppermute | solution.py:411
  30.3 4.4 %outer_step.1 = (f32[64,8,128]{2,1,0:T(8,128)}, f32[64,8,128]{2,1,0:T(8,128)}, f32[128,128]{1,0:T(8,128)S(1)}, f32[2,68,8,128]{3,2,1,0:T(8,128)S(1)}, f32[2,66,8...) custom-call(s32[1]{0:T(128)S(6)} %copy.17.counts, ...), custom_call_target="tpu_custom_call", output_to_operand_aliasing={{3}: (2, {}), {4}: (3, {}), {5}: (4, {}), {6}: (5, {})} | custom-call | flops 20000000 | bytes 1000000 | tf_op jit(solution)/shard_map/outer_step/pallas_call | solution.py:486
  34.7 24.0 %all_to_all.11 = f32[64,2,128]{2,1,0:T(2,128)S(1)} all-to-all(f32[64,2,128]{2,1,0:T(2,128)S(1)} %bitcast.3), channel_id=1, replica_groups=mesh['depth'=64,'lat'=16] {'depth'}, dimensions={0} | all-to-all | bytes 131072 | tf_op jit(solution)/shard_map/all_to_all | solution.py:563
  58.7 1.4 %composite.1 = f32[4,4,1,16]{3,2,1,0:T(1,128)} custom-call(s32[4]{0:T(128)S(1)} %copy-done.1, f32[128,128]{1,0:T(8,128)S(1)} %bitcast.2), custom_call_target="tpu_custom_call" | custom-call | tf_op jit(solution)/shard_map/composite/pallas_call | solution.py:504
  (1 shorter events, 0.0 us)
Async XLA Ops:
  2.4 19.0 %collective-permute-start.1 = (f32[4,64,128]{2,1,0:T(8,128)S(1)}, f32[4,64,128]{2,1,0:T(8,128)S(1)}, u32[]{:S(2)}, u32[]{:S(2)}) collective-permute-start(f32[4,64,128]{2,1,0:T(8,128)S(1)} %get-tuple-element.21.own_low), channel_id=1, source_target_pairs={{1,0},{2,1},{3,2},{4,3},{5,4},{6,5},{7,6},{8,7},{9,8},{10,9},{11,1... | collective-permute-start | bytes 393224 | tf_op jit(solution)/shard_map/ppermute | solution.py:411
  5.0 16.4 %collective-permute-start = (f32[4,64,128]{2,1,0:T(8,128)S(1)}, f32[4,64,128]{2,1,0:T(8,128)S(1)}, u32[]{:S(2)}, u32[]{:S(2)}) collective-permute-start(f32[4,64,128]{2,1,0:T(8,128)S(1)} %get-tuple-element.22.own_high), channel_id=1, source_target_pairs={{0,1},{1,2},{2,3},{3,4},{4,5},{5,6},{6,7},{7,8},{8,9},{9,10},{10,1... | collective-permute-start | bytes 393224 | tf_op jit(solution)/shard_map/ppermute | solution.py:411
  11.0 5.4 %collective-permute-start.2 = (f32[2,8,128]{2,1,0:T(8,128)S(1)}, f32[2,8,128]{2,1,0:T(8,128)S(1)}, u32[]{:S(2)}, u32[]{:S(2)}) collective-permute-start(f32[2,8,128]{2,1,0:T(8,128)S(1)} %get-tuple-element.30), channel_id=1, source_target_pairs={{0,32},{16,48},{32,64},{48,80},{64,96},{80,112},{96,128},{112,144}... | collective-permute-start | bytes 24584 | tf_op jit(solution)/shard_map/ppermute | solution.py:411
  15.1 6.3 %collective-permute-start.3 = (f32[2,8,128]{2,1,0:T(8,128)S(1)}, f32[2,8,128]{2,1,0:T(8,128)S(1)}, u32[]{:S(2)}, u32[]{:S(2)}) collective-permute-start(f32[2,8,128]{2,1,0:T(8,128)S(1)} %get-tuple-element.31), channel_id=1, source_target_pairs={{32,0},{48,16},{64,32},{80,48},{96,64},{112,80},{128,96},{144,112}... | collective-permute-start | bytes 24584 | tf_op jit(solution)/shard_map/ppermute | solution.py:411
  21.4 3.6 %copy-start = (bf16[8,4,128]{2,1,0:T(4,128)(2,1)S(1)}, bf16[8,4,128]{2,1,0:T(4,128)(2,1)}, u32[]{:S(2)}) copy-start(bf16[8,4,128]{2,1,0:T(4,128)(2,1)} %library.1) | copy-start | bytes 24580
  21.4 5.1 %collective-permute-start.4 = (f32[2,3,8,128]{3,2,1,0:T(8,128)S(1)}, f32[2,3,8,128]{3,2,1,0:T(8,128)S(1)}, u32[]{:S(2)}, u32[]{:S(2)}) collective-permute-start(f32[2,3,8,128]{3,2,1,0:T(8,128)S(1)} %get-tuple-element.32), channel_id=1, source_target_pairs={{0,16},{16,32},{32,48},{48,64},{64,80},{80,96},{96,112},{112,128},... | collective-permute-start | bytes 73736 | tf_op jit(solution)/shard_map/ppermute | solution.py:411
  23.7 1.3 %copy-start.1 = (s32[4]{0:T(128)S(1)}, s32[4]{0:T(128)}, u32[]{:S(2)}) copy-start(s32[4]{0:T(128)} %camera.5) | copy-start | bytes 52
  23.7 1.3 %copy-start.2 = (s32[4]{0:T(128)S(1)}, s32[4]{0:T(128)}, u32[]{:S(2)}) copy-start(s32[4]{0:T(128)} %choice.1) | copy-start | bytes 52
  23.7 6.6 %collective-permute-start.5 = (f32[2,3,8,128]{3,2,1,0:T(8,128)S(1)}, f32[2,3,8,128]{3,2,1,0:T(8,128)S(1)}, u32[]{:S(2)}, u32[]{:S(2)}) collective-permute-start(f32[2,3,8,128]{3,2,1,0:T(8,128)S(1)} %get-tuple-element.33), channel_id=1, source_target_pairs={{16,0},{32,16},{48,32},{64,48},{80,64},{96,80},{112,96},{128,112},... | collective-permute-start | bytes 73736 | tf_op jit(solution)/shard_map/ppermute | solution.py:411

commit v3 on v2

--- a/solution.py
+++ b/solution.py
@@ -32,49 +32,91 @@
 UNROLL_2 = 16
 
 
+def is_even(axis):
+    return lax.rem(lax.axis_index(axis), 2) == 0
+
+
+def select(which, first, second):
+    return jnp.where(which, first, second)
+
+
 def pack_rows(
-    counts, theta, fuel, field0, low_rows, high_rows, last_layer, first_layer, upward, downward, copies
+    counts_in,
+    choice_in,
+    camera_in,
+    theta,
+    fuel,
+    library_in,
+    counts,
+    choice,
+    camera,
+    library,
+    field0,
+    own_rows,
+    rows_pair,
+    rows_gap,
+    rim_pair,
+    rim_gap,
+    copies,
 ):
     places = theta.shape[0]
+    moves = [
+        (counts_in, counts),
+        (theta, field0.at[0, pl.ds(2, places)]),
+        (fuel, field0.at[1, pl.ds(2, places)]),
+        (choice_in, choice),
+        (camera_in, camera),
+        (library_in, library),
+    ]
     fetch = [
-        pltpu.make_async_copy(source, field0.at[number, pl.ds(2, places)], copies.at[number])
-        for number, source in enumerate((theta, fuel))
+        pltpu.make_async_copy(source, target, copies.at[number])
+        for number, (source, target) in enumerate(moves)
     ]
     for copy in fetch:
         copy.start()
+    lat_even, depth_even = is_even("lat"), is_even("depth")
+    for number in range(2):
+        fetch[1 + number].wait()
+        for row in range(2):
+            low = field0[number, 2 : places + 2, row, :]
+            high = field0[number, 2 : places + 2, 6 + row, :]
+            rows_pair[2 * number + row] = select(lat_even, high, low)
+            rows_gap[2 * number + row] = select(lat_even, low, high)
+            own_rows[2 * row + number] = (low, high)[row]
+    fetch[0].wait()
     depth_count = counts[0]
     last = depth_count + 1
     second_last = jnp.maximum(depth_count, 2)
     second = jnp.minimum(3, last)
     size = jnp.broadcast_to(depth_count.astype(F32), (8, 128))
     for number in range(2):
-        fetch[number].wait()
-        for row in range(2):
-            low_rows[2 * number + row] = field0[number, 2 : places + 2, row, :]
-            high_rows[2 * number + row] = field0[number, 2 : places + 2, 6 + row, :]
-        top = field0[number, last]
-        bottom = field0[number, 2]
-        last_layer[number] = top
-        first_layer[number] = bottom
-        upward[number, 0] = top
-        upward[number, 1] = field0[number, second_last]
-        upward[number, 2] = size
-        downward[number, 0] = bottom
-        downward[number, 1] = field0[number, second]
-        downward[number, 2] = size
-
-
-def pack_rims(
-    counts, upward_in, downward_in, rows_below, rows_above, below_2, above_2, upward, downward
-):
+        up = (field0[number, last], field0[number, second_last], size)
+        down = (field0[number, 2], field0[number, second], size)
+        for layer in range(3):
+            rim_pair[number, layer] = select(depth_even, up[layer], down[layer])
+            rim_gap[number, layer] = select(depth_even, down[layer], up[layer])
+    for copy in fetch[3:]:
+        copy.wait()
+
+
+def pack_rims(counts, rows_pair, rows_gap, rim_pair, rim_gap, next_pair, next_gap):
     last = counts[0] - 1
+    lat_even, depth_even = is_even("lat"), is_even("depth")
     for number in range(2):
-        upward[number] = upward_in[number]
-        downward[number] = downward_in[number]
-        upward[number, 2, 0:1] = rows_below[2 * number + 1, pl.ds(last, 1), :]
-        upward[number, 2, 1:2] = rows_above[2 * number, pl.ds(last, 1), :]
-        downward[number, 2, 0:1] = rows_below[2 * number + 1, 0:1, :]
-        downward[number, 2, 1:2] = rows_above[2 * number, 0:1, :]
+        from_above = select(depth_even, rim_pair[number, 0], rim_gap[number, 0])
+        from_below = select(depth_even, rim_gap[number, 0], rim_pair[number, 0])
+
+        def beside(place):
+            below = [ref[2 * number + 1, pl.ds(place, 1), :] for ref in (rows_gap, rows_pair)]
+            above = [ref[2 * number, pl.ds(place, 1), :] for ref in (rows_pair, rows_gap)]
+            rows = [select(lat_even, *below), select(lat_even, *above)]
+            return jnp.where(sublanes() == 0, *(jnp.broadcast_to(x, (8, 128)) for x in rows))
+
+        up = (from_below, beside(last))
+        down = (from_above, beside(0))
+        for layer in range(2):
+            next_pair[number, layer] = select(depth_even, up[layer], down[layer])
+            next_gap[number, layer] = select(depth_even, down[layer], up[layer])
 
 
 def lanes():
@@ -165,7 +207,7 @@
         edge(edge_row, -1),
         edge(edge_row, 1),
         edge(outer_row, 0),
-        rows(lambda n: inner, lambda n: 2 * n + side, inner_at),
+        rows(lambda n: inner, lambda n: 2 * side + n, inner_at),
         (left_of(heat), left_of(burn)),
         (right_of(heat), right_of(burn)),
     ]
@@ -177,14 +219,17 @@
     places,
     functions,
     all_layers,
+    counts,
     choice,
     camera,
+    field0_in,
+    library,
+    own_rows,
+    rows_pair,
+    rows_gap,
+    rim_pair,
+    rim_gap,
     field0,
-    library,
-    own_low,
-    own_high,
-    rows_below,
-    rows_above,
     field1,
     edge0,
     edge1,
@@ -192,6 +237,11 @@
     rise_table,
     tables,
 ):
+    lat_even, depth_even = is_even("lat"), is_even("depth")
+    for number in range(2):
+        above, below = rim_pair[number, 0], rim_gap[number, 0]
+        field0[number, 1] = select(depth_even, below, above)
+        field0[number, counts[0] + 2] = select(depth_even, above, below)
     bins = library.shape[2]
     tables[...] = library[...].astype(F32)
     per_cell = 3.0 / all_layers
@@ -208,13 +258,13 @@
 
     for number in range(2):
         for row in range(2):
-            edge0[number, row, LEAD : LEAD + places] = rows_below[2 * number + row]
-            edge0[number, 2 + row, LEAD : LEAD + places] = rows_above[2 * number + row]
+            pair, gap = rows_pair[2 * number + row], rows_gap[2 * number + row]
+            edge0[number, row, LEAD : LEAD + places] = select(lat_even, gap, pair)
+            edge0[number, 2 + row, LEAD : LEAD + places] = select(lat_even, pair, gap)
 
     for block in range(places // 8):
         for side in range(2):
-            inner = (own_low, own_high)[side]
-            fresh = step_edges(edge0, inner, side, LEAD + 8 * block, 8 * block, 8)
+            fresh = step_edges(edge0, own_rows, side, LEAD + 8 * block, 8 * block, 8)
             for number in range(2):
                 edge1[number, side, 8 * block : 8 * block + 8] = fresh[number]
 
@@ -245,12 +295,11 @@
     edge1_in,
     low_table,
     rise_table,
-    own_low,
-    own_high,
-    from_below,
-    from_above,
-    from_below_2,
-    from_above_2,
+    own_rows,
+    rim_pair,
+    rim_gap,
+    next_pair,
+    next_gap,
     theta_next,
     fuel_next,
     image,
@@ -263,41 +312,45 @@
 ):
     depth_count = counts[0]
     bins = low_table.shape[2]
-    below_size = jnp.broadcast_to(from_below[0, 2, 2:3], (8, 128))
-    above_size = jnp.broadcast_to(from_above[0, 2, 2:3], (8, 128))
+    depth_even = is_even("depth")
+
+    def from_below(pair, gap, *at):
+        return select(depth_even, gap[at], pair[at])
+
+    def from_above(pair, gap, *at):
+        return select(depth_even, pair[at], gap[at])
+
+    below_size = from_below(rim_pair, rim_gap, 0, 2)
+    above_size = from_above(rim_pair, rim_gap, 0, 2)
     for number in range(2):
-        field0[number, 0] = jnp.where(below_size == 1.0, from_below_2[number], from_below[number, 1])
-        field0[number, 1] = from_below[number, 0]
-        field0[number, depth_count + 2] = from_above[number, 0]
+        field0[number, 0] = jnp.where(
+            below_size == 1.0,
+            from_below(next_pair, next_gap, number, 0),
+            from_below(rim_pair, rim_gap, number, 1),
+        )
         field0[number, depth_count + 3] = jnp.where(
-            above_size == 1.0, from_above_2[number], from_above[number, 1]
+            above_size == 1.0,
+            from_above(next_pair, next_gap, number, 0),
+            from_above(rim_pair, rim_gap, number, 1),
         )
+        below_rows = from_below(next_pair, next_gap, number, 1)
+        above_rows = from_above(next_pair, next_gap, number, 1)
         for side in range(2):
-            edge0[number, 1 + side, LEAD - 1 : LEAD] = from_below[number, 2, side : side + 1]
-            edge0[number, 1 + side, pl.ds(LEAD + depth_count, 1)] = from_above[
-                number, 2, side : side + 1
-            ]
+            edge0[number, 1 + side, LEAD - 1 : LEAD] = below_rows[side : side + 1]
+            edge0[number, 1 + side, pl.ds(LEAD + depth_count, 1)] = above_rows[side : side + 1]
     for place in (0, depth_count - 1):
         for side in range(2):
-            fresh = step_edges(edge0, (own_low, own_high)[side], side, LEAD + place, place, 1)
+            fresh = step_edges(edge0, own_rows, side, LEAD + place, place, 1)
             for number in range(2):
                 edge1[number, side, pl.ds(place, 1)] = fresh[number][0:1]
-    for place, size in (
-        (-1, below_size),
-        (0, None),
-        (depth_count - 1, None),
-        (depth_count, above_size),
-    ):
+    for place, size in ((-1, below_size), (depth_count, above_size)):
 
         def edge_rows(j, place=place):
             return rows_beside(edge0, (1, 2), LEAD + place)
 
         (fresh,) = block_step(field0, place + 2, 1, edge_rows)
         for number in range(2):
-            value = fresh[number]
-            field1[number, place + 1] = (
-                value if size is None else jnp.where(size > 0.0, value, 0.0)
-            )
+            field1[number, place + 1] = jnp.where(size > 0.0, fresh[number], 0.0)
 
     unroll = UNROLL_2
 
@@ -405,9 +458,11 @@
             image[channel // 4, channel % 4] = line[:, 16 * clo : 16 * clo + 16]
 
 
-def shifted(array, axis, by):
+def swapped(array, axis, first):
     count = lax.axis_size(axis)
-    pairs = [(i, i + by) for i in range(count) if 0 <= i + by < count]
+    pairs = []
+    for i in range(first, count - 1, 2):
+        pairs += [(i, i + 1), (i + 1, i)]
     return lax.ppermute(array, axis, pairs)
 
 
@@ -427,35 +482,40 @@
     return pl.BlockSpec(memory_space=pl.ANY)
 
 
-def first_kernel(active_sheet_number, thermal_values, reactant_fraction):
-    places = thermal_values.shape[0]
+def in_scalars(array):
+    return pltpu.with_memory_space_constraint(array, SMEM)
+
+
+def first_kernel(counts, choice, camera, theta, fuel, library):
+    places = theta.shape[0]
     rows = VMEM((4, places, 128), F32)
-    layers = VMEM((2, 8, 128), F32)
     rim = VMEM((2, 3, 8, 128), F32)
     return pl.pallas_call(
         pack_rows,
-        out_shape=(VMEM((2, places + 4, 8, 128), F32), rows, rows, layers, layers, rim, rim),
-        in_specs=[in_smem()] + [anywhere()] * 2,
-        out_specs=(in_vmem(),) * 7,
-        scratch_shapes=[pltpu.SemaphoreType.DMA((2,))],
+        out_shape=tuple(SMEM(x.shape, jnp.int32) for x in (counts, choice, camera))
+        + (VMEM(library.shape, library.dtype), VMEM((2, places + 4, 8, 128), F32))
+        + (rows, rows, rows, rim, rim),
+        in_specs=[anywhere()] * 6,
+        out_specs=(in_smem(),) * 3 + (in_vmem(),) * 7,
+        scratch_shapes=[pltpu.SemaphoreType.DMA((6,))],
         compiler_params=params(),
         name="pack_rows",
-    )(active_sheet_number, *map(in_hbm, (thermal_values, reactant_fraction)))
-
-
-def rim_kernel(counts, upward, downward, *received):
-    rim = VMEM((2, 3, 8, 128), F32)
+    )(counts, *map(in_hbm, (choice, camera, theta, fuel, library)))
+
+
+def rim_kernel(counts, *received):
+    rim = VMEM((2, 2, 8, 128), F32)
     return pl.pallas_call(
         pack_rims,
         out_shape=(rim, rim),
-        in_specs=[in_smem()] + [in_vmem()] * 6,
+        in_specs=[in_smem()] + [in_vmem()] * 4,
         out_specs=(in_vmem(),) * 2,
         compiler_params=params(),
         name="pack_rims",
-    )(counts, *map(held, (upward, downward, *received)))
-
-
-def inner_kernel(devices, choice, camera, field0, library, *rows):
+    )(in_scalars(counts), *map(held, received))
+
+
+def inner_kernel(devices, counts, choice, camera, field0, library, *rows):
     places = field0.shape[1] - 4
     functions = choice.shape[0]
     bins = library.shape[2]
@@ -463,19 +523,21 @@
     return pl.pallas_call(
         functools.partial(inner_step, places, functions, float(MEAN_DEPTH * devices)),
         out_shape=(
+            VMEM(field0.shape, F32),
             VMEM((2, places + 2, 8, 128), F32),
             VMEM((2, 4, places + 16, 128), F32),
             VMEM((2, 2, places, 128), F32),
             table,
             table,
         ),
-        in_specs=[in_smem()] * 2 + [in_vmem()] * 6,
-        out_specs=(in_vmem(),) * 5,
+        in_specs=[in_smem()] * 3 + [in_vmem()] * 7,
+        out_specs=(in_vmem(),) * 6,
         scratch_shapes=[VMEM(library.shape, F32)],
+        input_output_aliases={3: 0},
         compiler_params=params(),
         cost_estimate=pl.CostEstimate(flops=10**7, bytes_accessed=10**6, transcendentals=10**5),
         name="inner_step",
-    )(choice, camera, held(field0), library, *map(held, rows))
+    )(*map(in_scalars, (counts, choice, camera)), *map(held, (field0, library, *rows)))
 
 
 def outer_kernel(devices, counts, camera, *arrays):
@@ -497,7 +559,7 @@
         compiler_params=params(),
         cost_estimate=pl.CostEstimate(flops=2 * 10**7, bytes_accessed=10**6, transcendentals=10**5),
         name="outer_step",
-    )(counts, camera, *map(held, arrays))[:3]
+    )(*map(in_scalars, (counts, camera)), *map(held, arrays))[:3]
 
 
 def last_kernel(functions, camera, pieces):
@@ -508,7 +570,7 @@
         out_specs=in_vmem(),
         compiler_params=params(),
         name="composite",
-    )(camera, held(pieces))
+    )(in_scalars(camera), held(pieces))
 
 
 def on_device(
@@ -520,48 +582,52 @@
     camera_direction,
 ):
     devices = lax.axis_size("depth")
-    field0, own_low, own_high, last_layer, first_layer, upward, downward = first_kernel(
-        active_sheet_number, thermal_values, reactant_fraction
-    )
-    rows_below = shifted(own_high, "lat", 1)
-    rows_above = shifted(own_low, "lat", -1)
-    below_2 = shifted(last_layer, "depth", 2)
-    above_2 = shifted(first_layer, "depth", -2)
-    upward, downward = rim_kernel(
-        active_sheet_number, upward, downward, rows_below, rows_above, below_2, above_2
-    )
-    from_below = shifted(upward, "depth", 1)
-    from_above = shifted(downward, "depth", -1)
-    field1, edge0, edge1, low_table, rise_table = inner_kernel(
-        devices,
+    counts, choice, camera, library, field0, own_rows, *messages = first_kernel(
+        active_sheet_number,
         colour_lookup_choice,
         camera_direction,
+        thermal_values,
+        reactant_fraction,
+        colour_lookup_library,
+    )
+    rows_gap = swapped(messages[1], "lat", 1)
+    rows_pair = swapped(messages[0], "lat", 0)
+    rim_gap = swapped(messages[3], "depth", 1)
+    rim_pair = swapped(messages[2], "depth", 0)
+    next_pair, next_gap = rim_kernel(counts, rows_pair, rows_gap, rim_pair, rim_gap)
+    next_gap = swapped(next_gap, "depth", 1)
+    next_pair = swapped(next_pair, "depth", 0)
+    field0, field1, edge0, edge1, low_table, rise_table = inner_kernel(
+        devices,
+        counts,
+        choice,
+        camera,
         field0,
-        colour_lookup_library,
-        own_low,
-        own_high,
-        rows_below,
-        rows_above,
+        library,
+        own_rows,
+        rows_pair,
+        rows_gap,
+        rim_pair,
+        rim_gap,
     )
     theta_next, fuel_next, pieces = outer_kernel(
         devices,
-        active_sheet_number,
-        camera_direction,
+        counts,
+        camera,
         field0,
         field1,
         edge0,
         edge1,
         low_table,
         rise_table,
-        own_low,
-        own_high,
-        from_below,
-        from_above,
-        below_2,
-        above_2,
+        own_rows,
+        rim_pair,
+        rim_gap,
+        next_pair,
+        next_gap,
     )
     pieces = lax.all_to_all(pieces, "depth", 0, 0, tiled=True)
-    image = last_kernel(colour_lookup_choice.shape[0], camera_direction, pieces)
+    image = last_kernel(colour_lookup_choice.shape[0], camera, pieces)
     return (theta_next, fuel_next, image)
 
 

time: 60.4 us -> 56.6 us (0.937)
  the two profiles are of different devices: /device:TPU:385 before, /device:TPU:128 now
where the time goes in v3:
time: 56.6 us; the launch traced here: 56.3 us
  starting transfers between devices  24.4 us (43%)
  blocking collectives  20.4 us (36%)
  Pallas kernels  6.95 us (12%)
  waiting for transfers between devices  3.2 us (6%)
  between operations  1.36 us (2%)
    ppermute x6, starting transfers between devices, swapped(): return lax.ppermute(array, axis, pairs)  24.4 us
    all_to_all x1, blocking collectives, on_device(): pieces = lax.all_to_all(pieces, 'depth', 0, 0, tiled=True)  20.4 us
    pallas_call x1, Pallas kernels, outer_kernel(): pl.pallas_call(functools.partial(outer_step, places, functions), out_shap...  3.81 us
    ppermute x6, waiting for transfers between devices, swapped(): return lax.ppermute(array, axis, pairs)  3.2 us
    pallas_call x1, Pallas kernels, first_kernel(): pl.pallas_call(pack_rows, out_shape=tuple((SMEM(x.shape, jnp.int32) for x...  1.35 us
  transfers between devices with their start and end apart: 6, of which 2 were waited for; matrix products, arithmetic and copies ran while one was open for 0% of the time, Pallas kernels for 2%

profile of v3, /device:TPU:128, one launch (start us, length us, event | category | flops | bytes accessed | tf_op | source)
XLA Modules:
  0.0 56.3 jit_solution(10325999650287878096)
XLA Ops:
  1.3 1.4 %pack_rows.1 = (s32[1]{0:T(128)S(4)}, s32[4]{0:T(128)S(4)}, s32[4]{0:T(128)S(4)}, bf16[8,4,128]{2,1,0:T(4,128)(2,1)S(1)}, f32[2,68,8,128]{3,2,1,0:T(8,128)S(1)},...) custom-call(s32[1]{0:T(128)S(6)} %copy.19.counts_in, ...), custom_call_target="tpu_custom_call" | custom-call | tf_op jit(solution)/shard_map/pack_rows/pallas_call | solution.py:493
  2.6 1.9 %collective-permute-start = (f32[4,64,128]{2,1,0:T(8,128)S(1)}, f32[4,64,128]{2,1,0:T(8,128)S(1)}, u32[]{:S(2)}, u32[]{:S(2)}) collective-permute-start(f32[4,64,128]{2,1,0:T(8,128)S(1)} %get-tuple-element.30), channel_id=1, source_target_pairs={{0,1},{1,0},{2,3},{3,2},{4,5},{5,4},{6,7},{7,6},{8,9},{9,8},{10,11... | collective-permute-start | bytes 393224 | tf_op jit(solution)/shard_map/ppermute | solution.py:466
  4.6 13.4 %collective-permute-start.1 = (f32[4,64,128]{2,1,0:T(8,128)S(1)}, f32[4,64,128]{2,1,0:T(8,128)S(1)}, u32[]{:S(2)}, u32[]{:S(2)}) collective-permute-start(f32[4,64,128]{2,1,0:T(8,128)S(1)} %get-tuple-element.31), channel_id=1, source_target_pairs={{1,2},{2,1},{3,4},{4,3},{5,6},{6,5},{7,8},{8,7},{9,10},{10,9},{11,... | collective-permute-start | bytes 393224 | tf_op jit(solution)/shard_map/ppermute | solution.py:466
  18.0 1.9 %collective-permute-start.2 = (f32[2,3,8,128]{3,2,1,0:T(8,128)S(1)}, f32[2,3,8,128]{3,2,1,0:T(8,128)S(1)}, u32[]{:S(2)}, u32[]{:S(2)}) collective-permute-start(f32[2,3,8,128]{3,2,1,0:T(8,128)S(1)} %get-tuple-element.32), channel_id=1, source_target_pairs={{0,16},{16,0},{32,48},{48,32},{64,80},{80,64},{96,112},{112,96},{1... | collective-permute-start | bytes 73736 | tf_op jit(solution)/shard_map/ppermute | solution.py:466
  19.9 0.7 %collective-permute-start.3 = (f32[2,3,8,128]{3,2,1,0:T(8,128)S(1)}, f32[2,3,8,128]{3,2,1,0:T(8,128)S(1)}, u32[]{:S(2)}, u32[]{:S(2)}) collective-permute-start(f32[2,3,8,128]{3,2,1,0:T(8,128)S(1)} %get-tuple-element.33), channel_id=1, source_target_pairs={{16,32},{32,16},{48,64},{64,48},{80,96},{96,80},{112,128},{128,112... | collective-permute-start | bytes 73736 | tf_op jit(solution)/shard_map/ppermute | solution.py:466
  20.6 3.1 %collective-permute-done.2.rim_pair = f32[2,3,8,128]{3,2,1,0:T(8,128)S(1)} collective-permute-done((f32[2,3,8,128]{3,2,1,0:T(8,128)S(1)}, f32[2,3,8,128]{3,2,1,0:T(8,128)S(1)}, u32[]{:S(2)}, u32[]{:S(2)}) %collective-permute-start.2) | collective-permute-done | bytes 24608 | tf_op jit(solution)/shard_map/ppermute | solution.py:466
  23.7 0.0 collective-permute-done.3.rim_gap
  23.7 0.0 collective-permute-done.rows_pair
  23.7 0.0 collective-permute-done.1.rows_gap
  23.7 5.8 %collective-permute-start.4 = (f32[2,2,8,128]{3,2,1,0:T(8,128)S(1)}, f32[2,2,8,128]{3,2,1,0:T(8,128)S(1)}, u32[]{:S(2)}, u32[]{:S(2)}) collective-permute-start(f32[2,2,8,128]{3,2,1,0:T(8,128)S(1)} %get-tuple-element.40), channel_id=1, source_target_pairs={{0,16},{16,0},{32,48},{48,32},{64,80},{80,64},{96,112},{112,96},{1... | collective-permute-start | bytes 49160 | tf_op jit(solution)/shard_map/ppermute | solution.py:466
  29.6 0.7 %collective-permute-start.5 = (f32[2,2,8,128]{3,2,1,0:T(8,128)S(1)}, f32[2,2,8,128]{3,2,1,0:T(8,128)S(1)}, u32[]{:S(2)}, u32[]{:S(2)}) collective-permute-start(f32[2,2,8,128]{3,2,1,0:T(8,128)S(1)} %get-tuple-element.41), channel_id=1, source_target_pairs={{16,32},{32,16},{48,64},{64,48},{80,96},{96,80},{112,128},{128,112... | collective-permute-start | bytes 49160 | tf_op jit(solution)/shard_map/ppermute | solution.py:466
  30.3 1.0 %inner_step.1 = (f32[2,68,8,128]{3,2,1,0:T(8,128)S(1)}, f32[2,66,8,128]{3,2,1,0:T(8,128)S(1)}, f32[2,4,80,128]{3,2,1,0:T(8,128)S(1)}, f32[2,2,64,128]{3,2,1,0:T(...) custom-call(s32[1]{0:T(128)S(4)} %get-tuple-element.24.counts, ...), custom_call_target="tpu_custom_call", output_to_operand_aliasing={{0}: (3, {})} | custom-call | flops 10000000 | bytes 1000000 | tf_op jit(solution)/shard_map/inner_step/pallas_call | solution.py:523
  31.2 0.1 collective-permute-done.4.next_pair
  31.3 0.0 collective-permute-done.5.next_gap
  31.3 3.8 %outer_step.1 = (f32[64,8,128]{2,1,0:T(8,128)}, f32[64,8,128]{2,1,0:T(8,128)}, f32[128,128]{1,0:T(8,128)S(1)}, f32[2,68,8,128]{3,2,1,0:T(8,128)S(1)}, f32[2,66,8...) custom-call(s32[1]{0:T(128)S(4)} %get-tuple-element.24.counts, ...), custom_call_target="tpu_custom_call", output_to_operand_aliasing={{3}: (2, {}), {4}: (3, {}), {5}: (4, {}), {6}: (5, {})} | custom-call | flops 20000000 | bytes 1000000 | tf_op jit(solution)/shard_map/outer_step/pallas_call | solution.py:548
  35.1 20.4 %all_to_all.11 = f32[64,2,128]{2,1,0:T(2,128)S(1)} all-to-all(f32[64,2,128]{2,1,0:T(2,128)S(1)} %bitcast.3), channel_id=1, replica_groups=mesh['depth'=64,'lat'=16] {'depth'}, dimensions={0} | all-to-all | bytes 131072 | tf_op jit(solution)/shard_map/all_to_all | solution.py:629
  55.5 0.8 %composite.1 = f32[4,4,1,16]{3,2,1,0:T(1,128)} custom-call(s32[4]{0:T(128)S(4)} %get-tuple-element.25.camera, f32[128,128]{1,0:T(8,128)S(1)} %bitcast.2), custom_call_target="tpu_custom_call" | custom-call | tf_op jit(solution)/shard_map/composite/pallas_call | solution.py:566
  (1 shorter events, 0.0 us)
Async XLA Ops:
  2.6 21.1 %collective-permute-start = (f32[4,64,128]{2,1,0:T(8,128)S(1)}, f32[4,64,128]{2,1,0:T(8,128)S(1)}, u32[]{:S(2)}, u32[]{:S(2)}) collective-permute-start(f32[4,64,128]{2,1,0:T(8,128)S(1)} %get-tuple-element.30), channel_id=1, source_target_pairs={{0,1},{1,0},{2,3},{3,2},{4,5},{5,4},{6,7},{7,6},{8,9},{9,8},{10,11... | collective-permute-start | bytes 393224 | tf_op jit(solution)/shard_map/ppermute | solution.py:466
  4.6 19.1 %collective-permute-start.1 = (f32[4,64,128]{2,1,0:T(8,128)S(1)}, f32[4,64,128]{2,1,0:T(8,128)S(1)}, u32[]{:S(2)}, u32[]{:S(2)}) collective-permute-start(f32[4,64,128]{2,1,0:T(8,128)S(1)} %get-tuple-element.31), channel_id=1, source_target_pairs={{1,2},{2,1},{3,4},{4,3},{5,6},{6,5},{7,8},{8,7},{9,10},{10,9},{11,... | collective-permute-start | bytes 393224 | tf_op jit(solution)/shard_map/ppermute | solution.py:466
  18.0 5.7 %collective-permute-start.2 = (f32[2,3,8,128]{3,2,1,0:T(8,128)S(1)}, f32[2,3,8,128]{3,2,1,0:T(8,128)S(1)}, u32[]{:S(2)}, u32[]{:S(2)}) collective-permute-start(f32[2,3,8,128]{3,2,1,0:T(8,128)S(1)} %get-tuple-element.32), channel_id=1, source_target_pairs={{0,16},{16,0},{32,48},{48,32},{64,80},{80,64},{96,112},{112,96},{1... | collective-permute-start | bytes 73736 | tf_op jit(solution)/shard_map/ppermute | solution.py:466
  19.9 3.8 %collective-permute-start.3 = (f32[2,3,8,128]{3,2,1,0:T(8,128)S(1)}, f32[2,3,8,128]{3,2,1,0:T(8,128)S(1)}, u32[]{:S(2)}, u32[]{:S(2)}) collective-permute-start(f32[2,3,8,128]{3,2,1,0:T(8,128)S(1)} %get-tuple-element.33), channel_id=1, source_target_pairs={{16,32},{32,16},{48,64},{64,48},{80,96},{96,80},{112,128},{128,112... | collective-permute-start | bytes 73736 | tf_op jit(solution)/shard_map/ppermute | solution.py:466
  23.7 7.6 %collective-permute-start.4 = (f32[2,2,8,128]{3,2,1,0:T(8,128)S(1)}, f32[2,2,8,128]{3,2,1,0:T(8,128)S(1)}, u32[]{:S(2)}, u32[]{:S(2)}) collective-permute-start(f32[2,2,8,128]{3,2,1,0:T(8,128)S(1)} %get-tuple-element.40), channel_id=1, source_target_pairs={{0,16},{16,0},{32,48},{48,32},{64,80},{80,64},{96,112},{112,96},{1... | collective-permute-start | bytes 49160 | tf_op jit(solution)/shard_map/ppermute | solution.py:466
  29.6 1.7 %collective-permute-start.5 = (f32[2,2,8,128]{3,2,1,0:T(8,128)S(1)}, f32[2,2,8,128]{3,2,1,0:T(8,128)S(1)}, u32[]{:S(2)}, u32[]{:S(2)}) collective-permute-start(f32[2,2,8,128]{3,2,1,0:T(8,128)S(1)} %get-tuple-element.41), channel_id=1, source_target_pairs={{16,32},{32,16},{48,64},{64,48},{80,96},{96,80},{112,128},{128,112... | collective-permute-start | bytes 49160 | tf_op jit(solution)/shard_map/ppermute | solution.py:466

commit v4 on v3

--- a/solution.py
+++ b/solution.py
@@ -29,7 +29,9 @@
 
 
 UNROLL_1 = 16
-UNROLL_2 = 16
+UNROLL_EARLY = 16
+UNROLL_MIDDLE = 22
+EARLY = 16
 
 
 def is_even(axis):
@@ -99,7 +101,7 @@
         copy.wait()
 
 
-def pack_rims(counts, rows_pair, rows_gap, rim_pair, rim_gap, next_pair, next_gap):
+def pack_rims(counts, rows_pair, rows_gap, rim_pair, rim_gap, order, next_pair, next_gap):
     last = counts[0] - 1
     lat_even, depth_even = is_even("lat"), is_even("depth")
     for number in range(2):
@@ -215,33 +217,77 @@
     return [jnp.where(outside, 0.0, x) for x in stepped(heat, burn, around)]
 
 
-def inner_step(
+def look_up(low_table, rise_table, value):
+    bins = low_table.shape[2]
+    position = jnp.clip(value, 0.0, 1.0) * (bins - 1)
+    lower = jnp.minimum(position.astype(jnp.int32), bins - 2)
+    fraction = position - lower.astype(F32)
+
+    def at(entry):
+        low = jnp.take_along_axis(low_table[entry], lower, axis=1)
+        rise = jnp.take_along_axis(rise_table[entry], lower, axis=1)
+        return low + fraction * rise
+
+    return at
+
+
+def add_layer(sums, number, at, alive):
+    for f in range(2 * number, 2 * number + 2):
+        gone, red, green, blue = sums[4 * f : 4 * f + 4]
+        depth = jnp.where(alive, at(4 * f + 3), 0.0)
+        gain = depth * (1.0 + depth * (0.5 + depth * (1.0 / 6.0)))
+        gain = gain + gone * gain
+        sums[4 * f] = gone + gain
+        sums[4 * f + 1] = red + gain * at(4 * f)
+        sums[4 * f + 2] = green + gain * at(4 * f + 1)
+        sums[4 * f + 3] = blue + gain * at(4 * f + 2)
+
+
+def inner_layers(
+    first, count, unroll, depth_count, field1, edge1, tables, results, sums, after=None
+):
+    def body(block, carry):
+        start = first + block * unroll
+
+        def edge_rows(j):
+            return rows_beside(edge1, (0, 1), start + j)
+
+        carry = list(carry)
+        for j, new in enumerate(block_step(field1, start + 1, unroll, edge_rows)):
+            for number in range(2):
+                value = jnp.where(start + j < depth_count, new[number], 0.0)
+                results[number][start + j] = value
+                add_layer(carry, number, look_up(*tables, value), start + j < depth_count - 2)
+        if after is not None:
+            after(start, unroll)
+        return tuple(carry)
+
+    return lax.fori_loop(0, count // unroll, body, tuple(sums))
+
+
+def early_step(
     places,
     functions,
     all_layers,
     counts,
     choice,
     camera,
-    field0_in,
+    field0,
     library,
     own_rows,
     rows_pair,
     rows_gap,
-    rim_pair,
-    rim_gap,
-    field0,
     field1,
     edge0,
     edge1,
     low_table,
     rise_table,
+    theta_next,
+    fuel_next,
+    sums,
     tables,
 ):
-    lat_even, depth_even = is_even("lat"), is_even("depth")
-    for number in range(2):
-        above, below = rim_pair[number, 0], rim_gap[number, 0]
-        field0[number, 1] = select(depth_even, below, above)
-        field0[number, counts[0] + 2] = select(depth_even, above, below)
+    lat_even = is_even("lat")
     bins = library.shape[2]
     tables[...] = library[...].astype(F32)
     per_cell = 3.0 / all_layers
@@ -268,24 +314,87 @@
             for number in range(2):
                 edge1[number, side, 8 * block : 8 * block + 8] = fresh[number]
 
-    unroll = UNROLL_1
-
     def first_step(block, carry):
-        start = block * unroll
+        start = block * UNROLL_1
 
         def edge_rows(j):
             return rows_beside(edge0, (1, 2), LEAD + start + j)
 
-        for j, new in enumerate(block_step(field0, start + 2, unroll, edge_rows)):
+        for j, new in enumerate(block_step(field0, start + 2, UNROLL_1, edge_rows)):
             for number in range(2):
                 field1[number, start + 1 + j] = new[number]
         return carry
 
-    lax.fori_loop(0, places // unroll, first_step, 0)
-
-
-def outer_step(
+    lax.fori_loop(0, places // UNROLL_1, first_step, 0)
+    zero = jnp.zeros((8, 128), F32)
+    for out in (theta_next, fuel_next):
+        for place in (0, 1, places - 2, places - 1):
+            out[place] = zero
+    found = inner_layers(
+        2,
+        EARLY,
+        UNROLL_EARLY,
+        counts[0],
+        field1,
+        edge1,
+        (low_table, rise_table),
+        (theta_next, fuel_next),
+        [zero] * (4 * functions),
+    )
+    for entry, value in enumerate(found):
+        sums[entry] = value
+
+
+def middle_step(
     places,
+    counts,
+    field1,
+    edge1,
+    low_table,
+    rise_table,
+    order,
+    theta_in,
+    fuel_in,
+    sums_in,
+    theta_out,
+    fuel_out,
+    theta_next,
+    fuel_next,
+    sums,
+    copies,
+):
+    def leave(number, first, count):
+        return pltpu.make_async_copy(
+            (theta_next, fuel_next)[number].at[pl.ds(first, count)],
+            (theta_out, fuel_out)[number].at[pl.ds(first, count)],
+            copies.at[number],
+        )
+
+    def start_leaving(first, count):
+        for number in range(2):
+            leave(number, first, count).start()
+
+    start_leaving(0, 2 + EARLY)
+    start_leaving(places - 2, 2)
+    found = inner_layers(
+        2 + EARLY,
+        places - 4 - EARLY,
+        UNROLL_MIDDLE,
+        counts[0],
+        field1,
+        edge1,
+        (low_table, rise_table),
+        (theta_next, fuel_next),
+        [sums_in[entry] for entry in range(sums_in.shape[0])],
+        start_leaving,
+    )
+    for entry, value in enumerate(found):
+        sums[entry] = value
+    for number in range(2):
+        leave(number, 0, places).wait()
+
+
+def late_step(
     functions,
     counts,
     camera,
@@ -295,23 +404,20 @@
     edge1_in,
     low_table,
     rise_table,
+    sums,
     own_rows,
     rim_pair,
     rim_gap,
     next_pair,
     next_gap,
-    theta_next,
-    fuel_next,
     image,
+    ends,
     field0,
     field1,
     edge0,
     edge1,
-    result,
-    copies,
 ):
     depth_count = counts[0]
-    bins = low_table.shape[2]
     depth_even = is_even("depth")
 
     def from_below(pair, gap, *at):
@@ -328,6 +434,8 @@
             from_below(next_pair, next_gap, number, 0),
             from_below(rim_pair, rim_gap, number, 1),
         )
+        field0[number, 1] = from_below(rim_pair, rim_gap, number, 0)
+        field0[number, depth_count + 2] = from_above(rim_pair, rim_gap, number, 0)
         field0[number, depth_count + 3] = jnp.where(
             above_size == 1.0,
             from_above(next_pair, next_gap, number, 0),
@@ -343,64 +451,51 @@
             fresh = step_edges(edge0, own_rows, side, LEAD + place, place, 1)
             for number in range(2):
                 edge1[number, side, pl.ds(place, 1)] = fresh[number][0:1]
-    for place, size in ((-1, below_size), (depth_count, above_size)):
+    for place, size in (
+        (-1, below_size),
+        (0, None),
+        (depth_count - 1, None),
+        (depth_count, above_size),
+    ):
 
         def edge_rows(j, place=place):
             return rows_beside(edge0, (1, 2), LEAD + place)
 
         (fresh,) = block_step(field0, place + 2, 1, edge_rows)
         for number in range(2):
-            field1[number, place + 1] = jnp.where(size > 0.0, fresh[number], 0.0)
-
-    unroll = UNROLL_2
-
-    def leave(number, first, count):
-        return pltpu.make_async_copy(
-            result.at[number, pl.ds(first, count)],
-            (theta_next, fuel_next)[number].at[pl.ds(first, count)],
-            copies.at[number],
-        )
-
-    def second_step(block, carry):
-        start = block * unroll
-
-        def edge_rows(j):
+            value = fresh[number]
+            field1[number, place + 1] = (
+                value if size is None else jnp.where(size > 0.0, value, 0.0)
+            )
+
+    zero = jnp.zeros((8, 128), F32)
+    segments = []
+    for slot, start in ((0, 0), (2, jnp.maximum(depth_count - 2, 2))):
+
+        def edge_rows(j, start=start):
             return rows_beside(edge1, (0, 1), start + j)
 
-        carry = list(carry)
-        for j, new in enumerate(block_step(field1, start + 1, unroll, edge_rows)):
-            alive = start + j < depth_count
+        segment = [zero] * (4 * functions)
+        for j, new in enumerate(block_step(field1, start + 1, 2, edge_rows)):
+            place = start + j
+            alive = place < depth_count
             for number in range(2):
                 value = jnp.where(alive, new[number], 0.0)
-                result[number, start + j] = value
-                position = jnp.clip(value, 0.0, 1.0) * (bins - 1)
-                lower = jnp.minimum(position.astype(jnp.int32), bins - 2)
-                fraction = position - lower.astype(F32)
-
-                def look_up(entry):
-                    low = jnp.take_along_axis(low_table[entry], lower, axis=1)
-                    rise = jnp.take_along_axis(rise_table[entry], lower, axis=1)
-                    return low + fraction * rise
-
-                for f in range(2 * number, 2 * number + 2):
-                    gone, red, green, blue = carry[4 * f : 4 * f + 4]
-                    depth = jnp.where(alive, look_up(4 * f + 3), 0.0)
-                    gain = depth * (1.0 + depth * (0.5 + depth * (1.0 / 6.0)))
-                    gain = gain + gone * gain
-                    carry[4 * f] = gone + gain
-                    carry[4 * f + 1] = red + gain * look_up(4 * f)
-                    carry[4 * f + 2] = green + gain * look_up(4 * f + 1)
-                    carry[4 * f + 3] = blue + gain * look_up(4 * f + 2)
-        for number in range(2):
-            leave(number, start, unroll).start()
-        return tuple(carry)
-
-    zero = jnp.zeros((8, 128), F32)
-    sums = lax.fori_loop(0, places // unroll, second_step, (zero,) * (4 * functions))
-
+                ends[number, slot + j] = value
+                at = look_up(low_table, rise_table, value)
+                add_layer(segment, number, at, alive)
+        segments.append(segment)
+
+    head, tail = segments
     channels = []
     for f in range(functions):
-        gone, red, green, blue = sums[4 * f : 4 * f + 4]
+        through_head = 1.0 + head[4 * f]
+        through_body = 1.0 + sums[4 * f]
+        gone, red, green, blue = [
+            head[4 * f + c]
+            + through_head * (sums[4 * f + c] + through_body * tail[4 * f + c])
+            for c in range(4)
+        ]
         scale = jnp.where(camera[f] == 0, -1.0, 1.0 / (1.0 + gone))
         channels += [red * scale, green * scale, blue * scale, gone * scale]
 
@@ -419,8 +514,20 @@
             regs = fresh
         for g in range(8):
             image[pl.ds(2 * g + half, 8, stride=16), :] = regs[g]
-    for number in range(2):
-        leave(number, 0, places).wait()
+
+
+def place_ends(counts, ends, theta_in, fuel_in, theta_next, fuel_next, copies):
+    leave = [
+        pltpu.make_async_copy(
+            ends.at[number, pl.ds(slot, 2)], out.at[pl.ds(place, 2)], copies.at[number, slot // 2]
+        )
+        for number, out in enumerate((theta_next, fuel_next))
+        for slot, place in ((0, 0), (2, jnp.maximum(counts[0] - 2, 2)))
+    ]
+    for copy in leave:
+        copy.start()
+    for copy in leave:
+        copy.wait()
 
 
 def composite(camera, pieces, image):
@@ -508,58 +615,90 @@
     return pl.pallas_call(
         pack_rims,
         out_shape=(rim, rim),
-        in_specs=[in_smem()] + [in_vmem()] * 4,
+        in_specs=[in_smem()] + [in_vmem()] * len(received),
         out_specs=(in_vmem(),) * 2,
         compiler_params=params(),
         name="pack_rims",
     )(in_scalars(counts), *map(held, received))
 
 
-def inner_kernel(devices, counts, choice, camera, field0, library, *rows):
+def cost(flops):
+    return pl.CostEstimate(flops=flops, bytes_accessed=10**6, transcendentals=10**5)
+
+
+def early_kernel(devices, counts, choice, camera, field0, library, *rows):
     places = field0.shape[1] - 4
     functions = choice.shape[0]
     bins = library.shape[2]
     table = VMEM((4 * functions, 8, bins), F32)
+    field = VMEM((places, 8, 128), F32)
     return pl.pallas_call(
-        functools.partial(inner_step, places, functions, float(MEAN_DEPTH * devices)),
+        functools.partial(early_step, places, functions, float(MEAN_DEPTH * devices)),
         out_shape=(
-            VMEM(field0.shape, F32),
             VMEM((2, places + 2, 8, 128), F32),
             VMEM((2, 4, places + 16, 128), F32),
             VMEM((2, 2, places, 128), F32),
             table,
             table,
+            field,
+            field,
+            VMEM((4 * functions, 8, 128), F32),
         ),
-        in_specs=[in_smem()] * 3 + [in_vmem()] * 7,
+        in_specs=[in_smem()] * 3 + [in_vmem()] * 5,
+        out_specs=(in_vmem(),) * 8,
+        scratch_shapes=[VMEM(library.shape, F32)],
+        compiler_params=params(),
+        cost_estimate=cost(10**7),
+        name="early_step",
+    )(*map(in_scalars, (counts, choice, camera)), *map(held, (field0, library, *rows)))
+
+
+def middle_kernel(counts, *arrays):
+    theta_next, fuel_next, sums = arrays[-3:]
+    field = jax.ShapeDtypeStruct(theta_next.shape, F32)
+    return pl.pallas_call(
+        functools.partial(middle_step, theta_next.shape[0]),
+        out_shape=(field, field) + tuple(VMEM(x.shape, F32) for x in (theta_next, fuel_next, sums)),
+        in_specs=[in_smem()] + [in_vmem()] * len(arrays),
+        out_specs=(anywhere(),) * 2 + (in_vmem(),) * 3,
+        scratch_shapes=[pltpu.SemaphoreType.DMA((2,))],
+        input_output_aliases={len(arrays) - 2 + i: 2 + i for i in range(2)},
+        compiler_params=params(),
+        cost_estimate=cost(10**7),
+        name="middle_step",
+    )(in_scalars(counts), *map(held, arrays))
+
+
+def late_kernel(devices, counts, camera, *arrays):
+    functions = camera.shape[0]
+    kept = arrays[:4]
+    image, ends, *_ = pl.pallas_call(
+        functools.partial(late_step, functions),
+        out_shape=(VMEM((2 * devices, 128), F32), VMEM((2, 4, 8, 128), F32))
+        + tuple(VMEM(x.shape, F32) for x in kept),
+        in_specs=[in_smem()] * 2 + [in_vmem()] * len(arrays),
         out_specs=(in_vmem(),) * 6,
-        scratch_shapes=[VMEM(library.shape, F32)],
-        input_output_aliases={3: 0},
+        input_output_aliases={2 + i: 2 + i for i in range(4)},
         compiler_params=params(),
-        cost_estimate=pl.CostEstimate(flops=10**7, bytes_accessed=10**6, transcendentals=10**5),
-        name="inner_step",
-    )(*map(in_scalars, (counts, choice, camera)), *map(held, (field0, library, *rows)))
-
-
-def outer_kernel(devices, counts, camera, *arrays):
-    field0, field1, edge0, edge1 = arrays[:4]
-    places = field0.shape[1] - 4
-    functions = camera.shape[0]
-    field = jax.ShapeDtypeStruct((places, 8, 128), F32)
+        cost_estimate=cost(10**6),
+        name="late_step",
+    )(*map(in_scalars, (counts, camera)), *map(held, arrays))
+    return image, ends
+
+
+def end_kernel(counts, ends, *fields):
+    field = jax.ShapeDtypeStruct(fields[0].shape, F32)
     return pl.pallas_call(
-        functools.partial(outer_step, places, functions),
-        out_shape=(field, field, VMEM((2 * devices, 128), F32))
-        + tuple(VMEM(x.shape, F32) for x in (field0, field1, edge0, edge1)),
-        in_specs=[in_smem()] * 2 + [in_vmem()] * len(arrays),
-        out_specs=(anywhere(),) * 2 + (in_vmem(),) * 5,
-        scratch_shapes=[
-            VMEM((2, places, 8, 128), F32),
-            pltpu.SemaphoreType.DMA((2,)),
-        ],
-        input_output_aliases={2 + i: 3 + i for i in range(4)},
+        place_ends,
+        out_shape=(field, field),
+        in_specs=[in_smem(), in_vmem()] + [anywhere()] * 2,
+        out_specs=(anywhere(),) * 2,
+        scratch_shapes=[pltpu.SemaphoreType.DMA((2, 2))],
+        input_output_aliases={2: 0, 3: 1},
         compiler_params=params(),
-        cost_estimate=pl.CostEstimate(flops=2 * 10**7, bytes_accessed=10**6, transcendentals=10**5),
-        name="outer_step",
-    )(*map(in_scalars, (counts, camera)), *map(held, arrays))[:3]
+        cost_estimate=cost(10**6),
+        name="place_ends",
+    )(in_scalars(counts), held(ends), *map(in_hbm, fields))
 
 
 def last_kernel(functions, camera, pieces):
@@ -594,23 +733,17 @@
     rows_pair = swapped(messages[0], "lat", 0)
     rim_gap = swapped(messages[3], "depth", 1)
     rim_pair = swapped(messages[2], "depth", 0)
-    next_pair, next_gap = rim_kernel(counts, rows_pair, rows_gap, rim_pair, rim_gap)
+    field1, edge0, edge1, low_table, rise_table, theta_next, fuel_next, sums = early_kernel(
+        devices, counts, choice, camera, field0, library, own_rows, rows_pair, rows_gap
+    )
+    next_pair, next_gap = rim_kernel(counts, rows_pair, rows_gap, rim_pair, rim_gap, sums)
+    order = next_pair
     next_gap = swapped(next_gap, "depth", 1)
     next_pair = swapped(next_pair, "depth", 0)
-    field0, field1, edge0, edge1, low_table, rise_table = inner_kernel(
-        devices,
-        counts,
-        choice,
-        camera,
-        field0,
-        library,
-        own_rows,
-        rows_pair,
-        rows_gap,
-        rim_pair,
-        rim_gap,
-    )
-    theta_next, fuel_next, pieces = outer_kernel(
+    theta_next, fuel_next, _, _, sums = middle_kernel(
+        counts, field1, edge1, low_table, rise_table, order, theta_next, fuel_next, sums
+    )
+    pieces, ends = late_kernel(
         devices,
         counts,
         camera,
@@ -620,6 +753,7 @@
         edge1,
         low_table,
         rise_table,
+        sums,
         own_rows,
         rim_pair,
         rim_gap,
@@ -627,7 +761,8 @@
         next_gap,
     )
     pieces = lax.all_to_all(pieces, "depth", 0, 0, tiled=True)
-    image = last_kernel(colour_lookup_choice.shape[0], camera, pieces)
+    theta_next, fuel_next = end_kernel(counts, ends, theta_next, fuel_next)
+    image = last_kernel(choice.shape[0], camera, pieces)
     return (theta_next, fuel_next, image)
 
 

time: 56.6 us -> 54.4 us (0.961)
  the two profiles are of different devices: /device:TPU:128 before, /device:TPU:385 now
where the time goes in v4:
time: 54.4 us; the launch traced here: 54.1 us
  starting transfers between devices  33.4 us (61%)
  waiting for transfers between devices  10.4 us (19%)
  Pallas kernels  8.81 us (16%)
  between operations  1.42 us (3%)
    ppermute x6, starting transfers between devices, swapped(): return lax.ppermute(array, axis, pairs)  20.7 us
    all_to_all x1, starting transfers between devices, on_device(): pieces = lax.all_to_all(pieces, 'depth', 0, 0, tiled=True)  12.8 us
    all_to_all x1, waiting for transfers between devices, on_device(): pieces = lax.all_to_all(pieces, 'depth', 0, 0, tiled=True)  10.4 us
    pallas_call x1, Pallas kernels, middle_kernel(): pl.pallas_call(functools.partial(middle_step, theta_next.shape[0]), out_s...  2.84 us
    pallas_call x1, Pallas kernels, early_kernel(): pl.pallas_call(functools.partial(early_step, places, functions, float(MEA...  1.8 us
    pallas_call x1, Pallas kernels, first_kernel(): pl.pallas_call(pack_rows, out_shape=tuple((SMEM(x.shape, jnp.int32) for x...  1.35 us
    pallas_call x1, Pallas kernels, late_kernel(): pl.pallas_call(functools.partial(late_step, functions), out_shape=(VMEM((...  1.34 us
  transfers between devices with their start and end apart: 7, of which 1 were waited for; matrix products, arithmetic and copies ran while one was open for 0% of the time, Pallas kernels for 10%

profile of v4, /device:TPU:385, one launch (start us, length us, event | category | flops | bytes accessed | tf_op | source)
XLA Modules:
  0.0 54.1 jit_solution(5450699820561150975)
XLA Ops:
  1.3 1.3 %pack_rows.1 = (s32[1]{0:T(128)S(4)}, s32[4]{0:T(128)S(4)}, s32[4]{0:T(128)S(4)}, bf16[8,4,128]{2,1,0:T(4,128)(2,1)S(1)}, f32[2,68,8,128]{3,2,1,0:T(8,128)S(1)},...) custom-call(s32[1]{0:T(128)S(6)} %copy.25.counts_in, ...), custom_call_target="tpu_custom_call" | custom-call | tf_op jit(solution)/shard_map/pack_rows/pallas_call | solution.py:600
  2.6 2.6 %collective-permute-start = (f32[4,64,128]{2,1,0:T(8,128)S(1)}, f32[4,64,128]{2,1,0:T(8,128)S(1)}, u32[]{:S(2)}, u32[]{:S(2)}) collective-permute-start(f32[4,64,128]{2,1,0:T(8,128)S(1)} %get-tuple-element.36), channel_id=1, source_target_pairs={{0,1},{1,0},{2,3},{3,2},{4,5},{5,4},{6,7},{7,6},{8,9},{9,8},{10,11... | collective-permute-start | bytes 393224 | tf_op jit(solution)/shard_map/ppermute | solution.py:573
  5.2 6.0 %collective-permute-start.1 = (f32[4,64,128]{2,1,0:T(8,128)S(1)}, f32[4,64,128]{2,1,0:T(8,128)S(1)}, u32[]{:S(2)}, u32[]{:S(2)}) collective-permute-start(f32[4,64,128]{2,1,0:T(8,128)S(1)} %get-tuple-element.37), channel_id=1, source_target_pairs={{1,2},{2,1},{3,4},{4,3},{5,6},{6,5},{7,8},{8,7},{9,10},{10,9},{11,... | collective-permute-start | bytes 393224 | tf_op jit(solution)/shard_map/ppermute | solution.py:573
  11.3 3.1 %collective-permute-start.2 = (f32[2,3,8,128]{3,2,1,0:T(8,128)S(1)}, f32[2,3,8,128]{3,2,1,0:T(8,128)S(1)}, u32[]{:S(2)}, u32[]{:S(2)}) collective-permute-start(f32[2,3,8,128]{3,2,1,0:T(8,128)S(1)} %get-tuple-element.43), channel_id=1, source_target_pairs={{0,16},{16,0},{32,48},{48,32},{64,80},{80,64},{96,112},{112,96},{1... | collective-permute-start | bytes 73736 | tf_op jit(solution)/shard_map/ppermute | solution.py:573
  14.4 0.7 %collective-permute-start.3 = (f32[2,3,8,128]{3,2,1,0:T(8,128)S(1)}, f32[2,3,8,128]{3,2,1,0:T(8,128)S(1)}, u32[]{:S(2)}, u32[]{:S(2)}) collective-permute-start(f32[2,3,8,128]{3,2,1,0:T(8,128)S(1)} %get-tuple-element.44), channel_id=1, source_target_pairs={{16,32},{32,16},{48,64},{64,48},{80,96},{96,80},{112,128},{128,112... | collective-permute-start | bytes 73736 | tf_op jit(solution)/shard_map/ppermute | solution.py:573
  15.0 0.0 collective-permute-done.rows_pair
  15.1 0.0 collective-permute-done.1.rows_gap
  15.1 1.8 %early_step.1 = (f32[2,66,8,128]{3,2,1,0:T(8,128)S(1)}, f32[2,4,80,128]{3,2,1,0:T(8,128)S(1)}, f32[2,2,64,128]{3,2,1,0:T(8,128)S(1)}, f32[16,8,128]{2,1,0:T(8,12...) custom-call(s32[1]{0:T(128)S(4)} %get-tuple-element.30.counts, ...), custom_call_target="tpu_custom_call" | custom-call | flops 10000000 | bytes 1000000 | tf_op jit(solution)/shard_map/early_step/pallas_call | solution.py:635
  16.9 0.0 collective-permute-done.2.rim_pair
  16.9 0.0 collective-permute-done.3.rim_gap
  16.9 0.7 %collective-permute-start.5 = (f32[2,2,8,128]{3,2,1,0:T(8,128)S(1)}, f32[2,2,8,128]{3,2,1,0:T(8,128)S(1)}, u32[]{:S(2)}, u32[]{:S(2)}) collective-permute-start(f32[2,2,8,128]{3,2,1,0:T(8,128)S(1)} %get-tuple-element.50), channel_id=1, source_target_pairs={{16,32},{32,16},{48,64},{64,48},{80,96},{96,80},{112,128},{128,112... | collective-permute-start | bytes 49160 | tf_op jit(solution)/shard_map/ppermute | solution.py:573
  17.6 7.6 %collective-permute-start.4 = (f32[2,2,8,128]{3,2,1,0:T(8,128)S(1)}, f32[2,2,8,128]{3,2,1,0:T(8,128)S(1)}, u32[]{:S(2)}, u32[]{:S(2)}) collective-permute-start(f32[2,2,8,128]{3,2,1,0:T(8,128)S(1)} %get-tuple-element.46.order), channel_id=1, source_target_pairs={{0,16},{16,0},{32,48},{48,32},{64,80},{80,64},{96,112},{112,96},{1... | collective-permute-start | bytes 49160 | tf_op jit(solution)/shard_map/ppermute | solution.py:573
  25.2 2.8 %middle_step.1 = (f32[64,8,128]{2,1,0:T(8,128)}, f32[64,8,128]{2,1,0:T(8,128)}, f32[64,8,128]{2,1,0:T(8,128)S(1)}, f32[64,8,128]{2,1,0:T(8,128)S(1)}, f32[16,8,128]{2,1,0:T(8,128)S(1)}) custom-call(s32[1]{0:T(128)S(4)} %get-tuple-element.30.counts, ...), custom_call_target="tpu_custom_call", output_to_operand_aliasing={{2}: (6, {}), {3}: (7, {})} | custom-call | flops 10000000 | bytes 1000000 | tf_op jit(solution)/shard_map/middle_step/pallas_call | solution.py:659
  28.1 0.0 collective-permute-done.5.next_gap
  28.1 0.0 collective-permute-done.4.next_pair
  28.1 1.3 %late_step.1 = (f32[128,128]{1,0:T(8,128)}, f32[2,4,8,128]{3,2,1,0:T(8,128)S(1)}, f32[2,68,8,128]{3,2,1,0:T(8,128)S(1)}, f32[2,66,8,128]{3,2,1,0:T(8,128)S(1)}, ...) custom-call(s32[1]{0:T(128)S(4)} %get-tuple-element.30.counts, ...), custom_call_target="tpu_custom_call", output_to_operand_aliasing={{2}: (2, {}), {3}: (3, {}), {4}: (4, {}), {5}: (5, {})} | custom-call | flops 1000000 | bytes 1000000 | tf_op jit(solution)/shard_map/late_step/pallas_call | solution.py:675
  29.4 12.8 %all-to-all-start = ((f32[64,2,128]{2,1,0:T(2,128)}), f32[64,2,128]{2,1,0:T(2,128)S(1)}, u32[]{:S(2)}, u32[]{:S(2)}) async-start(f32[64,2,128]{2,1,0:T(2,128)} %bitcast), calls=%async_computation | async-start | bytes 131072 | tf_op jit(solution)/shard_map/all_to_all | solution.py:763
  42.2 0.7 %place_ends.1 = (f32[64,8,128]{2,1,0:T(8,128)}, f32[64,8,128]{2,1,0:T(8,128)}) custom-call(s32[1]{0:T(128)S(4)} %get-tuple-element.30.counts, f32[2,4,8,128]{3,2,1,0:T(8,128)S(1)} %get-tuple-element.51.ends, f32[64,8,128]{2,1,0:T(8,128)} %get-tuple-element.52.theta_in, ...), custom_call_target="tpu_custom_call", output_to_operand_aliasing={{0}: (2, {}), {1}: (3, {})} | custom-call | flops 1000000 | bytes 1000000 | tf_op jit(solution)/shard_map/place_ends/pallas_call | solution.py:691
  42.9 10.4 %all-to-all-done = f32[64,2,128]{2,1,0:T(2,128)S(1)} async-done(((f32[64,2,128]{2,1,0:T(2,128)}), f32[64,2,128]{2,1,0:T(2,128)S(1)}, u32[]{:S(2)}, u32[]{:S(2)}) %all-to-all-start) | async-done | bytes 65568 | tf_op jit(solution)/shard_map/all_to_all | solution.py:763
  53.3 0.8 %composite.1 = f32[4,4,1,16]{3,2,1,0:T(1,128)} custom-call(s32[4]{0:T(128)S(4)} %get-tuple-element.31.camera, f32[128,128]{1,0:T(8,128)S(1)} %bitcast.2), custom_call_target="tpu_custom_call" | custom-call | tf_op jit(solution)/shard_map/composite/pallas_call | solution.py:705
  (1 shorter events, 0.0 us)
Async XLA Ops:
  2.6 12.4 %collective-permute-start = (f32[4,64,128]{2,1,0:T(8,128)S(1)}, f32[4,64,128]{2,1,0:T(8,128)S(1)}, u32[]{:S(2)}, u32[]{:S(2)}) collective-permute-start(f32[4,64,128]{2,1,0:T(8,128)S(1)} %get-tuple-element.36), channel_id=1, source_target_pairs={{0,1},{1,0},{2,3},{3,2},{4,5},{5,4},{6,7},{7,6},{8,9},{9,8},{10,11... | collective-permute-start | bytes 393224 | tf_op jit(solution)/shard_map/ppermute | solution.py:573
  5.2 9.8 %collective-permute-start.1 = (f32[4,64,128]{2,1,0:T(8,128)S(1)}, f32[4,64,128]{2,1,0:T(8,128)S(1)}, u32[]{:S(2)}, u32[]{:S(2)}) collective-permute-start(f32[4,64,128]{2,1,0:T(8,128)S(1)} %get-tuple-element.37), channel_id=1, source_target_pairs={{1,2},{2,1},{3,4},{4,3},{5,6},{6,5},{7,8},{8,7},{9,10},{10,9},{11,... | collective-permute-start | bytes 393224 | tf_op jit(solution)/shard_map/ppermute | solution.py:573
  11.3 5.6 %collective-permute-start.2 = (f32[2,3,8,128]{3,2,1,0:T(8,128)S(1)}, f32[2,3,8,128]{3,2,1,0:T(8,128)S(1)}, u32[]{:S(2)}, u32[]{:S(2)}) collective-permute-start(f32[2,3,8,128]{3,2,1,0:T(8,128)S(1)} %get-tuple-element.43), channel_id=1, source_target_pairs={{0,16},{16,0},{32,48},{48,32},{64,80},{80,64},{96,112},{112,96},{1... | collective-permute-start | bytes 73736 | tf_op jit(solution)/shard_map/ppermute | solution.py:573
  14.4 2.5 %collective-permute-start.3 = (f32[2,3,8,128]{3,2,1,0:T(8,128)S(1)}, f32[2,3,8,128]{3,2,1,0:T(8,128)S(1)}, u32[]{:S(2)}, u32[]{:S(2)}) collective-permute-start(f32[2,3,8,128]{3,2,1,0:T(8,128)S(1)} %get-tuple-element.44), channel_id=1, source_target_pairs={{16,32},{32,16},{48,64},{64,48},{80,96},{96,80},{112,128},{128,112... | collective-permute-start | bytes 73736 | tf_op jit(solution)/shard_map/ppermute | solution.py:573
  16.9 11.1 %collective-permute-start.5 = (f32[2,2,8,128]{3,2,1,0:T(8,128)S(1)}, f32[2,2,8,128]{3,2,1,0:T(8,128)S(1)}, u32[]{:S(2)}, u32[]{:S(2)}) collective-permute-start(f32[2,2,8,128]{3,2,1,0:T(8,128)S(1)} %get-tuple-element.50), channel_id=1, source_target_pairs={{16,32},{32,16},{48,64},{64,48},{80,96},{96,80},{112,128},{128,112... | collective-permute-start | bytes 49160 | tf_op jit(solution)/shard_map/ppermute | solution.py:573
  17.6 10.5 %collective-permute-start.4 = (f32[2,2,8,128]{3,2,1,0:T(8,128)S(1)}, f32[2,2,8,128]{3,2,1,0:T(8,128)S(1)}, u32[]{:S(2)}, u32[]{:S(2)}) collective-permute-start(f32[2,2,8,128]{3,2,1,0:T(8,128)S(1)} %get-tuple-element.46.order), channel_id=1, source_target_pairs={{0,16},{16,0},{32,48},{48,32},{64,80},{80,64},{96,112},{112,96},{1... | collective-permute-start | bytes 49160 | tf_op jit(solution)/shard_map/ppermute | solution.py:573
  29.4 23.8 %all-to-all-start = ((f32[64,2,128]{2,1,0:T(2,128)}), f32[64,2,128]{2,1,0:T(2,128)S(1)}, u32[]{:S(2)}, u32[]{:S(2)}) async-start(f32[64,2,128]{2,1,0:T(2,128)} %bitcast), calls=%async_computation | async-start | bytes 131072 | tf_op jit(solution)/shard_map/all_to_all | solution.py:763

commit v5 on v4

--- a/solution.py
+++ b/solution.py
@@ -29,9 +29,9 @@
 
 
 UNROLL_1 = 16
-UNROLL_EARLY = 16
-UNROLL_MIDDLE = 22
-EARLY = 16
+UNROLL_EARLY = 14
+UNROLL_MIDDLE = 16
+EARLY = 28
 
 
 def is_even(axis):
@@ -469,21 +469,27 @@
             )
 
     zero = jnp.zeros((8, 128), F32)
-    segments = []
-    for slot, start in ((0, 0), (2, jnp.maximum(depth_count - 2, 2))):
+    pairs = ((0, 0), (2, jnp.maximum(depth_count - 2, 2)))
+    stepped_ends = []
+    for slot, start in pairs:
 
         def edge_rows(j, start=start):
             return rows_beside(edge1, (0, 1), start + j)
 
+        fresh = block_step(field1, start + 1, 2, edge_rows)
+        alive = [start + j < depth_count for j in range(2)]
+        fresh = [[jnp.where(alive[j], value, 0.0) for value in fresh[j]] for j in range(2)]
+        stepped_ends.append((alive, fresh))
+        for number in range(2):
+            for j in range(2):
+                ends[number, slot + j] = fresh[j][number]
+    segments = []
+    for alive, fresh in stepped_ends:
         segment = [zero] * (4 * functions)
-        for j, new in enumerate(block_step(field1, start + 1, 2, edge_rows)):
-            place = start + j
-            alive = place < depth_count
+        for j in range(2):
             for number in range(2):
-                value = jnp.where(alive, new[number], 0.0)
-                ends[number, slot + j] = value
-                at = look_up(low_table, rise_table, value)
-                add_layer(segment, number, at, alive)
+                at = look_up(low_table, rise_table, fresh[j][number])
+                add_layer(segment, number, at, alive[j])
         segments.append(segment)
 
     head, tail = segments
@@ -516,22 +522,22 @@
             image[pl.ds(2 * g + half, 8, stride=16), :] = regs[g]
 
 
-def place_ends(counts, ends, theta_in, fuel_in, theta_next, fuel_next, copies):
+def composite(
+    counts, camera, pieces, ends, theta_in, fuel_in, image_out, theta_next, fuel_next, image, copies
+):
+    sources = pieces.shape[0] // 2
     leave = [
         pltpu.make_async_copy(
-            ends.at[number, pl.ds(slot, 2)], out.at[pl.ds(place, 2)], copies.at[number, slot // 2]
+            ends.at[number, pl.ds(slot, 2)],
+            out.at[pl.ds(place, 2)],
+            copies.at[slot + number],
         )
         for number, out in enumerate((theta_next, fuel_next))
         for slot, place in ((0, 0), (2, jnp.maximum(counts[0] - 2, 2)))
     ]
     for copy in leave:
         copy.start()
-    for copy in leave:
-        copy.wait()
-
-
-def composite(camera, pieces, image):
-    sources = pieces.shape[0] // 2
+    leave.append(pltpu.make_async_copy(image, image_out, copies.at[4]))
     lane = lanes()
     row = sublanes()
     opacity_lane = lane // 64 * 64 + 48 + lane % 16
@@ -563,6 +569,9 @@
         for clo in range(8):
             channel = 8 * half + clo
             image[channel // 4, channel % 4] = line[:, 16 * clo : 16 * clo + 16]
+    leave[-1].start()
+    for copy in leave:
+        copy.wait()
 
 
 def swapped(array, axis, first):
@@ -686,30 +695,19 @@
     return image, ends
 
 
-def end_kernel(counts, ends, *fields):
+def last_kernel(functions, counts, camera, pieces, ends, *fields):
     field = jax.ShapeDtypeStruct(fields[0].shape, F32)
-    return pl.pallas_call(
-        place_ends,
-        out_shape=(field, field),
-        in_specs=[in_smem(), in_vmem()] + [anywhere()] * 2,
-        out_specs=(anywhere(),) * 2,
-        scratch_shapes=[pltpu.SemaphoreType.DMA((2, 2))],
-        input_output_aliases={2: 0, 3: 1},
-        compiler_params=params(),
-        cost_estimate=cost(10**6),
-        name="place_ends",
-    )(in_scalars(counts), held(ends), *map(in_hbm, fields))
-
-
-def last_kernel(functions, camera, pieces):
+    image = (functions, 4, 1, 16)
     return pl.pallas_call(
         composite,
-        out_shape=jax.ShapeDtypeStruct((functions, 4, 1, 16), F32),
-        in_specs=[in_smem(), in_vmem()],
-        out_specs=in_vmem(),
+        out_shape=(jax.ShapeDtypeStruct(image, F32), field, field),
+        in_specs=[in_smem()] * 2 + [in_vmem()] * 2 + [anywhere()] * 2,
+        out_specs=(anywhere(),) * 3,
+        scratch_shapes=[VMEM(image, F32), pltpu.SemaphoreType.DMA((5,))],
+        input_output_aliases={4: 1, 5: 2},
         compiler_params=params(),
         name="composite",
-    )(in_scalars(camera), held(pieces))
+    )(*map(in_scalars, (counts, camera)), *map(held, (pieces, ends)), *map(in_hbm, fields))
 
 
 def on_device(
@@ -761,8 +759,9 @@
         next_gap,
     )
     pieces = lax.all_to_all(pieces, "depth", 0, 0, tiled=True)
-    theta_next, fuel_next = end_kernel(counts, ends, theta_next, fuel_next)
-    image = last_kernel(choice.shape[0], camera, pieces)
+    image, theta_next, fuel_next = last_kernel(
+        choice.shape[0], counts, camera, pieces, ends, theta_next, fuel_next
+    )
     return (theta_next, fuel_next, image)
 
 

time: 54.4 us -> 53.1 us (0.976)
  blocking collectives: 0 us -> 23.6 us
  starting transfers between devices: 33.4 us -> 20 us
  waiting for transfers between devices: 10.4 us -> 0.02 us
  Pallas kernels: 8.81 us -> 7.67 us
    all_to_all x0 -> x1, blocking collectives: none -> 23.6 us  [on_device(): pieces = lax.all_to_all(pieces, 'depth', 0, 0, tiled=True)]
    all_to_all x1 -> x0, starting transfers between devices: 12.8 us -> none  [on_device(): pieces = lax.all_to_all(pieces, 'depth', 0, 0, tiled=True)]
    all_to_all x1 -> x0, waiting for transfers between devices: 10.4 us -> none  [on_device(): pieces = lax.all_to_all(pieces, 'depth', 0, 0, tiled=True)]
    ppermute x6, starting transfers between devices: 20.7 us -> 20 us  [swapped(): return lax.ppermute(array, axis, pairs)]
    pallas_call x1, Pallas kernels: 1.8 us -> 2.46 us  [early_kernel(): pl.pallas_call(functools.partial(early_step, places, functions, float(MEA...]
    pallas_call x1, Pallas kernels: 1.34 us -> 0.71 us  [late_kernel(): pl.pallas_call(functools.partial(late_step, functions), out_shape=(VMEM((...]
    pallas_call x2 -> x1, Pallas kernels: 1.46 us -> 0.86 us  [last_kernel(): pl.pallas_call(composite, out_shape=(jax.ShapeDtypeStruct(image, F32), fi...]
    pallas_call x1, Pallas kernels: 2.84 us -> 2.27 us  [middle_kernel(): pl.pallas_call(functools.partial(middle_step, theta_next.shape[0]), out_s...]
  transfers between devices with their start and end apart: 7 -> 6, of which waited for: 1 -> 0; matrix products, arithmetic and copies ran while one was open for 0% -> 0% of each run, Pallas kernels for 10% -> 9%
where the time goes in v5:
time: 53.1 us; the launch traced here: 52.7 us
  blocking collectives  23.6 us (44%)
  starting transfers between devices  20 us (38%)
  Pallas kernels  7.67 us (14%)
  between operations  1.41 us (3%)
    all_to_all x1, blocking collectives, on_device(): pieces = lax.all_to_all(pieces, 'depth', 0, 0, tiled=True)  23.6 us
    ppermute x6, starting transfers between devices, swapped(): return lax.ppermute(array, axis, pairs)  20 us
    pallas_call x1, Pallas kernels, early_kernel(): pl.pallas_call(functools.partial(early_step, places, functions, float(MEA...  2.46 us
    pallas_call x1, Pallas kernels, middle_kernel(): pl.pallas_call(functools.partial(middle_step, theta_next.shape[0]), out_s...  2.27 us
    pallas_call x1, Pallas kernels, first_kernel(): pl.pallas_call(pack_rows, out_shape=tuple((SMEM(x.shape, jnp.int32) for x...  1.35 us
  transfers between devices with their start and end apart: 6, of which 0 were waited for; matrix products, arithmetic and copies ran while one was open for 0% of the time, Pallas kernels for 9%

profile of v5, /device:TPU:385, one launch (start us, length us, event | category | flops | bytes accessed | tf_op | source)
XLA Modules:
  0.0 52.7 jit_solution(3205508324158069777)
XLA Ops:
  1.3 1.3 %pack_rows.1 = (s32[1]{0:T(128)S(4)}, s32[4]{0:T(128)S(4)}, s32[4]{0:T(128)S(4)}, bf16[8,4,128]{2,1,0:T(4,128)(2,1)S(1)}, f32[2,68,8,128]{3,2,1,0:T(8,128)S(1)},...) custom-call(s32[1]{0:T(128)S(6)} %copy.25.counts_in, ...), custom_call_target="tpu_custom_call" | custom-call | tf_op jit(solution)/shard_map/pack_rows/pallas_call | solution.py:609
  2.6 2.6 %collective-permute-start = (f32[4,64,128]{2,1,0:T(8,128)S(1)}, f32[4,64,128]{2,1,0:T(8,128)S(1)}, u32[]{:S(2)}, u32[]{:S(2)}) collective-permute-start(f32[4,64,128]{2,1,0:T(8,128)S(1)} %get-tuple-element.37), channel_id=1, source_target_pairs={{0,1},{1,0},{2,3},{3,2},{4,5},{5,4},{6,7},{7,6},{8,9},{9,8},{10,11... | collective-permute-start | bytes 393224 | tf_op jit(solution)/shard_map/ppermute | solution.py:582
  5.2 6.0 %collective-permute-start.1 = (f32[4,64,128]{2,1,0:T(8,128)S(1)}, f32[4,64,128]{2,1,0:T(8,128)S(1)}, u32[]{:S(2)}, u32[]{:S(2)}) collective-permute-start(f32[4,64,128]{2,1,0:T(8,128)S(1)} %get-tuple-element.38), channel_id=1, source_target_pairs={{1,2},{2,1},{3,4},{4,3},{5,6},{6,5},{7,8},{8,7},{9,10},{10,9},{11,... | collective-permute-start | bytes 393224 | tf_op jit(solution)/shard_map/ppermute | solution.py:582
  11.3 3.1 %collective-permute-start.2 = (f32[2,3,8,128]{3,2,1,0:T(8,128)S(1)}, f32[2,3,8,128]{3,2,1,0:T(8,128)S(1)}, u32[]{:S(2)}, u32[]{:S(2)}) collective-permute-start(f32[2,3,8,128]{3,2,1,0:T(8,128)S(1)} %get-tuple-element.44), channel_id=1, source_target_pairs={{0,16},{16,0},{32,48},{48,32},{64,80},{80,64},{96,112},{112,96},{1... | collective-permute-start | bytes 73736 | tf_op jit(solution)/shard_map/ppermute | solution.py:582
  14.4 0.7 %collective-permute-start.3 = (f32[2,3,8,128]{3,2,1,0:T(8,128)S(1)}, f32[2,3,8,128]{3,2,1,0:T(8,128)S(1)}, u32[]{:S(2)}, u32[]{:S(2)}) collective-permute-start(f32[2,3,8,128]{3,2,1,0:T(8,128)S(1)} %get-tuple-element.45), channel_id=1, source_target_pairs={{16,32},{32,16},{48,64},{64,48},{80,96},{96,80},{112,128},{128,112... | collective-permute-start | bytes 73736 | tf_op jit(solution)/shard_map/ppermute | solution.py:582
  15.0 0.0 collective-permute-done.rows_pair
  15.1 0.0 collective-permute-done.1.rows_gap
  15.1 2.5 %early_step.1 = (f32[2,66,8,128]{3,2,1,0:T(8,128)S(1)}, f32[2,4,80,128]{3,2,1,0:T(8,128)S(1)}, f32[2,2,64,128]{3,2,1,0:T(8,128)S(1)}, f32[16,8,128]{2,1,0:T(8,12...) custom-call(s32[1]{0:T(128)S(4)} %get-tuple-element.31.counts, ...), custom_call_target="tpu_custom_call" | custom-call | flops 10000000 | bytes 1000000 | tf_op jit(solution)/shard_map/early_step/pallas_call | solution.py:644
  17.5 0.0 collective-permute-done.2.rim_pair
  17.5 0.0 collective-permute-done.3.rim_gap
  17.6 0.7 %collective-permute-start.5 = (f32[2,2,8,128]{3,2,1,0:T(8,128)S(1)}, f32[2,2,8,128]{3,2,1,0:T(8,128)S(1)}, u32[]{:S(2)}, u32[]{:S(2)}) collective-permute-start(f32[2,2,8,128]{3,2,1,0:T(8,128)S(1)} %get-tuple-element.51), channel_id=1, source_target_pairs={{16,32},{32,16},{48,64},{64,48},{80,96},{96,80},{112,128},{128,112... | collective-permute-start | bytes 49160 | tf_op jit(solution)/shard_map/ppermute | solution.py:582
  18.3 7.0 %collective-permute-start.4 = (f32[2,2,8,128]{3,2,1,0:T(8,128)S(1)}, f32[2,2,8,128]{3,2,1,0:T(8,128)S(1)}, u32[]{:S(2)}, u32[]{:S(2)}) collective-permute-start(f32[2,2,8,128]{3,2,1,0:T(8,128)S(1)} %get-tuple-element.47.order), channel_id=1, source_target_pairs={{0,16},{16,0},{32,48},{48,32},{64,80},{80,64},{96,112},{112,96},{1... | collective-permute-start | bytes 49160 | tf_op jit(solution)/shard_map/ppermute | solution.py:582
  25.2 2.3 %middle_step.1 = (f32[64,8,128]{2,1,0:T(8,128)}, f32[64,8,128]{2,1,0:T(8,128)}, f32[64,8,128]{2,1,0:T(8,128)S(1)}, f32[64,8,128]{2,1,0:T(8,128)S(1)}, f32[16,8,128]{2,1,0:T(8,128)S(1)}) custom-call(s32[1]{0:T(128)S(4)} %get-tuple-element.31.counts, ...), custom_call_target="tpu_custom_call", output_to_operand_aliasing={{2}: (6, {}), {3}: (7, {})} | custom-call | flops 10000000 | bytes 1000000 | tf_op jit(solution)/shard_map/middle_step/pallas_call | solution.py:668
  27.5 0.0 collective-permute-done.5.next_gap
  27.5 0.0 collective-permute-done.4.next_pair
  27.5 0.7 %late_step.1 = (f32[128,128]{1,0:T(8,128)S(1)}, f32[2,4,8,128]{3,2,1,0:T(8,128)S(1)}, f32[2,68,8,128]{3,2,1,0:T(8,128)S(1)}, f32[2,66,8,128]{3,2,1,0:T(8,128)S(1...) custom-call(s32[1]{0:T(128)S(4)} %get-tuple-element.31.counts, ...), custom_call_target="tpu_custom_call", output_to_operand_aliasing={{2}: (2, {}), {3}: (3, {}), {4}: (4, {}), {5}: (5, {})} | custom-call | flops 1000000 | bytes 1000000 | tf_op jit(solution)/shard_map/late_step/pallas_call | solution.py:684
  28.2 23.6 %all_to_all.11 = f32[64,2,128]{2,1,0:T(2,128)S(1)} all-to-all(f32[64,2,128]{2,1,0:T(2,128)S(1)} %bitcast.3), channel_id=1, replica_groups=mesh['depth'=64,'lat'=16] {'depth'}, dimensions={0} | all-to-all | bytes 131072 | tf_op jit(solution)/shard_map/all_to_all | solution.py:761
  51.9 0.9 %composite.1 = (f32[4,4,1,16]{3,2,1,0:T(1,128)}, f32[64,8,128]{2,1,0:T(8,128)}, f32[64,8,128]{2,1,0:T(8,128)}) custom-call(s32[1]{0:T(128)S(4)} %get-tuple-element.31.counts, s32[4]{0:T(128)S(4)} %get-tuple-element.32.camera, f32[128,128]{1,0:T(8,128)S(1)} %bitcast.2, ...), custom_call_target="tpu_custom_call", output_to_operand_aliasing={{1}: (4, {}), {2}: (5, {})} | custom-call | tf_op jit(solution)/shard_map/composite/pallas_call | solution.py:701
  (1 shorter events, 0.0 us)
Async XLA Ops:
  2.6 12.4 %collective-permute-start = (f32[4,64,128]{2,1,0:T(8,128)S(1)}, f32[4,64,128]{2,1,0:T(8,128)S(1)}, u32[]{:S(2)}, u32[]{:S(2)}) collective-permute-start(f32[4,64,128]{2,1,0:T(8,128)S(1)} %get-tuple-element.37), channel_id=1, source_target_pairs={{0,1},{1,0},{2,3},{3,2},{4,5},{5,4},{6,7},{7,6},{8,9},{9,8},{10,11... | collective-permute-start | bytes 393224 | tf_op jit(solution)/shard_map/ppermute | solution.py:582
  5.2 9.8 %collective-permute-start.1 = (f32[4,64,128]{2,1,0:T(8,128)S(1)}, f32[4,64,128]{2,1,0:T(8,128)S(1)}, u32[]{:S(2)}, u32[]{:S(2)}) collective-permute-start(f32[4,64,128]{2,1,0:T(8,128)S(1)} %get-tuple-element.38), channel_id=1, source_target_pairs={{1,2},{2,1},{3,4},{4,3},{5,6},{6,5},{7,8},{8,7},{9,10},{10,9},{11,... | collective-permute-start | bytes 393224 | tf_op jit(solution)/shard_map/ppermute | solution.py:582
  11.3 6.3 %collective-permute-start.2 = (f32[2,3,8,128]{3,2,1,0:T(8,128)S(1)}, f32[2,3,8,128]{3,2,1,0:T(8,128)S(1)}, u32[]{:S(2)}, u32[]{:S(2)}) collective-permute-start(f32[2,3,8,128]{3,2,1,0:T(8,128)S(1)} %get-tuple-element.44), channel_id=1, source_target_pairs={{0,16},{16,0},{32,48},{48,32},{64,80},{80,64},{96,112},{112,96},{1... | collective-permute-start | bytes 73736 | tf_op jit(solution)/shard_map/ppermute | solution.py:582
  14.4 3.2 %collective-permute-start.3 = (f32[2,3,8,128]{3,2,1,0:T(8,128)S(1)}, f32[2,3,8,128]{3,2,1,0:T(8,128)S(1)}, u32[]{:S(2)}, u32[]{:S(2)}) collective-permute-start(f32[2,3,8,128]{3,2,1,0:T(8,128)S(1)} %get-tuple-element.45), channel_id=1, source_target_pairs={{16,32},{32,16},{48,64},{64,48},{80,96},{96,80},{112,128},{128,112... | collective-permute-start | bytes 73736 | tf_op jit(solution)/shard_map/ppermute | solution.py:582
  17.6 9.9 %collective-permute-start.5 = (f32[2,2,8,128]{3,2,1,0:T(8,128)S(1)}, f32[2,2,8,128]{3,2,1,0:T(8,128)S(1)}, u32[]{:S(2)}, u32[]{:S(2)}) collective-permute-start(f32[2,2,8,128]{3,2,1,0:T(8,128)S(1)} %get-tuple-element.51), channel_id=1, source_target_pairs={{16,32},{32,16},{48,64},{64,48},{80,96},{96,80},{112,128},{128,112... | collective-permute-start | bytes 49160 | tf_op jit(solution)/shard_map/ppermute | solution.py:582
  18.3 9.3 %collective-permute-start.4 = (f32[2,2,8,128]{3,2,1,0:T(8,128)S(1)}, f32[2,2,8,128]{3,2,1,0:T(8,128)S(1)}, u32[]{:S(2)}, u32[]{:S(2)}) collective-permute-start(f32[2,2,8,128]{3,2,1,0:T(8,128)S(1)} %get-tuple-element.47.order), channel_id=1, source_target_pairs={{0,16},{16,0},{32,48},{48,32},{64,80},{80,64},{96,112},{112,96},{1... | collective-permute-start | bytes 49160 | tf_op jit(solution)/shard_map/ppermute | solution.py:582

commit v6 on v5

--- a/solution.py
+++ b/solution.py
@@ -29,9 +29,7 @@
 
 
 UNROLL_1 = 16
-UNROLL_EARLY = 14
-UNROLL_MIDDLE = 16
-EARLY = 28
+WINDOWS = ((12, 12), (24, 12), (24, 12))
 
 
 def is_even(axis):
@@ -58,7 +56,6 @@
     rows_pair,
     rows_gap,
     rim_pair,
-    rim_gap,
     copies,
 ):
     places = theta.shape[0]
@@ -96,29 +93,40 @@
         down = (field0[number, 2], field0[number, second], size)
         for layer in range(3):
             rim_pair[number, layer] = select(depth_even, up[layer], down[layer])
-            rim_gap[number, layer] = select(depth_even, down[layer], up[layer])
     for copy in fetch[3:]:
         copy.wait()
 
 
-def pack_rims(counts, rows_pair, rows_gap, rim_pair, rim_gap, order, next_pair, next_gap):
-    last = counts[0] - 1
-    lat_even, depth_even = is_even("lat"), is_even("depth")
+def beside(rows_pair, rows_gap, number, place):
+    lat_even = is_even("lat")
+    below = [ref[2 * number + 1, pl.ds(place, 1), :] for ref in (rows_gap, rows_pair)]
+    above = [ref[2 * number, pl.ds(place, 1), :] for ref in (rows_pair, rows_gap)]
+    rows = (select(lat_even, *below), select(lat_even, *above))
+    return tuple(jnp.broadcast_to(x, (8, 128)) for x in rows)
+
+
+def pack_gap(counts, field0, rows_pair, rows_gap, rim_pair, order, rim_gap):
+    depth_count = counts[0]
+    depth_even = is_even("depth")
+    end = jnp.where(depth_even, 0, depth_count - 1)
+    inward = jnp.where(depth_even, 1, jnp.maximum(depth_count - 2, 0))
+    size = depth_count.astype(F32)
+    row = sublanes()
     for number in range(2):
-        from_above = select(depth_even, rim_pair[number, 0], rim_gap[number, 0])
-        from_below = select(depth_even, rim_gap[number, 0], rim_pair[number, 0])
-
-        def beside(place):
-            below = [ref[2 * number + 1, pl.ds(place, 1), :] for ref in (rows_gap, rows_pair)]
-            above = [ref[2 * number, pl.ds(place, 1), :] for ref in (rows_pair, rows_gap)]
-            rows = [select(lat_even, *below), select(lat_even, *above)]
-            return jnp.where(sublanes() == 0, *(jnp.broadcast_to(x, (8, 128)) for x in rows))
-
-        up = (from_below, beside(last))
-        down = (from_above, beside(0))
-        for layer in range(2):
-            next_pair[number, layer] = select(depth_even, up[layer], down[layer])
-            next_gap[number, layer] = select(depth_even, down[layer], up[layer])
+        rim_gap[number, 0] = field0[number, 2 + end]
+        rim_gap[number, 1] = select(
+            depth_count == 1, rim_pair[number, 0], field0[number, 2 + inward]
+        )
+        below, above = beside(rows_pair, rows_gap, number, end)
+        rim_gap[number, 2] = jnp.where(row == 0, below, jnp.where(row == 1, above, size))
+
+
+def pack_next(counts, rows_pair, rows_gap, rim_gap, order, next_pair):
+    end = jnp.where(is_even("depth"), counts[0] - 1, 0)
+    for number in range(2):
+        next_pair[number, 0] = rim_gap[number, 0]
+        below, above = beside(rows_pair, rows_gap, number, end)
+        next_pair[number, 1] = jnp.where(sublanes() == 0, below, above)
 
 
 def lanes():
@@ -332,8 +340,7 @@
             out[place] = zero
     found = inner_layers(
         2,
-        EARLY,
-        UNROLL_EARLY,
+        *WINDOWS[0],
         counts[0],
         field1,
         edge1,
@@ -347,6 +354,7 @@
 
 def middle_step(
     places,
+    window,
     counts,
     field1,
     edge1,
@@ -356,13 +364,14 @@
     theta_in,
     fuel_in,
     sums_in,
-    theta_out,
-    fuel_out,
-    theta_next,
-    fuel_next,
-    sums,
-    copies,
+    *outs,
 ):
+    last = window == len(WINDOWS) - 1
+    if last:
+        theta_out, fuel_out, theta_next, fuel_next, sums, copies = outs
+    else:
+        theta_next, fuel_next, sums = outs
+
     def leave(number, first, count):
         return pltpu.make_async_copy(
             (theta_next, fuel_next)[number].at[pl.ds(first, count)],
@@ -374,24 +383,26 @@
         for number in range(2):
             leave(number, first, count).start()
 
-    start_leaving(0, 2 + EARLY)
-    start_leaving(places - 2, 2)
+    first = 2 + sum(layers for layers, unroll in WINDOWS[:window])
+    if last:
+        start_leaving(0, first)
+        start_leaving(places - 2, 2)
     found = inner_layers(
-        2 + EARLY,
-        places - 4 - EARLY,
-        UNROLL_MIDDLE,
+        first,
+        *WINDOWS[window],
         counts[0],
         field1,
         edge1,
         (low_table, rise_table),
         (theta_next, fuel_next),
         [sums_in[entry] for entry in range(sums_in.shape[0])],
-        start_leaving,
+        start_leaving if last else None,
     )
     for entry, value in enumerate(found):
         sums[entry] = value
-    for number in range(2):
-        leave(number, 0, places).wait()
+    if last:
+        for number in range(2):
+            leave(number, 0, places).wait()
 
 
 def late_step(
@@ -409,7 +420,6 @@
     rim_pair,
     rim_gap,
     next_pair,
-    next_gap,
     image,
     ends,
     field0,
@@ -420,32 +430,24 @@
     depth_count = counts[0]
     depth_even = is_even("depth")
 
-    def from_below(pair, gap, *at):
-        return select(depth_even, gap[at], pair[at])
-
-    def from_above(pair, gap, *at):
-        return select(depth_even, pair[at], gap[at])
-
-    below_size = from_below(rim_pair, rim_gap, 0, 2)
-    above_size = from_above(rim_pair, rim_gap, 0, 2)
+    def sides(pair, gap):
+        return select(depth_even, gap, pair), select(depth_even, pair, gap)
+
+    pair_size = rim_pair[0, 2]
+    gap_size = jnp.broadcast_to(rim_gap[0, 2, 2:3], (8, 128))
+    below_size, above_size = sides(pair_size, gap_size)
     for number in range(2):
-        field0[number, 0] = jnp.where(
-            below_size == 1.0,
-            from_below(next_pair, next_gap, number, 0),
-            from_below(rim_pair, rim_gap, number, 1),
-        )
-        field0[number, 1] = from_below(rim_pair, rim_gap, number, 0)
-        field0[number, depth_count + 2] = from_above(rim_pair, rim_gap, number, 0)
-        field0[number, depth_count + 3] = jnp.where(
-            above_size == 1.0,
-            from_above(next_pair, next_gap, number, 0),
-            from_above(rim_pair, rim_gap, number, 1),
-        )
-        below_rows = from_below(next_pair, next_gap, number, 1)
-        above_rows = from_above(next_pair, next_gap, number, 1)
+        nearest = sides(rim_pair[number, 0], rim_gap[number, 0])
+        second = jnp.where(pair_size == 1.0, next_pair[number, 0], rim_pair[number, 1])
+        second = sides(second, rim_gap[number, 1])
+        rows = sides(next_pair[number, 1], rim_gap[number, 2])
+        field0[number, 0] = second[0]
+        field0[number, 1] = nearest[0]
+        field0[number, depth_count + 2] = nearest[1]
+        field0[number, depth_count + 3] = second[1]
         for side in range(2):
-            edge0[number, 1 + side, LEAD - 1 : LEAD] = below_rows[side : side + 1]
-            edge0[number, 1 + side, pl.ds(LEAD + depth_count, 1)] = above_rows[side : side + 1]
+            edge0[number, 1 + side, LEAD - 1 : LEAD] = rows[0][side : side + 1]
+            edge0[number, 1 + side, pl.ds(LEAD + depth_count, 1)] = rows[1][side : side + 1]
     for place in (0, depth_count - 1):
         for side in range(2):
             fresh = step_edges(edge0, own_rows, side, LEAD + place, place, 1)
@@ -610,25 +612,24 @@
         pack_rows,
         out_shape=tuple(SMEM(x.shape, jnp.int32) for x in (counts, choice, camera))
         + (VMEM(library.shape, library.dtype), VMEM((2, places + 4, 8, 128), F32))
-        + (rows, rows, rows, rim, rim),
+        + (rows, rows, rows, rim),
         in_specs=[anywhere()] * 6,
-        out_specs=(in_smem(),) * 3 + (in_vmem(),) * 7,
+        out_specs=(in_smem(),) * 3 + (in_vmem(),) * 6,
         scratch_shapes=[pltpu.SemaphoreType.DMA((6,))],
         compiler_params=params(),
         name="pack_rows",
     )(counts, *map(in_hbm, (choice, camera, theta, fuel, library)))
 
 
-def rim_kernel(counts, *received):
-    rim = VMEM((2, 2, 8, 128), F32)
+def rim_kernel(body, layers, counts, *arrays):
     return pl.pallas_call(
-        pack_rims,
-        out_shape=(rim, rim),
-        in_specs=[in_smem()] + [in_vmem()] * len(received),
-        out_specs=(in_vmem(),) * 2,
+        body,
+        out_shape=VMEM((2, layers, 8, 128), F32),
+        in_specs=[in_smem()] + [in_vmem()] * len(arrays),
+        out_specs=in_vmem(),
         compiler_params=params(),
-        name="pack_rims",
-    )(in_scalars(counts), *map(held, received))
+        name=body.__name__,
+    )(in_scalars(counts), *map(held, arrays))
 
 
 def cost(flops):
@@ -662,16 +663,18 @@
     )(*map(in_scalars, (counts, choice, camera)), *map(held, (field0, library, *rows)))
 
 
-def middle_kernel(counts, *arrays):
+def middle_kernel(window, counts, *arrays):
     theta_next, fuel_next, sums = arrays[-3:]
     field = jax.ShapeDtypeStruct(theta_next.shape, F32)
+    last = window == len(WINDOWS) - 1
+    lead = 2 if last else 0
     return pl.pallas_call(
-        functools.partial(middle_step, theta_next.shape[0]),
-        out_shape=(field, field) + tuple(VMEM(x.shape, F32) for x in (theta_next, fuel_next, sums)),
+        functools.partial(middle_step, theta_next.shape[0], window),
+        out_shape=(field,) * lead + tuple(VMEM(x.shape, F32) for x in (theta_next, fuel_next, sums)),
         in_specs=[in_smem()] + [in_vmem()] * len(arrays),
-        out_specs=(anywhere(),) * 2 + (in_vmem(),) * 3,
-        scratch_shapes=[pltpu.SemaphoreType.DMA((2,))],
-        input_output_aliases={len(arrays) - 2 + i: 2 + i for i in range(2)},
+        out_specs=(anywhere(),) * lead + (in_vmem(),) * 3,
+        scratch_shapes=[pltpu.SemaphoreType.DMA((2,))] if last else [],
+        input_output_aliases={len(arrays) - 2 + i: lead + i for i in range(2)},
         compiler_params=params(),
         cost_estimate=cost(10**7),
         name="middle_step",
@@ -727,19 +730,21 @@
         reactant_fraction,
         colour_lookup_library,
     )
+    rows_pair = swapped(messages[0], "lat", 0)
     rows_gap = swapped(messages[1], "lat", 1)
-    rows_pair = swapped(messages[0], "lat", 0)
-    rim_gap = swapped(messages[3], "depth", 1)
     rim_pair = swapped(messages[2], "depth", 0)
     field1, edge0, edge1, low_table, rise_table, theta_next, fuel_next, sums = early_kernel(
         devices, counts, choice, camera, field0, library, own_rows, rows_pair, rows_gap
     )
-    next_pair, next_gap = rim_kernel(counts, rows_pair, rows_gap, rim_pair, rim_gap, sums)
-    order = next_pair
-    next_gap = swapped(next_gap, "depth", 1)
-    next_pair = swapped(next_pair, "depth", 0)
+    order = rim_kernel(pack_gap, 3, counts, field0, rows_pair, rows_gap, rim_pair, sums)
+    rim_gap = swapped(order, "depth", 1)
+    theta_next, fuel_next, sums = middle_kernel(
+        1, counts, field1, edge1, low_table, rise_table, order, theta_next, fuel_next, sums
+    )
+    order = rim_kernel(pack_next, 2, counts, rows_pair, rows_gap, rim_gap, sums)
+    next_pair = swapped(order, "depth", 0)
     theta_next, fuel_next, _, _, sums = middle_kernel(
-        counts, field1, edge1, low_table, rise_table, order, theta_next, fuel_next, sums
+        2, counts, field1, edge1, low_table, rise_table, order, theta_next, fuel_next, sums
     )
     pieces, ends = late_kernel(
         devices,
@@ -756,7 +761,6 @@
         rim_pair,
         rim_gap,
         next_pair,
-        next_gap,
     )
     pieces = lax.all_to_all(pieces, "depth", 0, 0, tiled=True)
     image, theta_next, fuel_next = last_kernel(

time: 53.1 us -> 53.6 us (level)
  the two profiles are of different devices: /device:TPU:385 before, /device:TPU:512 now
where the time goes in v6:
time: 53.6 us; the launch traced here: 53.4 us
  blocking collectives  27.2 us (51%)
  starting transfers between devices  15 us (28%)
  Pallas kernels  7.65 us (14%)
  waiting for transfers between devices  2.16 us (4%)
  between operations  1.4 us (3%)
    all_to_all x1, blocking collectives, on_device(): pieces = lax.all_to_all(pieces, 'depth', 0, 0, tiled=True)  27.2 us
    ppermute x5, starting transfers between devices, swapped(): return lax.ppermute(array, axis, pairs)  15 us
    pallas_call x2, Pallas kernels, middle_kernel(): pl.pallas_call(functools.partial(middle_step, theta_next.shape[0], window...  3.08 us
    ppermute x5, waiting for transfers between devices, swapped(): return lax.ppermute(array, axis, pairs)  2.16 us
    pallas_call x1, Pallas kernels, early_kernel(): pl.pallas_call(functools.partial(early_step, places, functions, float(MEA...  1.61 us
    pallas_call x1, Pallas kernels, first_kernel(): pl.pallas_call(pack_rows, out_shape=tuple((SMEM(x.shape, jnp.int32) for x...  1.35 us
  transfers between devices with their start and end apart: 5, of which 1 were waited for; matrix products, arithmetic and copies ran while one was open for 0% of the time, Pallas kernels for 9%

profile of v6, /device:TPU:512, one launch (start us, length us, event | category | flops | bytes accessed | tf_op | source)
XLA Modules:
  0.0 53.4 jit_solution(3060839951429354664)
XLA Ops:
  1.3 1.4 %pack_rows.1 = (s32[1]{0:T(128)S(4)}, s32[4]{0:T(128)S(4)}, s32[4]{0:T(128)S(4)}, bf16[8,4,128]{2,1,0:T(4,128)(2,1)S(1)}, f32[2,68,8,128]{3,2,1,0:T(8,128)S(1)},...) custom-call(s32[1]{0:T(128)S(6)} %copy.29.counts_in, ...), custom_call_target="tpu_custom_call" | custom-call | tf_op jit(solution)/shard_map/pack_rows/pallas_call | solution.py:611
  2.6 1.9 %collective-permute-start = (f32[4,64,128]{2,1,0:T(8,128)S(1)}, f32[4,64,128]{2,1,0:T(8,128)S(1)}, u32[]{:S(2)}, u32[]{:S(2)}) collective-permute-start(f32[4,64,128]{2,1,0:T(8,128)S(1)} %get-tuple-element.37), channel_id=1, source_target_pairs={{0,1},{1,0},{2,3},{3,2},{4,5},{5,4},{6,7},{7,6},{8,9},{9,8},{10,11... | collective-permute-start | bytes 393224 | tf_op jit(solution)/shard_map/ppermute | solution.py:584
  4.6 1.9 %collective-permute-start.1 = (f32[4,64,128]{2,1,0:T(8,128)S(1)}, f32[4,64,128]{2,1,0:T(8,128)S(1)}, u32[]{:S(2)}, u32[]{:S(2)}) collective-permute-start(f32[4,64,128]{2,1,0:T(8,128)S(1)} %get-tuple-element.38), channel_id=1, source_target_pairs={{1,2},{2,1},{3,4},{4,3},{5,6},{6,5},{7,8},{8,7},{9,10},{10,9},{11,... | collective-permute-start | bytes 393224 | tf_op jit(solution)/shard_map/ppermute | solution.py:584
  6.5 3.4 %collective-permute-start.2 = (f32[2,3,8,128]{3,2,1,0:T(8,128)S(1)}, f32[2,3,8,128]{3,2,1,0:T(8,128)S(1)}, u32[]{:S(2)}, u32[]{:S(2)}) collective-permute-start(f32[2,3,8,128]{3,2,1,0:T(8,128)S(1)} %get-tuple-element.44), channel_id=1, source_target_pairs={{0,16},{16,0},{32,48},{48,32},{64,80},{80,64},{96,112},{112,96},{1... | collective-permute-start | bytes 73736 | tf_op jit(solution)/shard_map/ppermute | solution.py:584
  9.9 0.0 collective-permute-done.rows_pair
  9.9 2.2 %collective-permute-done.1.rows_gap = f32[4,64,128]{2,1,0:T(8,128)S(1)} collective-permute-done((f32[4,64,128]{2,1,0:T(8,128)S(1)}, f32[4,64,128]{2,1,0:T(8,128)S(1)}, u32[]{:S(2)}, u32[]{:S(2)}) %collective-permute-start.1) | collective-permute-done | bytes 131104 | tf_op jit(solution)/shard_map/ppermute | solution.py:584
  12.1 1.6 %early_step.1 = (f32[2,66,8,128]{3,2,1,0:T(8,128)S(1)}, f32[2,4,80,128]{3,2,1,0:T(8,128)S(1)}, f32[2,2,64,128]{3,2,1,0:T(8,128)S(1)}, f32[16,8,128]{2,1,0:T(8,12...) custom-call(s32[1]{0:T(128)S(4)} %get-tuple-element.31.counts, ...), custom_call_target="tpu_custom_call" | custom-call | flops 10000000 | bytes 1000000 | tf_op jit(solution)/shard_map/early_step/pallas_call | solution.py:645
  13.7 0.0 collective-permute-done.2.rim_pair
  13.7 0.7 %collective-permute-start.3 = (f32[2,3,8,128]{3,2,1,0:T(8,128)S(1)}, f32[2,3,8,128]{3,2,1,0:T(8,128)S(1)}, u32[]{:S(2)}, u32[]{:S(2)}) collective-permute-start(f32[2,3,8,128]{3,2,1,0:T(8,128)S(1)} %pack_gap.1.order), channel_id=1, source_target_pairs={{16,32},{32,16},{48,64},{64,48},{80,96},{96,80},{112,128},{128,112... | collective-permute-start | bytes 73736 | tf_op jit(solution)/shard_map/ppermute | solution.py:584
  14.4 1.3 %middle_step.2 = (f32[64,8,128]{2,1,0:T(8,128)S(1)}, f32[64,8,128]{2,1,0:T(8,128)S(1)}, f32[16,8,128]{2,1,0:T(8,128)S(1)}) custom-call(s32[1]{0:T(128)S(4)} %get-tuple-element.31.counts, f32[2,66,8,128]{3,2,1,0:T(8,128)S(1)} %get-tuple-element.39.field1.field1_in, ...), custom_call_target="tpu_custom_call", output_to_operand_aliasing={{0}: (6, {}), {1}: (7, {})} | custom-call | flops 10000000 | bytes 1000000 | tf_op jit(solution)/shard_map/middle_step/pallas_call | solution.py:671
  15.7 0.0 collective-permute-done.3.rim_gap
  15.8 7.1 %collective-permute-start.4 = (f32[2,2,8,128]{3,2,1,0:T(8,128)S(1)}, f32[2,2,8,128]{3,2,1,0:T(8,128)S(1)}, u32[]{:S(2)}, u32[]{:S(2)}) collective-permute-start(f32[2,2,8,128]{3,2,1,0:T(8,128)S(1)} %pack_next.1.order), channel_id=1, source_target_pairs={{0,16},{16,0},{32,48},{48,32},{64,80},{80,64},{96,112},{112,96},{1... | collective-permute-start | bytes 49160 | tf_op jit(solution)/shard_map/ppermute | solution.py:584
  22.9 1.8 %middle_step.3 = (f32[64,8,128]{2,1,0:T(8,128)}, f32[64,8,128]{2,1,0:T(8,128)}, f32[64,8,128]{2,1,0:T(8,128)S(1)}, f32[64,8,128]{2,1,0:T(8,128)S(1)}, f32[16,8,128]{2,1,0:T(8,128)S(1)}) custom-call(s32[1]{0:T(128)S(4)} %get-tuple-element.31.counts, ...), custom_call_target="tpu_custom_call", output_to_operand_aliasing={{2}: (6, {}), {3}: (7, {})} | custom-call | flops 10000000 | bytes 1000000 | tf_op jit(solution)/shard_map/middle_step/pallas_call | solution.py:671
  24.6 0.0 collective-permute-done.4.next_pair
  24.6 0.7 %late_step.1 = (f32[128,128]{1,0:T(8,128)S(1)}, f32[2,4,8,128]{3,2,1,0:T(8,128)S(1)}, f32[2,68,8,128]{3,2,1,0:T(8,128)S(1)}, f32[2,66,8,128]{3,2,1,0:T(8,128)S(1...) custom-call(s32[1]{0:T(128)S(4)} %get-tuple-element.31.counts, ...), custom_call_target="tpu_custom_call", output_to_operand_aliasing={{2}: (2, {}), {3}: (3, {}), {4}: (4, {}), {5}: (5, {})} | custom-call | flops 1000000 | bytes 1000000 | tf_op jit(solution)/shard_map/late_step/pallas_call | solution.py:687
  25.4 27.2 %all_to_all.11 = f32[64,2,128]{2,1,0:T(2,128)S(1)} all-to-all(f32[64,2,128]{2,1,0:T(2,128)S(1)} %bitcast.3), channel_id=1, replica_groups=mesh['depth'=64,'lat'=16] {'depth'}, dimensions={0} | all-to-all | bytes 131072 | tf_op jit(solution)/shard_map/all_to_all | solution.py:765
  52.5 0.9 %composite.1 = (f32[4,4,1,16]{3,2,1,0:T(1,128)}, f32[64,8,128]{2,1,0:T(8,128)}, f32[64,8,128]{2,1,0:T(8,128)}) custom-call(s32[1]{0:T(128)S(4)} %get-tuple-element.31.counts, s32[4]{0:T(128)S(4)} %get-tuple-element.32.camera, f32[128,128]{1,0:T(8,128)S(1)} %bitcast.2, ...), custom_call_target="tpu_custom_call", output_to_operand_aliasing={{1}: (4, {}), {2}: (5, {})} | custom-call | tf_op jit(solution)/shard_map/composite/pallas_call | solution.py:704
  (2 shorter events, 0.0 us)
Async XLA Ops:
  2.6 7.3 %collective-permute-start = (f32[4,64,128]{2,1,0:T(8,128)S(1)}, f32[4,64,128]{2,1,0:T(8,128)S(1)}, u32[]{:S(2)}, u32[]{:S(2)}) collective-permute-start(f32[4,64,128]{2,1,0:T(8,128)S(1)} %get-tuple-element.37), channel_id=1, source_target_pairs={{0,1},{1,0},{2,3},{3,2},{4,5},{5,4},{6,7},{7,6},{8,9},{9,8},{10,11... | collective-permute-start | bytes 393224 | tf_op jit(solution)/shard_map/ppermute | solution.py:584
  4.6 7.5 %collective-permute-start.1 = (f32[4,64,128]{2,1,0:T(8,128)S(1)}, f32[4,64,128]{2,1,0:T(8,128)S(1)}, u32[]{:S(2)}, u32[]{:S(2)}) collective-permute-start(f32[4,64,128]{2,1,0:T(8,128)S(1)} %get-tuple-element.38), channel_id=1, source_target_pairs={{1,2},{2,1},{3,4},{4,3},{5,6},{6,5},{7,8},{8,7},{9,10},{10,9},{11,... | collective-permute-start | bytes 393224 | tf_op jit(solution)/shard_map/ppermute | solution.py:584
  6.5 7.2 %collective-permute-start.2 = (f32[2,3,8,128]{3,2,1,0:T(8,128)S(1)}, f32[2,3,8,128]{3,2,1,0:T(8,128)S(1)}, u32[]{:S(2)}, u32[]{:S(2)}) collective-permute-start(f32[2,3,8,128]{3,2,1,0:T(8,128)S(1)} %get-tuple-element.44), channel_id=1, source_target_pairs={{0,16},{16,0},{32,48},{48,32},{64,80},{80,64},{96,112},{112,96},{1... | collective-permute-start | bytes 73736 | tf_op jit(solution)/shard_map/ppermute | solution.py:584
  13.7 2.0 %collective-permute-start.3 = (f32[2,3,8,128]{3,2,1,0:T(8,128)S(1)}, f32[2,3,8,128]{3,2,1,0:T(8,128)S(1)}, u32[]{:S(2)}, u32[]{:S(2)}) collective-permute-start(f32[2,3,8,128]{3,2,1,0:T(8,128)S(1)} %pack_gap.1.order), channel_id=1, source_target_pairs={{16,32},{32,16},{48,64},{64,48},{80,96},{96,80},{112,128},{128,112... | collective-permute-start | bytes 73736 | tf_op jit(solution)/shard_map/ppermute | solution.py:584
  15.8 8.9 %collective-permute-start.4 = (f32[2,2,8,128]{3,2,1,0:T(8,128)S(1)}, f32[2,2,8,128]{3,2,1,0:T(8,128)S(1)}, u32[]{:S(2)}, u32[]{:S(2)}) collective-permute-start(f32[2,2,8,128]{3,2,1,0:T(8,128)S(1)} %pack_next.1.order), channel_id=1, source_target_pairs={{0,16},{16,0},{32,48},{48,32},{64,80},{80,64},{96,112},{112,96},{1... | collective-permute-start | bytes 49160 | tf_op jit(solution)/shard_map/ppermute | solution.py:584

commit v7 on v6

--- a/solution.py
+++ b/solution.py
@@ -53,8 +53,8 @@
     library,
     field0,
     own_rows,
+    rows_gap,
     rows_pair,
-    rows_gap,
     rim_pair,
     copies,
 ):
@@ -97,7 +97,7 @@
         copy.wait()
 
 
-def beside(rows_pair, rows_gap, number, place):
+def beside(rows_gap, rows_pair, number, place):
     lat_even = is_even("lat")
     below = [ref[2 * number + 1, pl.ds(place, 1), :] for ref in (rows_gap, rows_pair)]
     above = [ref[2 * number, pl.ds(place, 1), :] for ref in (rows_pair, rows_gap)]
@@ -105,7 +105,7 @@
     return tuple(jnp.broadcast_to(x, (8, 128)) for x in rows)
 
 
-def pack_gap(counts, field0, rows_pair, rows_gap, rim_pair, order, rim_gap):
+def pack_gap(counts, field0, rows_gap, rows_pair, rim_pair, order, rim_gap):
     depth_count = counts[0]
     depth_even = is_even("depth")
     end = jnp.where(depth_even, 0, depth_count - 1)
@@ -117,15 +117,15 @@
         rim_gap[number, 1] = select(
             depth_count == 1, rim_pair[number, 0], field0[number, 2 + inward]
         )
-        below, above = beside(rows_pair, rows_gap, number, end)
+        below, above = beside(rows_gap, rows_pair, number, end)
         rim_gap[number, 2] = jnp.where(row == 0, below, jnp.where(row == 1, above, size))
 
 
-def pack_next(counts, rows_pair, rows_gap, rim_gap, order, next_pair):
+def pack_next(counts, rows_gap, rows_pair, rim_gap, order, next_pair):
     end = jnp.where(is_even("depth"), counts[0] - 1, 0)
     for number in range(2):
         next_pair[number, 0] = rim_gap[number, 0]
-        below, above = beside(rows_pair, rows_gap, number, end)
+        below, above = beside(rows_gap, rows_pair, number, end)
         next_pair[number, 1] = jnp.where(sublanes() == 0, below, above)
 
 
@@ -283,8 +283,8 @@
     field0,
     library,
     own_rows,
+    rows_gap,
     rows_pair,
-    rows_gap,
     field1,
     edge0,
     edge1,
@@ -730,18 +730,18 @@
         reactant_fraction,
         colour_lookup_library,
     )
-    rows_pair = swapped(messages[0], "lat", 0)
-    rows_gap = swapped(messages[1], "lat", 1)
+    rows_gap = swapped(messages[0], "lat", 1)
+    rows_pair = swapped(messages[1], "lat", 0)
     rim_pair = swapped(messages[2], "depth", 0)
     field1, edge0, edge1, low_table, rise_table, theta_next, fuel_next, sums = early_kernel(
-        devices, counts, choice, camera, field0, library, own_rows, rows_pair, rows_gap
-    )
-    order = rim_kernel(pack_gap, 3, counts, field0, rows_pair, rows_gap, rim_pair, sums)
+        devices, counts, choice, camera, field0, library, own_rows, rows_gap, rows_pair
+    )
+    order = rim_kernel(pack_gap, 3, counts, field0, rows_gap, rows_pair, rim_pair, sums)
     rim_gap = swapped(order, "depth", 1)
     theta_next, fuel_next, sums = middle_kernel(
         1, counts, field1, edge1, low_table, rise_table, order, theta_next, fuel_next, sums
     )
-    order = rim_kernel(pack_next, 2, counts, rows_pair, rows_gap, rim_gap, sums)
+    order = rim_kernel(pack_next, 2, counts, rows_gap, rows_pair, rim_gap, sums)
     next_pair = swapped(order, "depth", 0)
     theta_next, fuel_next, _, _, sums = middle_kernel(
         2, counts, field1, edge1, low_table, rise_table, order, theta_next, fuel_next, sums

time: 53.6 us -> 56.8 us (1.060)
  the two profiles are of different devices: /device:TPU:512 before, /device:TPU:384 now
where the time goes in v7:
time: 56.8 us; the launch traced here: 56.5 us
  blocking collectives  27.2 us (48%)
  starting transfers between devices  19.6 us (35%)
  Pallas kernels  7.65 us (13%)
  between operations  1.39 us (2%)
  waiting for transfers between devices  0.69 us (1%)
    all_to_all x1, blocking collectives, on_device(): pieces = lax.all_to_all(pieces, 'depth', 0, 0, tiled=True)  27.2 us
    ppermute x5, starting transfers between devices, swapped(): return lax.ppermute(array, axis, pairs)  19.6 us
    pallas_call x2, Pallas kernels, middle_kernel(): pl.pallas_call(functools.partial(middle_step, theta_next.shape[0], window...  3.08 us
    pallas_call x1, Pallas kernels, early_kernel(): pl.pallas_call(functools.partial(early_step, places, functions, float(MEA...  1.61 us
    pallas_call x1, Pallas kernels, first_kernel(): pl.pallas_call(pack_rows, out_shape=tuple((SMEM(x.shape, jnp.int32) for x...  1.35 us
  transfers between devices with their start and end apart: 5, of which 1 were waited for; matrix products, arithmetic and copies ran while one was open for 0% of the time, Pallas kernels for 8%

profile of v7, /device:TPU:384, one launch (start us, length us, event | category | flops | bytes accessed | tf_op | source)
XLA Modules:
  0.0 56.5 jit_solution(11002605832637936157)
XLA Ops:
  1.3 1.4 %pack_rows.1 = (s32[1]{0:T(128)S(4)}, s32[4]{0:T(128)S(4)}, s32[4]{0:T(128)S(4)}, bf16[8,4,128]{2,1,0:T(4,128)(2,1)S(1)}, f32[2,68,8,128]{3,2,1,0:T(8,128)S(1)},...) custom-call(s32[1]{0:T(128)S(6)} %copy.29.counts_in, ...), custom_call_target="tpu_custom_call" | custom-call | tf_op jit(solution)/shard_map/pack_rows/pallas_call | solution.py:611
  2.6 1.9 %collective-permute-start = (f32[4,64,128]{2,1,0:T(8,128)S(1)}, f32[4,64,128]{2,1,0:T(8,128)S(1)}, u32[]{:S(2)}, u32[]{:S(2)}) collective-permute-start(f32[4,64,128]{2,1,0:T(8,128)S(1)} %get-tuple-element.37), channel_id=1, source_target_pairs={{1,2},{2,1},{3,4},{4,3},{5,6},{6,5},{7,8},{8,7},{9,10},{10,9},{11,... | collective-permute-start | bytes 393224 | tf_op jit(solution)/shard_map/ppermute | solution.py:584
  4.6 6.5 %collective-permute-start.1 = (f32[4,64,128]{2,1,0:T(8,128)S(1)}, f32[4,64,128]{2,1,0:T(8,128)S(1)}, u32[]{:S(2)}, u32[]{:S(2)}) collective-permute-start(f32[4,64,128]{2,1,0:T(8,128)S(1)} %get-tuple-element.38), channel_id=1, source_target_pairs={{0,1},{1,0},{2,3},{3,2},{4,5},{5,4},{6,7},{7,6},{8,9},{9,8},{10,11... | collective-permute-start | bytes 393224 | tf_op jit(solution)/shard_map/ppermute | solution.py:584
  11.1 3.4 %collective-permute-start.2 = (f32[2,3,8,128]{3,2,1,0:T(8,128)S(1)}, f32[2,3,8,128]{3,2,1,0:T(8,128)S(1)}, u32[]{:S(2)}, u32[]{:S(2)}) collective-permute-start(f32[2,3,8,128]{3,2,1,0:T(8,128)S(1)} %get-tuple-element.44), channel_id=1, source_target_pairs={{0,16},{16,0},{32,48},{48,32},{64,80},{80,64},{96,112},{112,96},{1... | collective-permute-start | bytes 73736 | tf_op jit(solution)/shard_map/ppermute | solution.py:584
  14.5 0.0 collective-permute-done.rows_gap
  14.5 0.0 collective-permute-done.1.rows_pair
  14.5 1.6 %early_step.1 = (f32[2,66,8,128]{3,2,1,0:T(8,128)S(1)}, f32[2,4,80,128]{3,2,1,0:T(8,128)S(1)}, f32[2,2,64,128]{3,2,1,0:T(8,128)S(1)}, f32[16,8,128]{2,1,0:T(8,12...) custom-call(s32[1]{0:T(128)S(4)} %get-tuple-element.31.counts, ...), custom_call_target="tpu_custom_call" | custom-call | flops 10000000 | bytes 1000000 | tf_op jit(solution)/shard_map/early_step/pallas_call | solution.py:645
  16.1 0.7 %collective-permute-done.2.rim_pair = f32[2,3,8,128]{3,2,1,0:T(8,128)S(1)} collective-permute-done((f32[2,3,8,128]{3,2,1,0:T(8,128)S(1)}, f32[2,3,8,128]{3,2,1,0:T(8,128)S(1)}, u32[]{:S(2)}, u32[]{:S(2)}) %collective-permute-start.2) | collective-permute-done | bytes 24608 | tf_op jit(solution)/shard_map/ppermute | solution.py:584
  16.8 0.7 %collective-permute-start.3 = (f32[2,3,8,128]{3,2,1,0:T(8,128)S(1)}, f32[2,3,8,128]{3,2,1,0:T(8,128)S(1)}, u32[]{:S(2)}, u32[]{:S(2)}) collective-permute-start(f32[2,3,8,128]{3,2,1,0:T(8,128)S(1)} %pack_gap.1.order), channel_id=1, source_target_pairs={{16,32},{32,16},{48,64},{64,48},{80,96},{96,80},{112,128},{128,112... | collective-permute-start | bytes 73736 | tf_op jit(solution)/shard_map/ppermute | solution.py:584
  17.5 1.3 %middle_step.2 = (f32[64,8,128]{2,1,0:T(8,128)S(1)}, f32[64,8,128]{2,1,0:T(8,128)S(1)}, f32[16,8,128]{2,1,0:T(8,128)S(1)}) custom-call(s32[1]{0:T(128)S(4)} %get-tuple-element.31.counts, f32[2,66,8,128]{3,2,1,0:T(8,128)S(1)} %get-tuple-element.39.field1.field1_in, ...), custom_call_target="tpu_custom_call", output_to_operand_aliasing={{0}: (6, {}), {1}: (7, {})} | custom-call | flops 10000000 | bytes 1000000 | tf_op jit(solution)/shard_map/middle_step/pallas_call | solution.py:671
  18.8 0.0 collective-permute-done.3.rim_gap
  18.9 7.1 %collective-permute-start.4 = (f32[2,2,8,128]{3,2,1,0:T(8,128)S(1)}, f32[2,2,8,128]{3,2,1,0:T(8,128)S(1)}, u32[]{:S(2)}, u32[]{:S(2)}) collective-permute-start(f32[2,2,8,128]{3,2,1,0:T(8,128)S(1)} %pack_next.1.order), channel_id=1, source_target_pairs={{0,16},{16,0},{32,48},{48,32},{64,80},{80,64},{96,112},{112,96},{1... | collective-permute-start | bytes 49160 | tf_op jit(solution)/shard_map/ppermute | solution.py:584
  26.0 1.8 %middle_step.3 = (f32[64,8,128]{2,1,0:T(8,128)}, f32[64,8,128]{2,1,0:T(8,128)}, f32[64,8,128]{2,1,0:T(8,128)S(1)}, f32[64,8,128]{2,1,0:T(8,128)S(1)}, f32[16,8,128]{2,1,0:T(8,128)S(1)}) custom-call(s32[1]{0:T(128)S(4)} %get-tuple-element.31.counts, ...), custom_call_target="tpu_custom_call", output_to_operand_aliasing={{2}: (6, {}), {3}: (7, {})} | custom-call | flops 10000000 | bytes 1000000 | tf_op jit(solution)/shard_map/middle_step/pallas_call | solution.py:671
  27.7 0.0 collective-permute-done.4.next_pair
  27.7 0.7 %late_step.1 = (f32[128,128]{1,0:T(8,128)S(1)}, f32[2,4,8,128]{3,2,1,0:T(8,128)S(1)}, f32[2,68,8,128]{3,2,1,0:T(8,128)S(1)}, f32[2,66,8,128]{3,2,1,0:T(8,128)S(1...) custom-call(s32[1]{0:T(128)S(4)} %get-tuple-element.31.counts, ...), custom_call_target="tpu_custom_call", output_to_operand_aliasing={{2}: (2, {}), {3}: (3, {}), {4}: (4, {}), {5}: (5, {})} | custom-call | flops 1000000 | bytes 1000000 | tf_op jit(solution)/shard_map/late_step/pallas_call | solution.py:687
  28.4 27.2 %all_to_all.11 = f32[64,2,128]{2,1,0:T(2,128)S(1)} all-to-all(f32[64,2,128]{2,1,0:T(2,128)S(1)} %bitcast.3), channel_id=1, replica_groups=mesh['depth'=64,'lat'=16] {'depth'}, dimensions={0} | all-to-all | bytes 131072 | tf_op jit(solution)/shard_map/all_to_all | solution.py:765
  55.6 0.9 %composite.1 = (f32[4,4,1,16]{3,2,1,0:T(1,128)}, f32[64,8,128]{2,1,0:T(8,128)}, f32[64,8,128]{2,1,0:T(8,128)}) custom-call(s32[1]{0:T(128)S(4)} %get-tuple-element.31.counts, s32[4]{0:T(128)S(4)} %get-tuple-element.32.camera, f32[128,128]{1,0:T(8,128)S(1)} %bitcast.2, ...), custom_call_target="tpu_custom_call", output_to_operand_aliasing={{1}: (4, {}), {2}: (5, {})} | custom-call | tf_op jit(solution)/shard_map/composite/pallas_call | solution.py:704
  (2 shorter events, 0.0 us)
Async XLA Ops:
  2.6 11.8 %collective-permute-start = (f32[4,64,128]{2,1,0:T(8,128)S(1)}, f32[4,64,128]{2,1,0:T(8,128)S(1)}, u32[]{:S(2)}, u32[]{:S(2)}) collective-permute-start(f32[4,64,128]{2,1,0:T(8,128)S(1)} %get-tuple-element.37), channel_id=1, source_target_pairs={{1,2},{2,1},{3,4},{4,3},{5,6},{6,5},{7,8},{8,7},{9,10},{10,9},{11,... | collective-permute-start | bytes 393224 | tf_op jit(solution)/shard_map/ppermute | solution.py:584
  4.6 9.9 %collective-permute-start.1 = (f32[4,64,128]{2,1,0:T(8,128)S(1)}, f32[4,64,128]{2,1,0:T(8,128)S(1)}, u32[]{:S(2)}, u32[]{:S(2)}) collective-permute-start(f32[4,64,128]{2,1,0:T(8,128)S(1)} %get-tuple-element.38), channel_id=1, source_target_pairs={{0,1},{1,0},{2,3},{3,2},{4,5},{5,4},{6,7},{7,6},{8,9},{9,8},{10,11... | collective-permute-start | bytes 393224 | tf_op jit(solution)/shard_map/ppermute | solution.py:584
  11.1 5.7 %collective-permute-start.2 = (f32[2,3,8,128]{3,2,1,0:T(8,128)S(1)}, f32[2,3,8,128]{3,2,1,0:T(8,128)S(1)}, u32[]{:S(2)}, u32[]{:S(2)}) collective-permute-start(f32[2,3,8,128]{3,2,1,0:T(8,128)S(1)} %get-tuple-element.44), channel_id=1, source_target_pairs={{0,16},{16,0},{32,48},{48,32},{64,80},{80,64},{96,112},{112,96},{1... | collective-permute-start | bytes 73736 | tf_op jit(solution)/shard_map/ppermute | solution.py:584
  16.8 2.0 %collective-permute-start.3 = (f32[2,3,8,128]{3,2,1,0:T(8,128)S(1)}, f32[2,3,8,128]{3,2,1,0:T(8,128)S(1)}, u32[]{:S(2)}, u32[]{:S(2)}) collective-permute-start(f32[2,3,8,128]{3,2,1,0:T(8,128)S(1)} %pack_gap.1.order), channel_id=1, source_target_pairs={{16,32},{32,16},{48,64},{64,48},{80,96},{96,80},{112,128},{128,112... | collective-permute-start | bytes 73736 | tf_op jit(solution)/shard_map/ppermute | solution.py:584
  18.9 8.9 %collective-permute-start.4 = (f32[2,2,8,128]{3,2,1,0:T(8,128)S(1)}, f32[2,2,8,128]{3,2,1,0:T(8,128)S(1)}, u32[]{:S(2)}, u32[]{:S(2)}) collective-permute-start(f32[2,2,8,128]{3,2,1,0:T(8,128)S(1)} %pack_next.1.order), channel_id=1, source_target_pairs={{0,16},{16,0},{32,48},{48,32},{64,80},{80,64},{96,112},{112,96},{1... | collective-permute-start | bytes 49160 | tf_op jit(solution)/shard_map/ppermute | solution.py:584

commit v8 on v6

--- a/solution.py
+++ b/solution.py
@@ -29,7 +29,7 @@
 
 
 UNROLL_1 = 16
-WINDOWS = ((12, 12), (24, 12), (24, 12))
+WINDOWS = ((36, 12), (24, 12))
 
 
 def is_even(axis):
@@ -105,7 +105,7 @@
     return tuple(jnp.broadcast_to(x, (8, 128)) for x in rows)
 
 
-def pack_gap(counts, field0, rows_pair, rows_gap, rim_pair, order, rim_gap):
+def pack_gap(counts, field0, rows_pair, rows_gap, rim_pair, rim_gap):
     depth_count = counts[0]
     depth_even = is_even("depth")
     end = jnp.where(depth_even, 0, depth_count - 1)
@@ -285,6 +285,7 @@
     own_rows,
     rows_pair,
     rows_gap,
+    order,
     field1,
     edge0,
     edge1,
@@ -354,7 +355,6 @@
 
 def middle_step(
     places,
-    window,
     counts,
     field1,
     edge1,
@@ -364,14 +364,13 @@
     theta_in,
     fuel_in,
     sums_in,
-    *outs,
+    theta_out,
+    fuel_out,
+    theta_next,
+    fuel_next,
+    sums,
+    copies,
 ):
-    last = window == len(WINDOWS) - 1
-    if last:
-        theta_out, fuel_out, theta_next, fuel_next, sums, copies = outs
-    else:
-        theta_next, fuel_next, sums = outs
-
     def leave(number, first, count):
         return pltpu.make_async_copy(
             (theta_next, fuel_next)[number].at[pl.ds(first, count)],
@@ -383,26 +382,24 @@
         for number in range(2):
             leave(number, first, count).start()
 
-    first = 2 + sum(layers for layers, unroll in WINDOWS[:window])
-    if last:
-        start_leaving(0, first)
-        start_leaving(places - 2, 2)
+    first = 2 + WINDOWS[0][0]
+    start_leaving(0, first)
+    start_leaving(places - 2, 2)
     found = inner_layers(
         first,
-        *WINDOWS[window],
+        *WINDOWS[1],
         counts[0],
         field1,
         edge1,
         (low_table, rise_table),
         (theta_next, fuel_next),
         [sums_in[entry] for entry in range(sums_in.shape[0])],
-        start_leaving if last else None,
+        start_leaving,
     )
     for entry, value in enumerate(found):
         sums[entry] = value
-    if last:
-        for number in range(2):
-            leave(number, 0, places).wait()
+    for number in range(2):
+        leave(number, 0, places).wait()
 
 
 def late_step(
@@ -654,7 +651,7 @@
             field,
             VMEM((4 * functions, 8, 128), F32),
         ),
-        in_specs=[in_smem()] * 3 + [in_vmem()] * 5,
+        in_specs=[in_smem()] * 3 + [in_vmem()] * 6,
         out_specs=(in_vmem(),) * 8,
         scratch_shapes=[VMEM(library.shape, F32)],
         compiler_params=params(),
@@ -663,18 +660,16 @@
     )(*map(in_scalars, (counts, choice, camera)), *map(held, (field0, library, *rows)))
 
 
-def middle_kernel(window, counts, *arrays):
+def middle_kernel(counts, *arrays):
     theta_next, fuel_next, sums = arrays[-3:]
     field = jax.ShapeDtypeStruct(theta_next.shape, F32)
-    last = window == len(WINDOWS) - 1
-    lead = 2 if last else 0
     return pl.pallas_call(
-        functools.partial(middle_step, theta_next.shape[0], window),
-        out_shape=(field,) * lead + tuple(VMEM(x.shape, F32) for x in (theta_next, fuel_next, sums)),
+        functools.partial(middle_step, theta_next.shape[0]),
+        out_shape=(field, field) + tuple(VMEM(x.shape, F32) for x in (theta_next, fuel_next, sums)),
         in_specs=[in_smem()] + [in_vmem()] * len(arrays),
-        out_specs=(anywhere(),) * lead + (in_vmem(),) * 3,
-        scratch_shapes=[pltpu.SemaphoreType.DMA((2,))] if last else [],
-        input_output_aliases={len(arrays) - 2 + i: lead + i for i in range(2)},
+        out_specs=(anywhere(),) * 2 + (in_vmem(),) * 3,
+        scratch_shapes=[pltpu.SemaphoreType.DMA((2,))],
+        input_output_aliases={len(arrays) - 2 + i: 2 + i for i in range(2)},
         compiler_params=params(),
         cost_estimate=cost(10**7),
         name="middle_step",
@@ -733,18 +728,15 @@
     rows_pair = swapped(messages[0], "lat", 0)
     rows_gap = swapped(messages[1], "lat", 1)
     rim_pair = swapped(messages[2], "depth", 0)
+    order = rim_kernel(pack_gap, 3, counts, field0, rows_pair, rows_gap, rim_pair)
+    rim_gap = swapped(order, "depth", 1)
     field1, edge0, edge1, low_table, rise_table, theta_next, fuel_next, sums = early_kernel(
-        devices, counts, choice, camera, field0, library, own_rows, rows_pair, rows_gap
-    )
-    order = rim_kernel(pack_gap, 3, counts, field0, rows_pair, rows_gap, rim_pair, sums)
-    rim_gap = swapped(order, "depth", 1)
-    theta_next, fuel_next, sums = middle_kernel(
-        1, counts, field1, edge1, low_table, rise_table, order, theta_next, fuel_next, sums
+        devices, counts, choice, camera, field0, library, own_rows, rows_pair, rows_gap, order
     )
     order = rim_kernel(pack_next, 2, counts, rows_pair, rows_gap, rim_gap, sums)
     next_pair = swapped(order, "depth", 0)
     theta_next, fuel_next, _, _, sums = middle_kernel(
-        2, counts, field1, edge1, low_table, rise_table, order, theta_next, fuel_next, sums
+        counts, field1, edge1, low_table, rise_table, order, theta_next, fuel_next, sums
     )
     pieces, ends = late_kernel(
         devices,

time: 53.6 us -> 52.7 us (0.983)
  the two profiles are of different devices: /device:TPU:512 before, /device:TPU:385 now
where the time goes in v8:
time: 52.7 us; the launch traced here: 52 us
  blocking collectives  23.6 us (45%)
  starting transfers between devices  18 us (34%)
  Pallas kernels  7.64 us (14%)
  waiting for transfers between devices  1.45 us (3%)
  between operations  1.38 us (3%)
    all_to_all x1, blocking collectives, on_device(): pieces = lax.all_to_all(pieces, 'depth', 0, 0, tiled=True)  23.6 us
    ppermute x5, starting transfers between devices, swapped(): return lax.ppermute(array, axis, pairs)  18 us
    pallas_call x1, Pallas kernels, early_kernel(): pl.pallas_call(functools.partial(early_step, places, functions, float(MEA...  2.93 us
    pallas_call x1, Pallas kernels, middle_kernel(): pl.pallas_call(functools.partial(middle_step, theta_next.shape[0]), out_s...  1.75 us
    ppermute x5, waiting for transfers between devices, swapped(): return lax.ppermute(array, axis, pairs)  1.45 us
    pallas_call x1, Pallas kernels, first_kernel(): pl.pallas_call(pack_rows, out_shape=tuple((SMEM(x.shape, jnp.int32) for x...  1.34 us
  transfers between devices with their start and end apart: 5, of which 1 were waited for; matrix products, arithmetic and copies ran while one was open for 0% of the time, Pallas kernels for 9%

profile of v8, /device:TPU:385, one launch (start us, length us, event | category | flops | bytes accessed | tf_op | source)
XLA Modules:
  0.0 52.0 jit_solution(4586103945253921263)
XLA Ops:
  1.3 1.3 %pack_rows.1 = (s32[1]{0:T(128)S(4)}, s32[4]{0:T(128)S(4)}, s32[4]{0:T(128)S(4)}, bf16[8,4,128]{2,1,0:T(4,128)(2,1)S(1)}, f32[2,68,8,128]{3,2,1,0:T(8,128)S(1)},...) custom-call(s32[1]{0:T(128)S(6)} %copy.25.counts_in, ...), custom_call_target="tpu_custom_call" | custom-call | tf_op jit(solution)/shard_map/pack_rows/pallas_call | solution.py:608
  2.6 2.6 %collective-permute-start = (f32[4,64,128]{2,1,0:T(8,128)S(1)}, f32[4,64,128]{2,1,0:T(8,128)S(1)}, u32[]{:S(2)}, u32[]{:S(2)}) collective-permute-start(f32[4,64,128]{2,1,0:T(8,128)S(1)} %get-tuple-element.34), channel_id=1, source_target_pairs={{0,1},{1,0},{2,3},{3,2},{4,5},{5,4},{6,7},{7,6},{8,9},{9,8},{10,11... | collective-permute-start | bytes 393224 | tf_op jit(solution)/shard_map/ppermute | solution.py:581
  5.2 6.0 %collective-permute-start.1 = (f32[4,64,128]{2,1,0:T(8,128)S(1)}, f32[4,64,128]{2,1,0:T(8,128)S(1)}, u32[]{:S(2)}, u32[]{:S(2)}) collective-permute-start(f32[4,64,128]{2,1,0:T(8,128)S(1)} %get-tuple-element.35), channel_id=1, source_target_pairs={{1,2},{2,1},{3,4},{4,3},{5,6},{6,5},{7,8},{8,7},{9,10},{10,9},{11,... | collective-permute-start | bytes 393224 | tf_op jit(solution)/shard_map/ppermute | solution.py:581
  11.2 3.1 %collective-permute-start.2 = (f32[2,3,8,128]{3,2,1,0:T(8,128)S(1)}, f32[2,3,8,128]{3,2,1,0:T(8,128)S(1)}, u32[]{:S(2)}, u32[]{:S(2)}) collective-permute-start(f32[2,3,8,128]{3,2,1,0:T(8,128)S(1)} %get-tuple-element.36), channel_id=1, source_target_pairs={{0,16},{16,0},{32,48},{48,32},{64,80},{80,64},{96,112},{112,96},{1... | collective-permute-start | bytes 73736 | tf_op jit(solution)/shard_map/ppermute | solution.py:581
  14.4 1.4 %collective-permute-done.2.rim_pair = f32[2,3,8,128]{3,2,1,0:T(8,128)S(1)} collective-permute-done((f32[2,3,8,128]{3,2,1,0:T(8,128)S(1)}, f32[2,3,8,128]{3,2,1,0:T(8,128)S(1)}, u32[]{:S(2)}, u32[]{:S(2)}) %collective-permute-start.2) | collective-permute-done | bytes 24608 | tf_op jit(solution)/shard_map/ppermute | solution.py:581
  15.8 0.0 collective-permute-done.rows_pair
  15.8 0.0 collective-permute-done.1.rows_gap
  15.9 0.7 %collective-permute-start.3 = (f32[2,3,8,128]{3,2,1,0:T(8,128)S(1)}, f32[2,3,8,128]{3,2,1,0:T(8,128)S(1)}, u32[]{:S(2)}, u32[]{:S(2)}) collective-permute-start(f32[2,3,8,128]{3,2,1,0:T(8,128)S(1)} %pack_gap.1.order), channel_id=1, source_target_pairs={{16,32},{32,16},{48,64},{64,48},{80,96},{96,80},{112,128},{128,112... | collective-permute-start | bytes 73736 | tf_op jit(solution)/shard_map/ppermute | solution.py:581
  16.5 2.9 %early_step.1 = (f32[2,66,8,128]{3,2,1,0:T(8,128)S(1)}, f32[2,4,80,128]{3,2,1,0:T(8,128)S(1)}, f32[2,2,64,128]{3,2,1,0:T(8,128)S(1)}, f32[16,8,128]{2,1,0:T(8,12...) custom-call(s32[1]{0:T(128)S(4)} %get-tuple-element.28.counts, ...), custom_call_target="tpu_custom_call" | custom-call | flops 10000000 | bytes 1000000 | tf_op jit(solution)/shard_map/early_step/pallas_call | solution.py:642
  19.5 0.0 collective-permute-done.3.rim_gap
  19.5 5.6 %collective-permute-start.4 = (f32[2,2,8,128]{3,2,1,0:T(8,128)S(1)}, f32[2,2,8,128]{3,2,1,0:T(8,128)S(1)}, u32[]{:S(2)}, u32[]{:S(2)}) collective-permute-start(f32[2,2,8,128]{3,2,1,0:T(8,128)S(1)} %pack_next.1.order), channel_id=1, source_target_pairs={{0,16},{16,0},{32,48},{48,32},{64,80},{80,64},{96,112},{112,96},{1... | collective-permute-start | bytes 49160 | tf_op jit(solution)/shard_map/ppermute | solution.py:581
  25.1 1.8 %middle_step.1 = (f32[64,8,128]{2,1,0:T(8,128)}, f32[64,8,128]{2,1,0:T(8,128)}, f32[64,8,128]{2,1,0:T(8,128)S(1)}, f32[64,8,128]{2,1,0:T(8,128)S(1)}, f32[16,8,128]{2,1,0:T(8,128)S(1)}) custom-call(s32[1]{0:T(128)S(4)} %get-tuple-element.28.counts, ...), custom_call_target="tpu_custom_call", output_to_operand_aliasing={{2}: (6, {}), {3}: (7, {})} | custom-call | flops 10000000 | bytes 1000000 | tf_op jit(solution)/shard_map/middle_step/pallas_call | solution.py:666
  26.8 0.0 collective-permute-done.4.next_pair
  26.9 0.7 %late_step.1 = (f32[128,128]{1,0:T(8,128)S(1)}, f32[2,4,8,128]{3,2,1,0:T(8,128)S(1)}, f32[2,68,8,128]{3,2,1,0:T(8,128)S(1)}, f32[2,66,8,128]{3,2,1,0:T(8,128)S(1...) custom-call(s32[1]{0:T(128)S(4)} %get-tuple-element.28.counts, ...), custom_call_target="tpu_custom_call", output_to_operand_aliasing={{2}: (2, {}), {3}: (3, {}), {4}: (4, {}), {5}: (5, {})} | custom-call | flops 1000000 | bytes 1000000 | tf_op jit(solution)/shard_map/late_step/pallas_call | solution.py:682
  27.6 23.6 %all_to_all.11 = f32[64,2,128]{2,1,0:T(2,128)S(1)} all-to-all(f32[64,2,128]{2,1,0:T(2,128)S(1)} %bitcast.3), channel_id=1, replica_groups=mesh['depth'=64,'lat'=16] {'depth'}, dimensions={0} | all-to-all | bytes 131072 | tf_op jit(solution)/shard_map/all_to_all | solution.py:757
  51.2 0.9 %composite.1 = (f32[4,4,1,16]{3,2,1,0:T(1,128)}, f32[64,8,128]{2,1,0:T(8,128)}, f32[64,8,128]{2,1,0:T(8,128)}) custom-call(s32[1]{0:T(128)S(4)} %get-tuple-element.28.counts, s32[4]{0:T(128)S(4)} %get-tuple-element.29.camera, f32[128,128]{1,0:T(8,128)S(1)} %bitcast.2, ...), custom_call_target="tpu_custom_call", output_to_operand_aliasing={{1}: (4, {}), {2}: (5, {})} | custom-call | tf_op jit(solution)/shard_map/composite/pallas_call | solution.py:699
  (2 shorter events, 0.0 us)
Async XLA Ops:
  2.6 13.2 %collective-permute-start = (f32[4,64,128]{2,1,0:T(8,128)S(1)}, f32[4,64,128]{2,1,0:T(8,128)S(1)}, u32[]{:S(2)}, u32[]{:S(2)}) collective-permute-start(f32[4,64,128]{2,1,0:T(8,128)S(1)} %get-tuple-element.34), channel_id=1, source_target_pairs={{0,1},{1,0},{2,3},{3,2},{4,5},{5,4},{6,7},{7,6},{8,9},{9,8},{10,11... | collective-permute-start | bytes 393224 | tf_op jit(solution)/shard_map/ppermute | solution.py:581
  5.2 10.6 %collective-permute-start.1 = (f32[4,64,128]{2,1,0:T(8,128)S(1)}, f32[4,64,128]{2,1,0:T(8,128)S(1)}, u32[]{:S(2)}, u32[]{:S(2)}) collective-permute-start(f32[4,64,128]{2,1,0:T(8,128)S(1)} %get-tuple-element.35), channel_id=1, source_target_pairs={{1,2},{2,1},{3,4},{4,3},{5,6},{6,5},{7,8},{8,7},{9,10},{10,9},{11,... | collective-permute-start | bytes 393224 | tf_op jit(solution)/shard_map/ppermute | solution.py:581
  11.2 4.6 %collective-permute-start.2 = (f32[2,3,8,128]{3,2,1,0:T(8,128)S(1)}, f32[2,3,8,128]{3,2,1,0:T(8,128)S(1)}, u32[]{:S(2)}, u32[]{:S(2)}) collective-permute-start(f32[2,3,8,128]{3,2,1,0:T(8,128)S(1)} %get-tuple-element.36), channel_id=1, source_target_pairs={{0,16},{16,0},{32,48},{48,32},{64,80},{80,64},{96,112},{112,96},{1... | collective-permute-start | bytes 73736 | tf_op jit(solution)/shard_map/ppermute | solution.py:581
  15.9 3.6 %collective-permute-start.3 = (f32[2,3,8,128]{3,2,1,0:T(8,128)S(1)}, f32[2,3,8,128]{3,2,1,0:T(8,128)S(1)}, u32[]{:S(2)}, u32[]{:S(2)}) collective-permute-start(f32[2,3,8,128]{3,2,1,0:T(8,128)S(1)} %pack_gap.1.order), channel_id=1, source_target_pairs={{16,32},{32,16},{48,64},{64,48},{80,96},{96,80},{112,128},{128,112... | collective-permute-start | bytes 73736 | tf_op jit(solution)/shard_map/ppermute | solution.py:581
  19.5 7.3 %collective-permute-start.4 = (f32[2,2,8,128]{3,2,1,0:T(8,128)S(1)}, f32[2,2,8,128]{3,2,1,0:T(8,128)S(1)}, u32[]{:S(2)}, u32[]{:S(2)}) collective-permute-start(f32[2,2,8,128]{3,2,1,0:T(8,128)S(1)} %pack_next.1.order), channel_id=1, source_target_pairs={{0,16},{16,0},{32,48},{48,32},{64,80},{80,64},{96,112},{112,96},{1... | collective-permute-start | bytes 49160 | tf_op jit(solution)/shard_map/ppermute | solution.py:581

commit v9 on v8

--- a/solution.py
+++ b/solution.py
@@ -29,7 +29,7 @@
 
 
 UNROLL_1 = 16
-WINDOWS = ((36, 12), (24, 12))
+WINDOWS = ((20, 20), (40, 20))
 
 
 def is_even(axis):
@@ -84,49 +84,49 @@
             own_rows[2 * row + number] = (low, high)[row]
     fetch[0].wait()
     depth_count = counts[0]
-    last = depth_count + 1
-    second_last = jnp.maximum(depth_count, 2)
-    second = jnp.minimum(3, last)
-    size = jnp.broadcast_to(depth_count.astype(F32), (8, 128))
     for number in range(2):
-        up = (field0[number, last], field0[number, second_last], size)
-        down = (field0[number, 2], field0[number, second], size)
-        for layer in range(3):
-            rim_pair[number, layer] = select(depth_even, up[layer], down[layer])
+        rim_pair[number] = select(
+            depth_even, field0[number, depth_count + 1], field0[number, 2]
+        )
     for copy in fetch[3:]:
         copy.wait()
 
 
-def beside(rows_pair, rows_gap, number, place):
+def beside(rows_pair, rows_gap, place, rest):
     lat_even = is_even("lat")
-    below = [ref[2 * number + 1, pl.ds(place, 1), :] for ref in (rows_gap, rows_pair)]
-    above = [ref[2 * number, pl.ds(place, 1), :] for ref in (rows_pair, rows_gap)]
-    rows = (select(lat_even, *below), select(lat_even, *above))
-    return tuple(jnp.broadcast_to(x, (8, 128)) for x in rows)
+    row = sublanes()
+    out = jnp.broadcast_to(rest, (8, 128))
+    for number in range(2):
+        below = [ref[2 * number + 1, pl.ds(place, 1), :] for ref in (rows_gap, rows_pair)]
+        above = [ref[2 * number, pl.ds(place, 1), :] for ref in (rows_pair, rows_gap)]
+        for side, rows in enumerate((below, above)):
+            line = jnp.broadcast_to(select(lat_even, *rows), (8, 128))
+            out = jnp.where(row == 2 * number + side, line, out)
+    return out
+
+
+def end_places(upward, depth_count):
+    return (
+        jnp.where(upward, depth_count + 1, 2),
+        jnp.where(upward, jnp.maximum(depth_count, 2), 3),
+    )
 
 
 def pack_gap(counts, field0, rows_pair, rows_gap, rim_pair, rim_gap):
     depth_count = counts[0]
-    depth_even = is_even("depth")
-    end = jnp.where(depth_even, 0, depth_count - 1)
-    inward = jnp.where(depth_even, 1, jnp.maximum(depth_count - 2, 0))
-    size = depth_count.astype(F32)
-    row = sublanes()
+    end, inward = end_places(jnp.logical_not(is_even("depth")), depth_count)
     for number in range(2):
-        rim_gap[number, 0] = field0[number, 2 + end]
-        rim_gap[number, 1] = select(
-            depth_count == 1, rim_pair[number, 0], field0[number, 2 + inward]
-        )
-        below, above = beside(rows_pair, rows_gap, number, end)
-        rim_gap[number, 2] = jnp.where(row == 0, below, jnp.where(row == 1, above, size))
-
-
-def pack_next(counts, rows_pair, rows_gap, rim_gap, order, next_pair):
-    end = jnp.where(is_even("depth"), counts[0] - 1, 0)
+        rim_gap[number] = field0[number, end]
+        rim_gap[2 + number] = select(depth_count == 1, rim_pair[number], field0[number, inward])
+    rim_gap[4] = beside(rows_pair, rows_gap, end - 2, depth_count.astype(F32))
+
+
+def pack_next(counts, field0, rows_pair, rows_gap, rim_gap, order, next_pair):
+    depth_count = counts[0]
+    end, inward = end_places(is_even("depth"), depth_count)
     for number in range(2):
-        next_pair[number, 0] = rim_gap[number, 0]
-        below, above = beside(rows_pair, rows_gap, number, end)
-        next_pair[number, 1] = jnp.where(sublanes() == 0, below, above)
+        next_pair[number] = select(depth_count == 1, rim_gap[number], field0[number, inward])
+    next_pair[2] = beside(rows_pair, rows_gap, end - 2, 0.0)
 
 
 def lanes():
@@ -430,14 +430,14 @@
     def sides(pair, gap):
         return select(depth_even, gap, pair), select(depth_even, pair, gap)
 
-    pair_size = rim_pair[0, 2]
-    gap_size = jnp.broadcast_to(rim_gap[0, 2, 2:3], (8, 128))
-    below_size, above_size = sides(pair_size, gap_size)
+    gap_size = jnp.broadcast_to(rim_gap[4, 4:5], (8, 128))
+    below_size, above_size = sides(jnp.ones((8, 128), F32), gap_size)
     for number in range(2):
-        nearest = sides(rim_pair[number, 0], rim_gap[number, 0])
-        second = jnp.where(pair_size == 1.0, next_pair[number, 0], rim_pair[number, 1])
-        second = sides(second, rim_gap[number, 1])
-        rows = sides(next_pair[number, 1], rim_gap[number, 2])
+        nearest = sides(rim_pair[number], rim_gap[number])
+        second = sides(next_pair[number], rim_gap[2 + number])
+        rows = sides(
+            next_pair[2, 2 * number : 2 * number + 2], rim_gap[4, 2 * number : 2 * number + 2]
+        )
         field0[number, 0] = second[0]
         field0[number, 1] = nearest[0]
         field0[number, depth_count + 2] = nearest[1]
@@ -604,7 +604,7 @@
 def first_kernel(counts, choice, camera, theta, fuel, library):
     places = theta.shape[0]
     rows = VMEM((4, places, 128), F32)
-    rim = VMEM((2, 3, 8, 128), F32)
+    rim = VMEM((2, 8, 128), F32)
     return pl.pallas_call(
         pack_rows,
         out_shape=tuple(SMEM(x.shape, jnp.int32) for x in (counts, choice, camera))
@@ -621,7 +621,7 @@
 def rim_kernel(body, layers, counts, *arrays):
     return pl.pallas_call(
         body,
-        out_shape=VMEM((2, layers, 8, 128), F32),
+        out_shape=VMEM((layers, 8, 128), F32),
         in_specs=[in_smem()] + [in_vmem()] * len(arrays),
         out_specs=in_vmem(),
         compiler_params=params(),
@@ -728,12 +728,12 @@
     rows_pair = swapped(messages[0], "lat", 0)
     rows_gap = swapped(messages[1], "lat", 1)
     rim_pair = swapped(messages[2], "depth", 0)
-    order = rim_kernel(pack_gap, 3, counts, field0, rows_pair, rows_gap, rim_pair)
+    order = rim_kernel(pack_gap, 5, counts, field0, rows_pair, rows_gap, rim_pair)
     rim_gap = swapped(order, "depth", 1)
     field1, edge0, edge1, low_table, rise_table, theta_next, fuel_next, sums = early_kernel(
         devices, counts, choice, camera, field0, library, own_rows, rows_pair, rows_gap, order
     )
-    order = rim_kernel(pack_next, 2, counts, rows_pair, rows_gap, rim_gap, sums)
+    order = rim_kernel(pack_next, 3, counts, field0, rows_pair, rows_gap, rim_gap, sums)
     next_pair = swapped(order, "depth", 0)
     theta_next, fuel_next, _, _, sums = middle_kernel(
         counts, field1, edge1, low_table, rise_table, order, theta_next, fuel_next, sums

time: 52.7 us -> 52.6 us (level)
    pallas_call x1, Pallas kernels: 2.93 us -> 2.03 us  [early_kernel(): pl.pallas_call(functools.partial(early_step, places, functions, float(MEA...]
    pallas_call x1, Pallas kernels: 1.75 us -> 2.58 us  [middle_kernel(): pl.pallas_call(functools.partial(middle_step, theta_next.shape[0]), out_s...]
where the time goes in v9:
time: 52.6 us; the launch traced here: 52.3 us
  blocking collectives  24.1 us (46%)
  starting transfers between devices  18 us (34%)
  Pallas kernels  7.57 us (14%)
  between operations  1.38 us (3%)
  waiting for transfers between devices  1.28 us (2%)
    all_to_all x1, blocking collectives, on_device(): pieces = lax.all_to_all(pieces, 'depth', 0, 0, tiled=True)  24.1 us
    ppermute x5, starting transfers between devices, swapped(): return lax.ppermute(array, axis, pairs)  18 us
    pallas_call x1, Pallas kernels, middle_kernel(): pl.pallas_call(functools.partial(middle_step, theta_next.shape[0]), out_s...  2.58 us
    pallas_call x1, Pallas kernels, early_kernel(): pl.pallas_call(functools.partial(early_step, places, functions, float(MEA...  2.03 us
    pallas_call x1, Pallas kernels, first_kernel(): pl.pallas_call(pack_rows, out_shape=tuple((SMEM(x.shape, jnp.int32) for x...  1.35 us
    ppermute x5, waiting for transfers between devices, swapped(): return lax.ppermute(array, axis, pairs)  1.28 us
  transfers between devices with their start and end apart: 5, of which 1 were waited for; matrix products, arithmetic and copies ran while one was open for 0% of the time, Pallas kernels for 9%

profile of v9, /device:TPU:385, one launch (start us, length us, event | category | flops | bytes accessed | tf_op | source)
XLA Modules:
  0.0 52.3 jit_solution(5659032922458685780)
XLA Ops:
  1.3 1.3 %pack_rows.1 = (s32[1]{0:T(128)S(4)}, s32[4]{0:T(128)S(4)}, s32[4]{0:T(128)S(4)}, bf16[8,4,128]{2,1,0:T(4,128)(2,1)S(1)}, f32[2,68,8,128]{3,2,1,0:T(8,128)S(1)},...) custom-call(s32[1]{0:T(128)S(6)} %copy.25.counts_in, ...), custom_call_target="tpu_custom_call" | custom-call | tf_op jit(solution)/shard_map/pack_rows/pallas_call | solution.py:608
  2.6 2.6 %collective-permute-start = (f32[4,64,128]{2,1,0:T(8,128)S(1)}, f32[4,64,128]{2,1,0:T(8,128)S(1)}, u32[]{:S(2)}, u32[]{:S(2)}) collective-permute-start(f32[4,64,128]{2,1,0:T(8,128)S(1)} %get-tuple-element.34), channel_id=1, source_target_pairs={{0,1},{1,0},{2,3},{3,2},{4,5},{5,4},{6,7},{7,6},{8,9},{9,8},{10,11... | collective-permute-start | bytes 393224 | tf_op jit(solution)/shard_map/ppermute | solution.py:581
  5.2 6.0 %collective-permute-start.1 = (f32[4,64,128]{2,1,0:T(8,128)S(1)}, f32[4,64,128]{2,1,0:T(8,128)S(1)}, u32[]{:S(2)}, u32[]{:S(2)}) collective-permute-start(f32[4,64,128]{2,1,0:T(8,128)S(1)} %get-tuple-element.35), channel_id=1, source_target_pairs={{1,2},{2,1},{3,4},{4,3},{5,6},{6,5},{7,8},{8,7},{9,10},{10,9},{11,... | collective-permute-start | bytes 393224 | tf_op jit(solution)/shard_map/ppermute | solution.py:581
  11.2 3.1 %collective-permute-start.2 = (f32[2,8,128]{2,1,0:T(8,128)S(1)}, f32[2,8,128]{2,1,0:T(8,128)S(1)}, u32[]{:S(2)}, u32[]{:S(2)}) collective-permute-start(f32[2,8,128]{2,1,0:T(8,128)S(1)} %get-tuple-element.36), channel_id=1, source_target_pairs={{0,16},{16,0},{32,48},{48,32},{64,80},{80,64},{96,112},{112,96},{1... | collective-permute-start | bytes 24584 | tf_op jit(solution)/shard_map/ppermute | solution.py:581
  14.4 1.3 %collective-permute-done.2.rim_pair = f32[2,8,128]{2,1,0:T(8,128)S(1)} collective-permute-done((f32[2,8,128]{2,1,0:T(8,128)S(1)}, f32[2,8,128]{2,1,0:T(8,128)S(1)}, u32[]{:S(2)}, u32[]{:S(2)}) %collective-permute-start.2) | collective-permute-done | bytes 8224 | tf_op jit(solution)/shard_map/ppermute | solution.py:581
  15.6 0.0 collective-permute-done.rows_pair
  15.6 0.0 collective-permute-done.1.rows_gap
  15.7 0.7 %collective-permute-start.3 = (f32[5,8,128]{2,1,0:T(8,128)S(1)}, f32[5,8,128]{2,1,0:T(8,128)S(1)}, u32[]{:S(2)}, u32[]{:S(2)}) collective-permute-start(f32[5,8,128]{2,1,0:T(8,128)S(1)} %pack_gap.1.order), channel_id=1, source_target_pairs={{16,32},{32,16},{48,64},{64,48},{80,96},{96,80},{112,128},{128,112... | collective-permute-start | bytes 61448 | tf_op jit(solution)/shard_map/ppermute | solution.py:581
  16.3 2.0 %early_step.1 = (f32[2,66,8,128]{3,2,1,0:T(8,128)S(1)}, f32[2,4,80,128]{3,2,1,0:T(8,128)S(1)}, f32[2,2,64,128]{3,2,1,0:T(8,128)S(1)}, f32[16,8,128]{2,1,0:T(8,12...) custom-call(s32[1]{0:T(128)S(4)} %get-tuple-element.28.counts, ...), custom_call_target="tpu_custom_call" | custom-call | flops 10000000 | bytes 1000000 | tf_op jit(solution)/shard_map/early_step/pallas_call | solution.py:642
  18.4 0.0 collective-permute-done.3.rim_gap
  18.4 5.6 %collective-permute-start.4 = (f32[3,8,128]{2,1,0:T(8,128)S(1)}, f32[3,8,128]{2,1,0:T(8,128)S(1)}, u32[]{:S(2)}, u32[]{:S(2)}) collective-permute-start(f32[3,8,128]{2,1,0:T(8,128)S(1)} %pack_next.1.order), channel_id=1, source_target_pairs={{0,16},{16,0},{32,48},{48,32},{64,80},{80,64},{96,112},{112,96},{1... | collective-permute-start | bytes 36872 | tf_op jit(solution)/shard_map/ppermute | solution.py:581
  24.0 2.6 %middle_step.1 = (f32[64,8,128]{2,1,0:T(8,128)}, f32[64,8,128]{2,1,0:T(8,128)}, f32[64,8,128]{2,1,0:T(8,128)S(1)}, f32[64,8,128]{2,1,0:T(8,128)S(1)}, f32[16,8,128]{2,1,0:T(8,128)S(1)}) custom-call(s32[1]{0:T(128)S(4)} %get-tuple-element.28.counts, ...), custom_call_target="tpu_custom_call", output_to_operand_aliasing={{2}: (6, {}), {3}: (7, {})} | custom-call | flops 10000000 | bytes 1000000 | tf_op jit(solution)/shard_map/middle_step/pallas_call | solution.py:666
  26.6 0.0 collective-permute-done.4.next_pair
  26.6 0.7 %late_step.1 = (f32[128,128]{1,0:T(8,128)S(1)}, f32[2,4,8,128]{3,2,1,0:T(8,128)S(1)}, f32[2,68,8,128]{3,2,1,0:T(8,128)S(1)}, f32[2,66,8,128]{3,2,1,0:T(8,128)S(1...) custom-call(s32[1]{0:T(128)S(4)} %get-tuple-element.28.counts, ...), custom_call_target="tpu_custom_call", output_to_operand_aliasing={{2}: (2, {}), {3}: (3, {}), {4}: (4, {}), {5}: (5, {})} | custom-call | flops 1000000 | bytes 1000000 | tf_op jit(solution)/shard_map/late_step/pallas_call | solution.py:682
  27.3 24.1 %all_to_all.11 = f32[64,2,128]{2,1,0:T(2,128)S(1)} all-to-all(f32[64,2,128]{2,1,0:T(2,128)S(1)} %bitcast.3), channel_id=1, replica_groups=mesh['depth'=64,'lat'=16] {'depth'}, dimensions={0} | all-to-all | bytes 131072 | tf_op jit(solution)/shard_map/all_to_all | solution.py:757
  51.4 0.9 %composite.1 = (f32[4,4,1,16]{3,2,1,0:T(1,128)}, f32[64,8,128]{2,1,0:T(8,128)}, f32[64,8,128]{2,1,0:T(8,128)}) custom-call(s32[1]{0:T(128)S(4)} %get-tuple-element.28.counts, s32[4]{0:T(128)S(4)} %get-tuple-element.29.camera, f32[128,128]{1,0:T(8,128)S(1)} %bitcast.2, ...), custom_call_target="tpu_custom_call", output_to_operand_aliasing={{1}: (4, {}), {2}: (5, {})} | custom-call | tf_op jit(solution)/shard_map/composite/pallas_call | solution.py:699
  (2 shorter events, 0.0 us)
Async XLA Ops:
  2.6 13.0 %collective-permute-start = (f32[4,64,128]{2,1,0:T(8,128)S(1)}, f32[4,64,128]{2,1,0:T(8,128)S(1)}, u32[]{:S(2)}, u32[]{:S(2)}) collective-permute-start(f32[4,64,128]{2,1,0:T(8,128)S(1)} %get-tuple-element.34), channel_id=1, source_target_pairs={{0,1},{1,0},{2,3},{3,2},{4,5},{5,4},{6,7},{7,6},{8,9},{9,8},{10,11... | collective-permute-start | bytes 393224 | tf_op jit(solution)/shard_map/ppermute | solution.py:581
  5.2 10.4 %collective-permute-start.1 = (f32[4,64,128]{2,1,0:T(8,128)S(1)}, f32[4,64,128]{2,1,0:T(8,128)S(1)}, u32[]{:S(2)}, u32[]{:S(2)}) collective-permute-start(f32[4,64,128]{2,1,0:T(8,128)S(1)} %get-tuple-element.35), channel_id=1, source_target_pairs={{1,2},{2,1},{3,4},{4,3},{5,6},{6,5},{7,8},{8,7},{9,10},{10,9},{11,... | collective-permute-start | bytes 393224 | tf_op jit(solution)/shard_map/ppermute | solution.py:581
  11.2 4.4 %collective-permute-start.2 = (f32[2,8,128]{2,1,0:T(8,128)S(1)}, f32[2,8,128]{2,1,0:T(8,128)S(1)}, u32[]{:S(2)}, u32[]{:S(2)}) collective-permute-start(f32[2,8,128]{2,1,0:T(8,128)S(1)} %get-tuple-element.36), channel_id=1, source_target_pairs={{0,16},{16,0},{32,48},{48,32},{64,80},{80,64},{96,112},{112,96},{1... | collective-permute-start | bytes 24584 | tf_op jit(solution)/shard_map/ppermute | solution.py:581
  15.7 2.7 %collective-permute-start.3 = (f32[5,8,128]{2,1,0:T(8,128)S(1)}, f32[5,8,128]{2,1,0:T(8,128)S(1)}, u32[]{:S(2)}, u32[]{:S(2)}) collective-permute-start(f32[5,8,128]{2,1,0:T(8,128)S(1)} %pack_gap.1.order), channel_id=1, source_target_pairs={{16,32},{32,16},{48,64},{64,48},{80,96},{96,80},{112,128},{128,112... | collective-permute-start | bytes 61448 | tf_op jit(solution)/shard_map/ppermute | solution.py:581
  18.4 8.2 %collective-permute-start.4 = (f32[3,8,128]{2,1,0:T(8,128)S(1)}, f32[3,8,128]{2,1,0:T(8,128)S(1)}, u32[]{:S(2)}, u32[]{:S(2)}) collective-permute-start(f32[3,8,128]{2,1,0:T(8,128)S(1)} %pack_next.1.order), channel_id=1, source_target_pairs={{0,16},{16,0},{32,48},{48,32},{64,80},{80,64},{96,112},{112,96},{1... | collective-permute-start | bytes 36872 | tf_op jit(solution)/shard_map/ppermute | solution.py:581

commit v10 on v6

--- a/solution.py
+++ b/solution.py
@@ -29,7 +29,7 @@
 
 
 UNROLL_1 = 16
-WINDOWS = ((12, 12), (24, 12), (24, 12))
+WINDOWS = ((0, 12), (24, 12), (36, 12))
 
 
 def is_even(axis):

time: 53.6 us -> 53 us (0.989)
  blocking collectives: 27.2 us -> 26.5 us
    pallas_call x2, Pallas kernels: 3.08 us -> 3.74 us  [middle_kernel(): pl.pallas_call(functools.partial(middle_step, theta_next.shape[0], window...]
    pallas_call x1, Pallas kernels: 1.61 us -> 0.95 us  [early_kernel(): pl.pallas_call(functools.partial(early_step, places, functions, float(MEA...]
    all_to_all x1, blocking collectives: 27.2 us -> 26.5 us  [on_device(): pieces = lax.all_to_all(pieces, 'depth', 0, 0, tiled=True)]
where the time goes in v10:
time: 53 us; the launch traced here: 52.7 us
  blocking collectives  26.5 us (50%)
  starting transfers between devices  15 us (28%)
  Pallas kernels  7.65 us (14%)
  waiting for transfers between devices  2.16 us (4%)
  between operations  1.4 us (3%)
    all_to_all x1, blocking collectives, on_device(): pieces = lax.all_to_all(pieces, 'depth', 0, 0, tiled=True)  26.5 us
    ppermute x5, starting transfers between devices, swapped(): return lax.ppermute(array, axis, pairs)  15 us
    pallas_call x2, Pallas kernels, middle_kernel(): pl.pallas_call(functools.partial(middle_step, theta_next.shape[0], window...  3.74 us
    ppermute x5, waiting for transfers between devices, swapped(): return lax.ppermute(array, axis, pairs)  2.16 us
    pallas_call x1, Pallas kernels, first_kernel(): pl.pallas_call(pack_rows, out_shape=tuple((SMEM(x.shape, jnp.int32) for x...  1.35 us
  transfers between devices with their start and end apart: 5, of which 1 were waited for; matrix products, arithmetic and copies ran while one was open for 0% of the time, Pallas kernels for 9%

profile of v10, /device:TPU:512, one launch (start us, length us, event | category | flops | bytes accessed | tf_op | source)
XLA Modules:
  0.0 52.7 jit_solution(1592462566222986770)
XLA Ops:
  1.3 1.4 %pack_rows.1 = (s32[1]{0:T(128)S(4)}, s32[4]{0:T(128)S(4)}, s32[4]{0:T(128)S(4)}, bf16[8,4,128]{2,1,0:T(4,128)(2,1)S(1)}, f32[2,68,8,128]{3,2,1,0:T(8,128)S(1)},...) custom-call(s32[1]{0:T(128)S(6)} %copy.29.counts_in, ...), custom_call_target="tpu_custom_call" | custom-call | tf_op jit(solution)/shard_map/pack_rows/pallas_call | solution.py:611
  2.6 1.9 %collective-permute-start = (f32[4,64,128]{2,1,0:T(8,128)S(1)}, f32[4,64,128]{2,1,0:T(8,128)S(1)}, u32[]{:S(2)}, u32[]{:S(2)}) collective-permute-start(f32[4,64,128]{2,1,0:T(8,128)S(1)} %get-tuple-element.37), channel_id=1, source_target_pairs={{0,1},{1,0},{2,3},{3,2},{4,5},{5,4},{6,7},{7,6},{8,9},{9,8},{10,11... | collective-permute-start | bytes 393224 | tf_op jit(solution)/shard_map/ppermute | solution.py:584
  4.6 1.9 %collective-permute-start.1 = (f32[4,64,128]{2,1,0:T(8,128)S(1)}, f32[4,64,128]{2,1,0:T(8,128)S(1)}, u32[]{:S(2)}, u32[]{:S(2)}) collective-permute-start(f32[4,64,128]{2,1,0:T(8,128)S(1)} %get-tuple-element.38), channel_id=1, source_target_pairs={{1,2},{2,1},{3,4},{4,3},{5,6},{6,5},{7,8},{8,7},{9,10},{10,9},{11,... | collective-permute-start | bytes 393224 | tf_op jit(solution)/shard_map/ppermute | solution.py:584
  6.5 3.4 %collective-permute-start.2 = (f32[2,3,8,128]{3,2,1,0:T(8,128)S(1)}, f32[2,3,8,128]{3,2,1,0:T(8,128)S(1)}, u32[]{:S(2)}, u32[]{:S(2)}) collective-permute-start(f32[2,3,8,128]{3,2,1,0:T(8,128)S(1)} %get-tuple-element.44), channel_id=1, source_target_pairs={{0,16},{16,0},{32,48},{48,32},{64,80},{80,64},{96,112},{112,96},{1... | collective-permute-start | bytes 73736 | tf_op jit(solution)/shard_map/ppermute | solution.py:584
  9.9 0.0 collective-permute-done.rows_pair
  9.9 2.2 %collective-permute-done.1.rows_gap = f32[4,64,128]{2,1,0:T(8,128)S(1)} collective-permute-done((f32[4,64,128]{2,1,0:T(8,128)S(1)}, f32[4,64,128]{2,1,0:T(8,128)S(1)}, u32[]{:S(2)}, u32[]{:S(2)}) %collective-permute-start.1) | collective-permute-done | bytes 131104 | tf_op jit(solution)/shard_map/ppermute | solution.py:584
  12.1 0.9 %early_step.1 = (f32[2,66,8,128]{3,2,1,0:T(8,128)S(1)}, f32[2,4,80,128]{3,2,1,0:T(8,128)S(1)}, f32[2,2,64,128]{3,2,1,0:T(8,128)S(1)}, f32[16,8,128]{2,1,0:T(8,12...) custom-call(s32[1]{0:T(128)S(4)} %get-tuple-element.31.counts, ...), custom_call_target="tpu_custom_call" | custom-call | flops 10000000 | bytes 1000000 | tf_op jit(solution)/shard_map/early_step/pallas_call | solution.py:645
  13.0 0.0 collective-permute-done.2.rim_pair
  13.1 0.7 %collective-permute-start.3 = (f32[2,3,8,128]{3,2,1,0:T(8,128)S(1)}, f32[2,3,8,128]{3,2,1,0:T(8,128)S(1)}, u32[]{:S(2)}, u32[]{:S(2)}) collective-permute-start(f32[2,3,8,128]{3,2,1,0:T(8,128)S(1)} %pack_gap.1.order), channel_id=1, source_target_pairs={{16,32},{32,16},{48,64},{64,48},{80,96},{96,80},{112,128},{128,112... | collective-permute-start | bytes 73736 | tf_op jit(solution)/shard_map/ppermute | solution.py:584
  13.7 1.3 %middle_step.2 = (f32[64,8,128]{2,1,0:T(8,128)S(1)}, f32[64,8,128]{2,1,0:T(8,128)S(1)}, f32[16,8,128]{2,1,0:T(8,128)S(1)}) custom-call(s32[1]{0:T(128)S(4)} %get-tuple-element.31.counts, f32[2,66,8,128]{3,2,1,0:T(8,128)S(1)} %get-tuple-element.39.field1.field1_in, ...), custom_call_target="tpu_custom_call", output_to_operand_aliasing={{0}: (6, {}), {1}: (7, {})} | custom-call | flops 10000000 | bytes 1000000 | tf_op jit(solution)/shard_map/middle_step/pallas_call | solution.py:671
  15.1 0.0 collective-permute-done.3.rim_gap
  15.1 7.1 %collective-permute-start.4 = (f32[2,2,8,128]{3,2,1,0:T(8,128)S(1)}, f32[2,2,8,128]{3,2,1,0:T(8,128)S(1)}, u32[]{:S(2)}, u32[]{:S(2)}) collective-permute-start(f32[2,2,8,128]{3,2,1,0:T(8,128)S(1)} %pack_next.1.order), channel_id=1, source_target_pairs={{0,16},{16,0},{32,48},{48,32},{64,80},{80,64},{96,112},{112,96},{1... | collective-permute-start | bytes 49160 | tf_op jit(solution)/shard_map/ppermute | solution.py:584
  22.2 2.4 %middle_step.3 = (f32[64,8,128]{2,1,0:T(8,128)}, f32[64,8,128]{2,1,0:T(8,128)}, f32[64,8,128]{2,1,0:T(8,128)S(1)}, f32[64,8,128]{2,1,0:T(8,128)S(1)}, f32[16,8,128]{2,1,0:T(8,128)S(1)}) custom-call(s32[1]{0:T(128)S(4)} %get-tuple-element.31.counts, ...), custom_call_target="tpu_custom_call", output_to_operand_aliasing={{2}: (6, {}), {3}: (7, {})} | custom-call | flops 10000000 | bytes 1000000 | tf_op jit(solution)/shard_map/middle_step/pallas_call | solution.py:671
  24.6 0.0 collective-permute-done.4.next_pair
  24.6 0.7 %late_step.1 = (f32[128,128]{1,0:T(8,128)S(1)}, f32[2,4,8,128]{3,2,1,0:T(8,128)S(1)}, f32[2,68,8,128]{3,2,1,0:T(8,128)S(1)}, f32[2,66,8,128]{3,2,1,0:T(8,128)S(1...) custom-call(s32[1]{0:T(128)S(4)} %get-tuple-element.31.counts, ...), custom_call_target="tpu_custom_call", output_to_operand_aliasing={{2}: (2, {}), {3}: (3, {}), {4}: (4, {}), {5}: (5, {})} | custom-call | flops 1000000 | bytes 1000000 | tf_op jit(solution)/shard_map/late_step/pallas_call | solution.py:687
  25.4 26.5 %all_to_all.11 = f32[64,2,128]{2,1,0:T(2,128)S(1)} all-to-all(f32[64,2,128]{2,1,0:T(2,128)S(1)} %bitcast.3), channel_id=1, replica_groups=mesh['depth'=64,'lat'=16] {'depth'}, dimensions={0} | all-to-all | bytes 131072 | tf_op jit(solution)/shard_map/all_to_all | solution.py:765
  51.9 0.9 %composite.1 = (f32[4,4,1,16]{3,2,1,0:T(1,128)}, f32[64,8,128]{2,1,0:T(8,128)}, f32[64,8,128]{2,1,0:T(8,128)}) custom-call(s32[1]{0:T(128)S(4)} %get-tuple-element.31.counts, s32[4]{0:T(128)S(4)} %get-tuple-element.32.camera, f32[128,128]{1,0:T(8,128)S(1)} %bitcast.2, ...), custom_call_target="tpu_custom_call", output_to_operand_aliasing={{1}: (4, {}), {2}: (5, {})} | custom-call | tf_op jit(solution)/shard_map/composite/pallas_call | solution.py:704
  (2 shorter events, 0.0 us)
Async XLA Ops:
  2.6 7.3 %collective-permute-start = (f32[4,64,128]{2,1,0:T(8,128)S(1)}, f32[4,64,128]{2,1,0:T(8,128)S(1)}, u32[]{:S(2)}, u32[]{:S(2)}) collective-permute-start(f32[4,64,128]{2,1,0:T(8,128)S(1)} %get-tuple-element.37), channel_id=1, source_target_pairs={{0,1},{1,0},{2,3},{3,2},{4,5},{5,4},{6,7},{7,6},{8,9},{9,8},{10,11... | collective-permute-start | bytes 393224 | tf_op jit(solution)/shard_map/ppermute | solution.py:584
  4.6 7.5 %collective-permute-start.1 = (f32[4,64,128]{2,1,0:T(8,128)S(1)}, f32[4,64,128]{2,1,0:T(8,128)S(1)}, u32[]{:S(2)}, u32[]{:S(2)}) collective-permute-start(f32[4,64,128]{2,1,0:T(8,128)S(1)} %get-tuple-element.38), channel_id=1, source_target_pairs={{1,2},{2,1},{3,4},{4,3},{5,6},{6,5},{7,8},{8,7},{9,10},{10,9},{11,... | collective-permute-start | bytes 393224 | tf_op jit(solution)/shard_map/ppermute | solution.py:584
  6.5 6.5 %collective-permute-start.2 = (f32[2,3,8,128]{3,2,1,0:T(8,128)S(1)}, f32[2,3,8,128]{3,2,1,0:T(8,128)S(1)}, u32[]{:S(2)}, u32[]{:S(2)}) collective-permute-start(f32[2,3,8,128]{3,2,1,0:T(8,128)S(1)} %get-tuple-element.44), channel_id=1, source_target_pairs={{0,16},{16,0},{32,48},{48,32},{64,80},{80,64},{96,112},{112,96},{1... | collective-permute-start | bytes 73736 | tf_op jit(solution)/shard_map/ppermute | solution.py:584
  13.1 2.0 %collective-permute-start.3 = (f32[2,3,8,128]{3,2,1,0:T(8,128)S(1)}, f32[2,3,8,128]{3,2,1,0:T(8,128)S(1)}, u32[]{:S(2)}, u32[]{:S(2)}) collective-permute-start(f32[2,3,8,128]{3,2,1,0:T(8,128)S(1)} %pack_gap.1.order), channel_id=1, source_target_pairs={{16,32},{32,16},{48,64},{64,48},{80,96},{96,80},{112,128},{128,112... | collective-permute-start | bytes 73736 | tf_op jit(solution)/shard_map/ppermute | solution.py:584
  15.1 9.5 %collective-permute-start.4 = (f32[2,2,8,128]{3,2,1,0:T(8,128)S(1)}, f32[2,2,8,128]{3,2,1,0:T(8,128)S(1)}, u32[]{:S(2)}, u32[]{:S(2)}) collective-permute-start(f32[2,2,8,128]{3,2,1,0:T(8,128)S(1)} %pack_next.1.order), channel_id=1, source_target_pairs={{0,16},{16,0},{32,48},{48,32},{64,80},{80,64},{96,112},{112,96},{1... | collective-permute-start | bytes 49160 | tf_op jit(solution)/shard_map/ppermute | solution.py:584
